TPU v7x, 32 devices: a whole 2x2x4 slice. The times are simulated.
32 devices in a mesh: src: 8 (over z, core), freq: 4 (over y, x).
Axes of the slice: x: 2, y: 2, z: 4, core: 2. Of those that a mesh axis runs over, the one named last changes fastest.
Arguments:
- weights: bfloat16 [512, 512, 128], P('src', 'freq'), may hold values from -6 to 6
- kernels: bfloat16 [4, 2, 2, 128, 128], replicated, as said below
- src_phase: float32 [4, 64, 512], replicated, may hold values from -3.140625 to 3.140625
- freq_phase: float32 [4, 64, 512], replicated, may hold values from 0.5 to 4
Outputs:
- result: bfloat16 [512, 512, 128], P(('src', 'freq'))
Inputs may be any that keep to these rules, and one draw needn't show every extreme that they name: Every kernels[l, b, c] has the form [[A, B], [-B, A]] with 64 x 64 blocks A and B.
All inputs are finite; a program needn't handle non-finite values.
Results may differ from a plain program's by a relative error of at most 0.0064.
Values may be sent and summed in bfloat16 or wider, within the bound.
No kernel may reach another device: no remote copies, remote signals or barrier semaphores. Data moves between devices by JAX's collectives and lax.ppermute only.
A program may use at most 128 MiB of HBM per device.

v0:
```python
import jax
import jax.numpy as jnp
from jax import lax
from jax.sharding import PartitionSpec as P


def swapped(block, axis, distance):
    count = lax.axis_size(axis)
    route = []
    for low in range(count):
        high = low | 1 << distance
        if high != low and high < count:
            route += [(low, high), (high, low)]
    return lax.ppermute(block, axis, route)


def mix(lower, upper, kern):
    shape = lower.shape
    width = shape[-1]
    low2 = lower.reshape(-1, width)
    up2 = upper.reshape(-1, width)
    first = jnp.dot(low2, kern[0, 0], preferred_element_type=jnp.float32) + jnp.dot(
        up2, kern[0, 1], preferred_element_type=jnp.float32
    )
    second = jnp.dot(low2, kern[1, 0], preferred_element_type=jnp.float32) + jnp.dot(
        up2, kern[1, 1], preferred_element_type=jnp.float32
    )
    return (first.reshape(shape), second.reshape(shape))


def phase_part(phase, start, count):
    piece = lax.dynamic_slice_in_dim(phase, start, count, 1)
    return jnp.concatenate([piece, piece], 0).T


def rotate(values, angle):
    half = values.shape[-1] // 2
    flipped = jnp.concatenate([-values[..., half:], values[..., :half]], -1)
    return (values * jnp.cos(angle) + flipped * jnp.sin(angle)).astype(jnp.bfloat16)


def level_cols(block, kern, row_angle, col_angle):
    count, cols, width = block.shape
    grouped = block.reshape(count, 2, cols // 2, width)
    first, second = mix(grouped[:, 0], grouped[:, 1], kern)
    mixed = jnp.stack([first, second], 1).reshape(count, cols, width)
    return rotate(mixed, row_angle[:, None, :] * col_angle[None, :, :])


def pair_level(state, partner, kern, side, row_angle, col_angle):
    count, cols, width = state.shape
    chosen = lax.dynamic_index_in_dim(kern, side, 0, False)
    own_kern = lax.dynamic_index_in_dim(chosen, side, 0, False)
    other_kern = lax.dynamic_index_in_dim(chosen, 1 - side, 0, False)
    mixed = jnp.dot(
        state.reshape(-1, width), own_kern, preferred_element_type=jnp.float32
    ) + jnp.dot(partner.reshape(-1, width), other_kern, preferred_element_type=jnp.float32)
    mixed = mixed.reshape(count, cols, width)
    return rotate(mixed, row_angle[:, None, :] * col_angle[None, :, :])


def finish_early(state, kernels, src_phase, freq_phase, row_start, sub_rows, f_total):
    moved = lax.all_to_all(state, "freq", split_axis=0, concat_axis=1, tiled=True)
    row_angle = phase_part(src_phase[3], row_start, sub_rows)
    col_angle = phase_part(freq_phase[3], 0, f_total)
    return level_cols(moved, kernels[3], row_angle, col_angle)


def body(weights, kernels, src_phase, freq_phase):
    n_src = lax.axis_size("src")
    n_freq = lax.axis_size("freq")
    src_index = lax.axis_index("src")
    freq_index = lax.axis_index("freq")
    s_dev, f_dev, width = weights.shape
    src_bits = n_src.bit_length() - 1
    f_total = f_dev * n_freq
    sub_rows = s_dev // n_freq
    row_start = src_index * s_dev + freq_index * sub_rows
    state = weights
    for level in range(3):
        bit = src_bits - 1 - level
        partner = swapped(state, "src", bit)
        side = src_index >> bit & 1
        row_angle = phase_part(src_phase[level], src_index * s_dev, s_dev)
        col_angle = phase_part(freq_phase[level], freq_index * f_dev, f_dev)
        state = pair_level(state, partner, kernels[level], side, row_angle, col_angle)
    return finish_early(state, kernels, src_phase, freq_phase, row_start, sub_rows, f_total)


def solution(mesh):
    placed = (P("src", "freq", None), P(), P(), P())
    return jax.shard_map(
        body, mesh=mesh, in_specs=placed, out_specs=P(("src", "freq"), None, None), check_vma=False
    )
```

profile of v0, /device:TPU:0, one launch (start us, length us, event | category | flops | bytes accessed | tf_op | source)
XLA Modules:
  0.0 264.8 jit_solution(10211432566580499738)
XLA Ops:
  0.0 4.0 %collective-permute-start = (bf16[64,128,128]{2,1,0:T(8,128)(2,1)}, bf16[64,128,128]{2,1,0:T(8,128)(2,1)}, u32[]{:S(2)}, u32[]{:S(2)}) collective-permute-start(bf16[64,128,128]{2,1,0:T(8,128)(2,1)} %param.4), channel_id=1, source_target_pairs={{0,16},{16,0},{4,20},{20,4},{8,24},{24,8},{12,28},{28,12},{1,17},{... | collective-permute-start | bytes 6291464 | tf_op jit(solution)/shard_map/ppermute | solution.py:14
  4.0 1.8 fusion.44
  6.0 1.2 slice_bitcast_fusion
  7.4 0.7 copy.17
  8.2 1.1 slice_bitcast_fusion.1
  9.4 0.7 fusion.28
  10.1 84.9 %collective-permute-done = bf16[64,128,128]{2,1,0:T(8,128)(2,1)} collective-permute-done((bf16[64,128,128]{2,1,0:T(8,128)(2,1)}, bf16[64,128,128]{2,1,0:T(8,128)(2,1)}, u32[]{:S(2)}, u32[]{:S(2)}) %collective-permute-start) | collective-permute-done | bytes 2097184 | tf_op jit(solution)/shard_map/ppermute | solution.py:14
  95.0 2.4 convolution_add_fusion.2
  97.4 0.7 copy.25
  98.5 18.0 %fusion.11 = (bf16[64,128,128]{1,0,2:T(8,128)(2,1)S(1)}, f32[64,128,128]{1,0,2:T(8,128)S(1)}, f32[64,128,128]{1,0,2:T(8,128)S(1)}) fusion(f32[64,128,64]{1,0,2:T(8,128)S(1)} %get-tuple-element.12, f32[64,128,64]{1,0,2:T(8,128)S(1)} %get-tuple-element.11, f32[128,128]{0,1:T(8,128)S(1)} %maximum_bitcast_fusion.2, f32[64,128]{0,1:T(8,128)S(1)} %maximum_bitcast_fusion.1, ...), kind=kLoop, calls=%fused_computation.30 | loop fusion | flops 6291456 | bytes 18972672 | tf_op jit(solution)/shard_map/convert_element_type | solution.py:39
  116.5 0.7 collective-permute-start.1
  117.2 3.3 %copy_bitcast_fusion = (f32[8192,64]{0,1:T(8,128)S(1)}, f32[8192,64]{0,1:T(8,128)S(1)}) fusion(f32[8,8,64,128]{3,2,1,0:T(8,128)S(1)} %bitcast.146, f32[8,8,64,128]{3,2,1,0:T(8,128)S(1)} %bitcast.145), kind=kLoop, calls=%fused_computation.42 | loop fusion | bytes 8388608 | tf_op jit(solution)/shard_map/concatenate | solution.py:38
  120.5 9.0 %fusion.16 = f32[8192,128]{1,0:T(8,128)S(1)} fusion(f32[16,8,64,128]{3,2,1,0:T(8,128)S(1)} %bitcast.147, f32[16,8,64,128]{3,2,1,0:T(8,128)S(1)} %bitcast.148, f32[8192,64]{0,1:T(8,128)S(1)} %get-tuple-element.37, f32[8192,64]{0,1:T(8,128)S(1)} %get-tuple-element.38, f32[128,8192]{1,0:T(8,128)S(1)} %convolution_add_fusion.2, ...), kind=kOutput, calls=%fused_computation.39 | convolution fusion | flops 273678336 | bytes 21004292 | tf_op jit(solution)/shard_map/dot_general | solution.py:55
  129.5 33.9 %collective-permute-done.1 = bf16[64,128,128]{1,0,2:T(8,128)(2,1)S(1)} collective-permute-done((bf16[64,128,128]{1,0,2:T(8,128)(2,1)S(1)}, bf16[64,128,128]{1,0,2:T(8,128)(2,1)S(1)}, u32[]{:S(2)}, u32[]{:S(2)}) %collective-permute-start.1) | collective-permute-done | bytes 2097184 | tf_op jit(solution)/shard_map/ppermute | solution.py:14
  163.4 2.5 convolution_add_fusion.1
  165.9 1.6 slice_negate_fusion.2
  167.5 17.2 %fusion.15 = (bf16[64,128,128]{2,1,0:T(8,128)(2,1)}, f32[64,128,128]{2,1,0:T(8,128)}, f32[64,128,128]{2,1,0:T(8,128)}) fusion(f32[64,128,64]{2,1,0:T(8,128)S(1)} %get-tuple-element.10, f32[64,128,64]{2,1,0:T(8,128)S(1)} %get-tuple-element.9, f32[64,128,128]{2,1,0:T(8,128)S(1)} %bitcast.137, f32[128,128]{1,0:T(8,128)S(1)} %copy.15, f32[64,128]{1,0:T(8,128)S(1)} %copy.14), kind=kLoop, calls=%fused_computation.36 | loop fusion | flops 6291456 | bytes 18972672 | tf_op jit(solution)/shard_map/convert_element_type | solution.py:39
  184.8 7.1 %fusion.13 = bf16[8192,128]{1,0:T(8,128)(2,1)S(1)} fusion(f32[8192,64]{1,0:T(8,128)} %bitcast.144, f32[8192,64]{1,0:T(8,128)} %bitcast.143, f32[64,128,128]{2,1,0:T(8,128)} %get-tuple-element.31, f32[8192,128]{1,0:T(8,128)S(1)} %convolution_add_fusion.1, f32[64,128,128]{2,1,0:T(8,128)} %get-tuple-element.32), kind=kLoop, calls=%fused_computation.33 | loop fusion | flops 5242880 | bytes 18874368 | tf_op jit(solution)/shard_map/convert_element_type | solution.py:39
  191.9 0.7 fusion.23
  192.6 2.3 convolution_add_fusion
  194.9 1.8 slice_negate_fusion.1
  196.7 17.0 %fusion.2 = bf16[64,128,128]{2,1,0:T(8,128)(2,1)} fusion(f32[64,128,128]{2,1,0:T(8,128)S(1)} %bitcast.139, f32[64,128,64]{2,1,0:T(8,128)S(1)} %get-tuple-element.8, f32[64,128,64]{2,1,0:T(8,128)S(1)} %get-tuple-element.7, f32[128,128]{1,0:T(8,128)S(1)} %copy-done.3, f32[64,128]{1,0:T(8,128)S(1)} %copy.16), kind=kLoop, calls=%fused_computation.15 | loop fusion | flops 6291456 | bytes 10584064 | tf_op jit(solution)/shard_map/convert_element_type | solution.py:39
  213.6 3.9 %all-to-all-start = ((bf16[64,128,128]{2,1,0:T(8,128)(2,1)}), bf16[64,128,128]{2,1,0:T(8,128)(2,1)S(1)}, u32[]{:S(2)}, u32[]{:S(2)}) async-start(bf16[64,128,128]{2,1,0:T(8,128)(2,1)} %fusion.2), calls=%async_computation | async-start | bytes 4194304 | tf_op jit(solution)/shard_map/all_to_all | solution.py:63
  217.5 0.8 constant_dynamic-slice_fusion
  218.7 24.4 %all-to-all-done = bf16[64,128,128]{2,1,0:T(8,128)(2,1)S(1)} async-done(((bf16[64,128,128]{2,1,0:T(8,128)(2,1)}), bf16[64,128,128]{2,1,0:T(8,128)(2,1)S(1)}, u32[]{:S(2)}, u32[]{:S(2)}) %all-to-all-start) | async-done | bytes 2097184 | tf_op jit(solution)/shard_map/all_to_all | solution.py:63
  243.8 0.4 fusion.20
  244.2 0.4 convolution_add_fusion.4
  244.7 0.4 convolution_add_fusion.3
  245.1 0.4 pad_maximum_fusion
  245.5 0.4 copy.19
  246.0 1.5 slice_negate_fusion
  247.4 17.4 %fusion.6 = bf16[16,512,128]{2,1,0:T(8,128)(2,1)} fusion(f32[16,512,64]{2,1,0:T(8,128)S(1)} %get-tuple-element.6, f32[16,512,64]{2,1,0:T(8,128)S(1)} %get-tuple-element.5, f32[512,128]{1,0:T(8,128)S(1)} %copy.21, f32[16,128]{1,0:T(8,128)S(1)} %maximum_bitcast_fusion.7, f32[16,2,256,128]{3,2,1,0:T(8,128)S(1)} %copy.19), kind=kLoop, calls=%fused_computation.19 | loop fusion | flops 6291456 | bytes 10756096 | tf_op jit(solution)/shard_map/convert_element_type | solution.py:39
  (31 shorter events, 2.0 us)
Async XLA Ops:
  0.0 9.4 %copy-start.2 = (bf16[64,128,128]{2,1,0:T(8,128)(2,1)S(1)}, bf16[64,128,128]{2,1,0:T(8,128)(2,1)}, u32[]{:S(2)}) copy-start(bf16[64,128,128]{2,1,0:T(8,128)(2,1)} %param.4) | copy-start | bytes 6291460
  0.0 95.0 %collective-permute-start = (bf16[64,128,128]{2,1,0:T(8,128)(2,1)}, bf16[64,128,128]{2,1,0:T(8,128)(2,1)}, u32[]{:S(2)}, u32[]{:S(2)}) collective-permute-start(bf16[64,128,128]{2,1,0:T(8,128)(2,1)} %param.4), channel_id=1, source_target_pairs={{0,16},{16,0},{4,20},{20,4},{8,24},{24,8},{12,28},{28,12},{1,17},{... | collective-permute-start | bytes 6291464 | tf_op jit(solution)/shard_map/ppermute | solution.py:14
  116.5 46.9 %collective-permute-start.1 = (bf16[64,128,128]{1,0,2:T(8,128)(2,1)S(1)}, bf16[64,128,128]{1,0,2:T(8,128)(2,1)S(1)}, u32[]{:S(2)}, u32[]{:S(2)}) collective-permute-start(bf16[64,128,128]{1,0,2:T(8,128)(2,1)S(1)} %get-tuple-element.27), channel_id=1, source_target_pairs={{0,8},{8,0},{4,12},{12,4},{16,24},{24,16},{20,28},{28,20},{1,9},{9... | collective-permute-start | bytes 6291464 | tf_op jit(solution)/shard_map/ppermute | solution.py:14
  167.5 17.2 %copy-start = (f32[64,128,64]{2,1,0:T(8,128)}, f32[64,128,64]{2,1,0:T(8,128)S(1)}, u32[]{:S(2)}) copy-start(f32[64,128,64]{2,1,0:T(8,128)S(1)} %get-tuple-element.9) | copy-start | bytes 6291460
  167.5 17.2 %copy-start.1 = (f32[64,128,64]{2,1,0:T(8,128)}, f32[64,128,64]{2,1,0:T(8,128)S(1)}, u32[]{:S(2)}) copy-start(f32[64,128,64]{2,1,0:T(8,128)S(1)} %get-tuple-element.10) | copy-start | bytes 6291460
  184.7 7.8 %collective-permute-start.2 = (bf16[64,128,128]{2,1,0:T(8,128)(2,1)}, bf16[64,128,128]{2,1,0:T(8,128)(2,1)}, u32[]{:S(2)}, u32[]{:S(2)}) collective-permute-start(bf16[64,128,128]{2,1,0:T(8,128)(2,1)} %get-tuple-element.30), channel_id=1, source_target_pairs={{0,4},{4,0},{8,12},{12,8},{16,20},{20,16},{24,28},{28,24},{1,5},{5... | collective-permute-start | bytes 6291464 | tf_op jit(solution)/shard_map/ppermute | solution.py:14
  194.9 1.8 copy-start.3
  213.6 29.4 %all-to-all-start = ((bf16[64,128,128]{2,1,0:T(8,128)(2,1)}), bf16[64,128,128]{2,1,0:T(8,128)(2,1)S(1)}, u32[]{:S(2)}, u32[]{:S(2)}) async-start(bf16[64,128,128]{2,1,0:T(8,128)(2,1)} %fusion.2), calls=%async_computation | async-start | bytes 4194304 | tf_op jit(solution)/shard_map/all_to_all | solution.py:63
where the time goes:
time: 265 us
  waiting for transfers between devices  143 us (54%)
  other arithmetic  82.3 us (31%)
  matrix products  19.3 us (7%)
  local copies, waits for them, and re-layouts  11 us (4%)
  starting transfers between devices  8.7 us (3%)
    ppermute x3, waiting for transfers between devices, swapped(): return lax.ppermute(block, axis, route)  119 us
    convert_element_type x5, other arithmetic, rotate(): (values * jnp.cos(angle) + flipped * jnp.sin(angle)).astype(jnp.bfloat16)  76.6 us
    all_to_all x1, waiting for transfers between devices, finish_early(): lax.all_to_all(state, 'freq', split_axis=0, concat_axis=1, tiled=True)  24.4 us
    dot_general x3, matrix products, pair_level(): jnp.dot(state.reshape(-1, width), own_kern, preferred_element_type=jnp.fl...  10.4 us
    dot_general x3, matrix products, pair_level(): jnp.dot(partner.reshape(-1, width), other_kern, preferred_element_type=jn...  7.2 us
  transfers between devices with their start and end apart: 4, of which 3 were waited for; matrix products, arithmetic and copies ran while one was open for 10% of the time, Pallas kernels for 0%

commit v1 on v0

v1 whole, which is shorter than its diff:
```python
import functools

import jax
import jax.numpy as jnp
from jax import lax
from jax.experimental import pallas as pl
from jax.experimental.pallas import tpu as pltpu
from jax.sharding import PartitionSpec as P

SIN = (4.44288292, -7.3082457, 3.60635441, -0.84611289, 0.10982699)
COS = (1.4142135, -6.97885099, 5.73946117, -1.88356299, 0.31069819)
NEAREST = 12582912.0
FIRST = 48
VMEM = 48 * 2**20


def swapped(block, axis, mask):
    count = lax.axis_size(axis)
    return lax.ppermute(block, axis, [(at, at ^ mask) for at in range(count)])


def after(value, *earlier):
    return lax.optimization_barrier((value, *earlier))[0]


def turned(u, v, turns):
    part = turns - ((turns + NEAREST) - NEAREST)
    square = part * part
    sine, cosine = SIN[-1], COS[-1]
    for term in SIN[-2::-1]:
        sine = sine * square + term
    for term in COS[-2::-1]:
        cosine = cosine * square + term
    sine = sine * part
    cosine, sine = 1.0 - sine * sine, sine * cosine
    return u * cosine - v * sine, v * cosine + u * sine


def halves(y, turns):
    return turned(y[:, :128], y[:, 128:], turns)


def packed(y, turns):
    u, v = halves(y, turns)
    return jnp.concatenate([u, v], -1).astype(jnp.bfloat16)


def product(left, right, kern):
    return jnp.dot(jnp.concatenate([left, right], -1), kern, preferred_element_type=jnp.float32)


def split_pairs(y, turns):
    u, v = halves(y, turns)
    low = lax.broadcasted_iota(jnp.int32, u.shape, 1) < u.shape[1] // 2
    half = u.shape[1] // 2
    even = jnp.where(low, u, pltpu.roll(v, half, 1))
    odd = jnp.where(low, pltpu.roll(u, half, 1), v)
    return even.astype(jnp.bfloat16), odd.astype(jnp.bfloat16)


def first_levels(low, count, at, x0, x1, x2, x3, kern0, kern1, src, freq, out):
    x = (x0, x1, x2, x3)
    pairs = out.shape[2]
    rows = pairs * count
    turns = [freq[level, 0, low : low + count] for level in range(2)]

    def raw(block):
        both = block[0].reshape(pairs, 2, count, 128)
        return jnp.concatenate([both[:, 0].reshape(rows, 128), both[:, 1].reshape(rows, 128)], -1)

    left = jnp.concatenate([raw(x[0]), raw(x[1])], 0)
    right = jnp.concatenate([raw(x[2]), raw(x[3])], 0)
    mid = [[None, None], [None, None]]
    for b0 in range(2):
        y = product(left, right, kern0[b0])
        for b1 in range(2):
            mid[b0][b1] = jnp.concatenate(
                [
                    packed(
                        y[b1 * rows + p * count : b1 * rows + (p + 1) * count],
                        src[0, 2 * b0 + b1, 0, p : p + 1] * turns[0],
                    )
                    for p in range(pairs)
                ],
                0,
            )
    left = jnp.concatenate([mid[0][0], mid[1][0]], 0)
    right = jnp.concatenate([mid[0][1], mid[1][1]], 0)
    for b1 in range(2):
        y = product(left, right, kern1[b1])
        for b0 in range(2):
            for p in range(pairs):
                out[2 * b0 + b1, 0, p] = packed(
                    y[b0 * rows + p * count : b0 * rows + (p + 1) * count],
                    src[1, 2 * b0 + b1, 0, p : p + 1] * turns[1],
                )


def third_level(low, count, at, own, other, kern, src, freq, *outs):
    parts = len(outs)
    pairs = own.shape[2]
    here = at[0]
    turns = freq[2, here, low : low + count]
    for q in range(parts):
        to = here ^ q
        y = product(
            own[:, to].reshape(4 * pairs * count, 256), other[:, to].reshape(4 * pairs * count, 256), kern[...]
        )
        for k in range(4):
            for p in range(pairs):
                at_row = (k * pairs + p) * count
                outs[q][k, p] = packed(y[at_row : at_row + count], src[2, k, to, p : p + 1] * turns)


def last_level(low, count, here, x, kern, src, freq, outs):
    parts = len(x)
    pairs = x[0].shape[1]
    for q in range(parts // 2):
        left = x[q][...].reshape(4 * pairs * count, 256)
        right = x[q + parts // 2][...].reshape(4 * pairs * count, 256)
        for b in range(2):
            to = here ^ (q + b * (parts // 2))
            turns = freq[3, to, low : low + count]
            y = product(left, right, kern[b])
            for k in range(4):
                for p in range(pairs):
                    at_row = (k * pairs + p) * count
                    even, odd = split_pairs(y[at_row : at_row + count], src[3, k, here, p : p + 1] * turns)
                    outs[k][2 * p, to] = even
                    outs[k][2 * p + 1, to] = odd


def fourth_level(low, count, parts, at, *refs):
    x, (kern, src, freq), outs = refs[:parts], refs[parts : parts + 3], refs[parts + 3 :]
    last_level(low, count, at[0], x, kern, src, freq, outs)


def last_levels(low, count, parts, at, own, other, kern2, kern3, src, freq, *refs):
    outs, held = refs[:4], refs[4:]
    pairs = own.shape[2]
    here = at[0]
    for q in range(parts):
        turns = freq[2, here ^ q, low : low + count]
        y = product(
            own[:, q].reshape(4 * pairs * count, 256), other[:, q].reshape(4 * pairs * count, 256), kern2[...]
        )
        for k in range(4):
            for p in range(pairs):
                at_row = (k * pairs + p) * count
                held[q][k, p] = packed(y[at_row : at_row + count], src[2, k, here, p : p + 1] * turns)
    last_level(low, count, here, held, kern3, src, freq, outs)


def gather(spans, at, *refs):
    count = 4 * len(spans)
    parts, out, sems = refs[:count], refs[count], refs[count + 1]
    copies = []
    for c, (low, size) in enumerate(spans):
        for k in range(4):
            n = 4 * c + k
            copies.append(
                pltpu.make_async_copy(parts[n], out.at[at[0] ^ k, :, :, pl.ds(low, size)], sems.at[n])
            )
    for copy in copies:
        copy.start()
    for copy in copies:
        copy.wait()


def whole(shape):
    return pl.BlockSpec(shape, lambda *_: (0,) * len(shape))


def call(kernel, at, operands, outs, scratch=(), grid=(), in_specs=None, out_specs=None, flops=0):
    return pl.pallas_call(
        kernel,
        out_shape=outs,
        grid_spec=pltpu.PrefetchScalarGridSpec(
            num_scalar_prefetch=1,
            grid=grid,
            in_specs=in_specs or [whole(x.shape) for x in operands],
            out_specs=out_specs or [whole(x.shape) for x in outs],
            scratch_shapes=list(scratch),
        ),
        compiler_params=pltpu.CompilerParams(vmem_limit_bytes=VMEM),
        cost_estimate=pl.CostEstimate(
            flops=flops,
            bytes_accessed=sum(x.size * x.dtype.itemsize for x in [*operands, *outs]),
            transcendentals=0,
        ),
    )(at, *operands)


def paired(kern, raw):
    parts = kern.reshape(*kern.shape[:-2], 2, 64, 2, 64)
    eye = jnp.eye(2, dtype=kern.dtype)
    form = "...apbq,st->...saptbq" if raw else "...apbq,st->...aspbtq"
    wide = jnp.einsum("...apbq,st->...sapbtq" if raw else "...apbq,st->...aspbtq", parts, eye)
    return wide.reshape(*kern.shape[:-2], 256, 256)


def flipped(kern, bit):
    turned_kern = jnp.where(bit == 1, kern[::-1, ::-1], kern)
    return turned_kern.reshape(2, 512, 256)


def body(weights, kernels, src_phase, freq_phase):
    n_src, n_freq = lax.axis_size("src"), lax.axis_size("freq")
    src_index, here = lax.axis_index("src"), lax.axis_index("freq")
    s_dev, f_dev, _ = weights.shape
    bits = n_src.bit_length() - 1
    shift = bits - 2
    chip = src_index >> shift
    rest = src_index & ((1 << shift) - 1)
    side = src_index >> (shift - 1) & 1
    near = s_dev // n_freq
    each = near // 4
    pairs = each // 2
    spans = ((0, FIRST), (FIRST, f_dev - FIRST))
    at = jnp.reshape(here, (1,)).astype(jnp.int32)
    bf16 = jnp.bfloat16

    raw = weights.reshape(n_freq, 4, each, f_dev, 128)

    def to_chip(k, span):
        return lax.dynamic_index_in_dim(raw, chip ^ k, 1, False)[:, :, span[0] : span[0] + span[1]]

    def over_chips(parts, *earlier):
        return [swapped(after(parts[k], *earlier), "src", k << shift) for k in (3, 2, 1)]

    out_a = [to_chip(k, spans[0]) for k in range(4)]
    a3 = swapped(out_a[3], "src", 3 << shift)
    a2 = swapped(out_a[2], "src", 2 << shift)
    a1 = swapped(out_a[1], "src", 1 << shift)

    low, count = spans[1]
    parts_b = [
        lax.dynamic_index_in_dim(raw, here ^ q, 0, False)[:, :, low : low + count] for q in range(n_freq)
    ]
    moved = [parts_b[0]] + [swapped(parts_b[q], "freq", q) for q in range(1, n_freq)]

    def to_chip_b(k):
        return jnp.stack([lax.dynamic_index_in_dim(x, chip ^ k, 0, False) for x in moved], 0)

    turn = 1.0 / (2.0 * jnp.pi)
    src = src_phase.reshape(4, 64, 4, 1 << shift, n_freq, 4, each)
    src = lax.dynamic_index_in_dim(src, rest, 3, False)
    src = lax.dynamic_index_in_dim(src, chip, 4, False)
    src = jnp.stack([lax.dynamic_index_in_dim(src, chip ^ k, 2, False) for k in range(4)], 2)
    src = src.transpose(0, 2, 3, 4, 1).reshape(4, 4, n_freq, pairs, 128) * turn
    freq = freq_phase.transpose(0, 2, 1).reshape(4, n_freq, f_dev, 64)
    freq = jnp.concatenate([freq, freq], -1)
    wide0 = flipped(paired(kernels[0], True), chip >> 1)
    wide1 = flipped(paired(kernels[1], False), chip & 1)
    wide2 = paired(lax.dynamic_index_in_dim(kernels[2], side, 0, False), False)
    wide2 = jnp.where(side == 1, wide2[::-1], wide2).reshape(512, 256)
    wide3 = flipped(paired(kernels[3], False), here // (n_freq // 2))

    def levels01(x, span, early):
        low, count = span
        prefetch = jnp.concatenate([at, jnp.arange(n_freq, dtype=jnp.int32) ^ (at if early else 0)])
        src_spec = pl.BlockSpec(
            (2, 4, 1, pairs, 128),
            (lambda m, s: (0, 0, s[0], 0, 0)) if early else (lambda m, s: (0, 0, m, 0, 0)),
        )
        freq_spec = pl.BlockSpec(
            (2, 1, f_dev, 128),
            (lambda m, s: (0, s[1 + m], 0, 0)) if early else (lambda m, s: (0, s[0], 0, 0)),
        )
        x_spec = pl.BlockSpec((1, each, count, 128), lambda m, s: (m, 0, 0, 0))
        rows = 4 * n_freq * pairs * count
        return call(
            functools.partial(first_levels, low, count),
            prefetch,
            [*x, wide0, wide1, src, freq],
            [jax.ShapeDtypeStruct((4, n_freq, pairs, count, 256), bf16)],
            grid=(n_freq,),
            in_specs=[x_spec] * 4 + [whole(wide0.shape), whole(wide1.shape), src_spec, freq_spec],
            out_specs=[pl.BlockSpec((4, 1, pairs, count, 256), lambda m, s: (0, m, 0, 0, 0))],
            flops=2 * 2 * rows * 512 * 256,
        )[0]

    def back_shapes(count):
        return [jax.ShapeDtypeStruct((each, n_freq, count, 128), bf16)] * 4

    out_b = [to_chip_b(k) for k in range(4)]
    b3 = swapped(after(out_b[3], a3), "src", 3 << shift)
    b2 = swapped(after(out_b[2], a2), "src", 2 << shift)
    b1 = swapped(after(out_b[1], a1), "src", 1 << shift)

    low, count = spans[0]
    state_a = levels01([out_a[0], a1, a2, a3], spans[0], False)
    other_a = swapped(state_a, "src", 1 << (shift - 1))
    sent = call(
        functools.partial(third_level, low, count),
        at,
        [state_a, other_a, wide2, src, freq],
        [jax.ShapeDtypeStruct((4, pairs, count, 256), bf16)] * n_freq,
        flops=2 * 4 * n_freq * pairs * count * 512 * 256,
    )
    got = [sent[0]] + [swapped(sent[q], "freq", q) for q in range(1, n_freq)]
    back_a = call(
        functools.partial(fourth_level, low, count, n_freq),
        at,
        [*got, wide3, src, freq],
        back_shapes(count),
        flops=2 * 4 * n_freq * pairs * count * 512 * 256,
    )
    end_a = [None] * 4
    end_a[0] = back_a[0]
    for k, earlier in ((3, b3), (2, b2), (1, b1)):
        end_a[k] = swapped(after(back_a[k], earlier), "src", k << shift)

    low, count = spans[1]
    state_b = levels01([out_b[0], b1, b2, b3], spans[1], True)
    other_b = swapped(state_b, "src", 1 << (shift - 1))
    back_b = call(
        functools.partial(last_levels, low, count, n_freq),
        at,
        [state_b, other_b, wide2, wide3, src, freq],
        back_shapes(count),
        scratch=[pltpu.VMEM((4, pairs, count, 256), bf16)] * n_freq,
        flops=2 * 2 * 4 * n_freq * pairs * count * 512 * 256,
    )
    end_b = [None] * 4
    end_b[0] = back_b[0]
    for k in (3, 2, 1):
        end_b[k] = swapped(after(back_b[k], end_a[k]), "src", k << shift)

    ends = [*end_a, *end_b]
    out = call(
        functools.partial(gather, spans),
        jnp.reshape(chip, (1,)).astype(jnp.int32),
        ends,
        [jax.ShapeDtypeStruct((4, each, n_freq, f_dev, 128), bf16)],
        scratch=[pltpu.SemaphoreType.DMA((len(ends),))],
        in_specs=[pl.BlockSpec(memory_space=pl.ANY)] * len(ends),
        out_specs=[pl.BlockSpec(memory_space=pl.ANY)],
    )[0]
    return out.reshape(near, n_freq * f_dev, 128)


def solution(mesh):
    placed = (P("src", "freq", None), P(), P(), P())
    return jax.shard_map(
        body, mesh=mesh, in_specs=placed, out_specs=P(("src", "freq"), None, None), check_vma=False
    )
```

time: 265 us -> 143 us (0.54)
  the two profiles are of different devices: /device:TPU:0 before, /device:TPU:8 now
where the time goes in v1:
time: 143 us
  waiting for transfers between devices  73.7 us (52%)
  starting transfers between devices  23.3 us (16%)
  local copies, waits for them, and re-layouts  22.3 us (16%)
  Pallas kernels  17.3 us (12%)
  other arithmetic  5.94 us (4%)
    ppermute x20, waiting for transfers between devices, swapped(): return lax.ppermute(block, axis, [(at, at ^ mask) for at in range(count)])  73.7 us
    ppermute x20, starting transfers between devices, swapped(): return lax.ppermute(block, axis, [(at, at ^ mask) for at in range(count)])  23.3 us
    pallas_call x6, Pallas kernels, call(): pl.pallas_call(kernel, out_shape=outs, grid_spec=pltpu.PrefetchScalarGrid...  17.3 us
    reshape x4, local copies, waits for them, and re-layouts, paired(): return wide.reshape(*kern.shape[:-2], 256, 256)  6.99 us
    transpose x2, other arithmetic, paired(): jnp.einsum('...apbq,st->...sapbtq' if raw else '...apbq,st->...aspbtq', p...  4.87 us
    slice x4, local copies, waits for them, and re-layouts, body(): lax.dynamic_index_in_dim(raw, here ^ q, 0, False)[:, :, low:low + count]  3.27 us
    slice x4, local copies, waits for them, and re-layouts, to_chip(): lax.dynamic_index_in_dim(raw, chip ^ k, 1, False)  3.03 us
  transfers between devices with their start and end apart: 20, of which 10 were waited for; matrix products, arithmetic and copies ran while one was open for 17% of the time, Pallas kernels for 8%

profile of v1, /device:TPU:8, one launch (start us, length us, event | category | flops | bytes accessed | tf_op | source)
XLA Modules:
  0.0 143.0 jit_solution(3020263010684962645)
XLA Ops:
  0.0 2.7 %dynamic-slice_bitcast_fusion.4 = (bf16[4,4,128,128]{3,2,1,0:T(8,128)(2,1)S(1)}, bf16[4,4,128,128]{3,2,1,0:T(8,128)(2,1)S(1)}, bf16[4,4,128,128]{3,2,1,0:T(8,128)(2,1)S(1)}, bf16[4,4,128,128]{3,2,1,0:T(8,128)(2,1)}) fusion(bf16[4,4,4,128,128]{4,3,2,1,0:T(8,128)(2,1)} %bitcast.61, s32[]{:T(128)S(6)} %select_n.104, s32[]{:T(128)S(6)} %select_n.103, ...), kind=kLoop, calls=%fused_computation.12 | loop fusion | bytes 4194320 | tf_op jit(solution)/shard_map/jit(dynamic_index_in_dim)/squeeze | solution.py:226
  4.1 3.0 %collective-permute-start.1 = (bf16[4,4,48,128]{3,2,1,0:T(8,128)(2,1)}, bf16[4,4,48,128]{3,2,1,0:T(8,128)(2,1)S(1)}, u32[]{:S(2)}, u32[]{:S(2)}) collective-permute-start(bf16[4,4,48,128]{3,2,1,0:T(8,128)(2,1)} %slice.50), channel_id=1, source_target_pairs={{0,16},{4,20},{8,24},{12,28},{16,0},{20,4},{24,8},{28,12},{1,17},{... | collective-permute-start | bytes 589832 | tf_op jit(solution)/shard_map/ppermute | solution.py:19
  8.9 2.4 %collective-permute-start.9 = (bf16[4,4,80,128]{3,2,1,0:T(8,128)(2,1)}, bf16[4,4,80,128]{3,2,1,0:T(8,128)(2,1)}, u32[]{:S(2)}, u32[]{:S(2)}) collective-permute-start(bf16[4,4,80,128]{3,2,1,0:T(8,128)(2,1)} %slice.55), channel_id=1, source_target_pairs={{0,3},{1,2},{2,1},{3,0},{4,7},{5,6},{6,5},{7,4},{8,11},{9,10},{10,... | collective-permute-start | bytes 983048 | tf_op jit(solution)/shard_map/ppermute | solution.py:19
  15.0 3.6 %multiply_bitcast_fusion = (bf16[2,2,2,2,64,2,2,64]{7,6,5,4,3,2,1,0:T(2,128)(2,1)}, bf16[2,2,2,2,64,2,2,64]{7,6,5,4,3,2,1,0:T(2,128)(2,1)S(1)}, bf16[2,2,2,2,64,2,2,64]{7,6,5,4,2,3,1,0:T(2,128)(2,1)S(1)}) fusion(bf16[2,2,2,64,2,64]{5,4,3,2,1,0:T(2,128)(2,1)S(1)} %reshape_squeeze.11, bf16[2,2]{1,0:T(2,128)(2,1)S(1)} %compare_convert_fusion, ...), kind=kLoop, calls=%fused_computation.1 | loop fusion | flops 786432 | bytes 1966088 | tf_op jit(solution)/shard_map/...apbq,st->...aspbtq/transpose | solution.py:198
  19.4 1.5 %reshape.61 = bf16[2,2,256,256]{3,2,1,0:T(8,128)(2,1)} reshape(bf16[2,2,2,2,64,2,2,64]{7,6,5,4,3,2,1,0:T(2,128)(2,1)S(1)} %copy.11) | data formatting | bytes 1048576 | tf_op jit(solution)/shard_map/reshape | solution.py:199
  22.1 1.4 copy.13
  27.8 1.2 collective-permute-start.10
  29.1 2.4 %collective-permute-start.12 = (bf16[4,4,80,128]{3,2,1,0:T(8,128)(2,1)S(1)}, bf16[4,4,80,128]{3,2,1,0:T(8,128)(2,1)S(1)}, u32[]{:S(2)}, u32[]{:S(2)}) collective-permute-start(bf16[4,4,80,128]{3,2,1,0:T(8,128)(2,1)S(1)} %pad_maximum_fusion.2), channel_id=1, source_target_pairs={{0,16},{4,20},{8,24},{12,28},{16,0},{20,4},{24,8},{28,12},{1,17},{... | collective-permute-start | bytes 983048 | tf_op jit(solution)/shard_map/ppermute | solution.py:19
  31.5 4.6 %collective-permute-done.2.x3 = bf16[4,4,48,128]{3,2,1,0:T(8,128)(2,1)S(1)} collective-permute-done((bf16[4,4,48,128]{3,2,1,0:T(8,128)(2,1)S(1)}, bf16[4,4,48,128]{3,2,1,0:T(8,128)(2,1)S(1)}, u32[]{:S(2)}, u32[]{:S(2)}) %collective-permute-start.2) | collective-permute-done | bytes 196640 | tf_op jit(solution)/shard_map/ppermute | solution.py:19
  36.3 7.1 %collective-permute-done.10.x1 = bf16[4,4,80,128]{3,2,1,0:T(8,128)(2,1)S(1)} collective-permute-done((bf16[4,4,80,128]{3,2,1,0:T(8,128)(2,1)S(1)}, bf16[4,4,80,128]{3,2,1,0:T(8,128)(2,1)S(1)}, u32[]{:S(2)}, u32[]{:S(2)}) %collective-permute-start.10) | collective-permute-done | bytes 327712 | tf_op jit(solution)/shard_map/ppermute | solution.py:19
  43.4 11.2 %collective-permute-done.12.x2 = bf16[4,4,80,128]{3,2,1,0:T(8,128)(2,1)S(1)} collective-permute-done((bf16[4,4,80,128]{3,2,1,0:T(8,128)(2,1)S(1)}, bf16[4,4,80,128]{3,2,1,0:T(8,128)(2,1)S(1)}, u32[]{:S(2)}, u32[]{:S(2)}) %collective-permute-start.12) | collective-permute-done | bytes 327712 | tf_op jit(solution)/shard_map/ppermute | solution.py:19
  54.7 8.0 %collective-permute-done.14.x3 = bf16[4,4,80,128]{3,2,1,0:T(8,128)(2,1)S(1)} collective-permute-done((bf16[4,4,80,128]{3,2,1,0:T(8,128)(2,1)S(1)}, bf16[4,4,80,128]{3,2,1,0:T(8,128)(2,1)S(1)}, u32[]{:S(2)}, u32[]{:S(2)}) %collective-permute-start.14) | collective-permute-done | bytes 327712 | tf_op jit(solution)/shard_map/ppermute | solution.py:19
  62.7 5.2 %shard_map.49.own = bf16[4,4,2,80,256]{4,3,2,1,0:T(8,128)(2,1)} custom-call(s32[5]{0:T(128)S(1)} %pad_add_fusion.1.at, bf16[4,4,80,128]{3,2,1,0:T(8,128)(2,1)S(1)} %pad_maximum_fusion.4.x0, bf16[4,4,80,128]{3,2,1,0:T(8,128)(2,1)S(1)} %collective-permute-done.10.x1, bf16[4,4,80,128]{3,2,1,0:T(8,128)(2,1)S(1)} %collective-permute-done.12.x2, ...), custom_call_target="tpu_custom_call" | custom-call | flops 1342177280 | bytes 4784128 | tf_op jit(solution)/shard_map/pallas_call | solution.py:175
  68.9 3.3 %shard_map.46.own = bf16[4,4,2,48,256]{4,3,2,1,0:T(8,128)(2,1)S(1)} custom-call(s32[5]{0:T(128)S(1)} %pad_add_fusion.at, bf16[4,4,48,128]{3,2,1,0:T(8,128)(2,1)S(1)} %slice.48.x0, bf16[4,4,48,128]{3,2,1,0:T(8,128)(2,1)S(1)} %collective-permute-done.x1, bf16[4,4,48,128]{3,2,1,0:T(8,128)(2,1)S(1)} %collective-permute-done.1.x2, ...), custom_call_target="tpu_custom_call" | custom-call | flops 805306368 | bytes 3735552 | tf_op jit(solution)/shard_map/pallas_call | solution.py:175
  72.9 1.3 multiply_bitcast_fusion.3
  74.2 1.5 %reshape.68 = bf16[2,256,256]{2,1,0:T(8,128)(2,1)S(1)} reshape(bf16[2,2,2,64,2,2,64]{6,5,4,3,2,1,0:T(2,128)(2,1)} %multiply_bitcast_fusion.3) | data formatting | bytes 524288 | tf_op jit(solution)/shard_map/reshape | solution.py:199
  75.6 3.4 %reshape.70 = bf16[2,2,256,256]{3,2,1,0:T(8,128)(2,1)} reshape(bf16[2,2,2,2,64,2,2,64]{7,6,5,4,3,2,1,0:T(2,128)(2,1)} %get-tuple-element.79) | data formatting | bytes 1048576 | tf_op jit(solution)/shard_map/reshape | solution.py:199
  79.1 1.0 shard_map.47
  80.2 1.5 %collective-permute-start.4 = (bf16[4,2,48,256]{3,2,1,0:T(8,128)(2,1)S(1)}, bf16[4,2,48,256]{3,2,1,0:T(8,128)(2,1)S(1)}, u32[]{:S(2)}, u32[]{:S(2)}) collective-permute-start(bf16[4,2,48,256]{3,2,1,0:T(8,128)(2,1)S(1)} %get-tuple-element.27), channel_id=1, source_target_pairs={{0,1},{1,0},{2,3},{3,2},{4,5},{5,4},{6,7},{7,6},{8,9},{9,8},{10,11... | collective-permute-start | bytes 589832 | tf_op jit(solution)/shard_map/ppermute | solution.py:19
  81.7 1.5 %collective-permute-start.5 = (bf16[4,2,48,256]{3,2,1,0:T(8,128)(2,1)S(1)}, bf16[4,2,48,256]{3,2,1,0:T(8,128)(2,1)S(1)}, u32[]{:S(2)}, u32[]{:S(2)}) collective-permute-start(bf16[4,2,48,256]{3,2,1,0:T(8,128)(2,1)S(1)} %get-tuple-element.28), channel_id=1, source_target_pairs={{0,2},{1,3},{2,0},{3,1},{4,6},{5,7},{6,4},{7,5},{8,10},{9,11},{10,... | collective-permute-start | bytes 589832 | tf_op jit(solution)/shard_map/ppermute | solution.py:19
  83.8 4.2 %collective-permute-done.4.refs_1_ = bf16[4,2,48,256]{3,2,1,0:T(8,128)(2,1)S(1)} collective-permute-done((bf16[4,2,48,256]{3,2,1,0:T(8,128)(2,1)S(1)}, bf16[4,2,48,256]{3,2,1,0:T(8,128)(2,1)S(1)}, u32[]{:S(2)}, u32[]{:S(2)}) %collective-permute-start.4) | collective-permute-done | bytes 196640 | tf_op jit(solution)/shard_map/ppermute | solution.py:19
  88.0 4.5 %collective-permute-done.5.refs_2_ = bf16[4,2,48,256]{3,2,1,0:T(8,128)(2,1)S(1)} collective-permute-done((bf16[4,2,48,256]{3,2,1,0:T(8,128)(2,1)S(1)}, bf16[4,2,48,256]{3,2,1,0:T(8,128)(2,1)S(1)}, u32[]{:S(2)}, u32[]{:S(2)}) %collective-permute-start.5) | collective-permute-done | bytes 196640 | tf_op jit(solution)/shard_map/ppermute | solution.py:19
  92.5 1.2 shard_map.48
  93.8 2.0 %collective-permute-start.13 = (bf16[4,4,48,128]{3,2,1,0:T(8,128)(2,1)S(1)}, bf16[4,4,48,128]{3,2,1,0:T(8,128)(2,1)S(1)}, u32[]{:S(2)}, u32[]{:S(2)}) collective-permute-start(bf16[4,4,48,128]{3,2,1,0:T(8,128)(2,1)S(1)} %get-tuple-element.36), channel_id=1, source_target_pairs={{0,16},{4,20},{8,24},{12,28},{16,0},{20,4},{24,8},{28,12},{1,17},{... | collective-permute-start | bytes 589832 | tf_op jit(solution)/shard_map/ppermute | solution.py:19
  95.7 1.5 %collective-permute-start.15 = (bf16[4,4,48,128]{3,2,1,0:T(8,128)(2,1)S(1)}, bf16[4,4,48,128]{3,2,1,0:T(8,128)(2,1)S(1)}, u32[]{:S(2)}, u32[]{:S(2)}) collective-permute-start(bf16[4,4,48,128]{3,2,1,0:T(8,128)(2,1)S(1)} %get-tuple-element.39), channel_id=1, source_target_pairs={{0,24},{4,28},{8,16},{12,20},{16,8},{20,12},{24,0},{28,4},{1,25},{... | collective-permute-start | bytes 589832 | tf_op jit(solution)/shard_map/ppermute | solution.py:19
  97.2 5.2 %shard_map.50 = (bf16[4,4,80,128]{3,2,1,0:T(8,128)(2,1)S(1)}, bf16[4,4,80,128]{3,2,1,0:T(8,128)(2,1)S(1)}, bf16[4,4,80,128]{3,2,1,0:T(8,128)(2,1)S(1)}, bf16[4,4,80,128]{3,2,1,0:T(8,128)(2,1)S(1)}) custom-call(s32[1]{0:T(128)} %bitcast.1.at, bf16[4,4,2,80,256]{4,3,2,1,0:T(8,128)(2,1)} %shard_map.49.own, ...), custom_call_target="tpu_custom_call" | custom-call | flops 1342177280 | bytes 5832704 | tf_op jit(solution)/shard_map/pallas_call | solution.py:175
  103.5 5.8 %collective-permute-done.13.refs_2_ = bf16[4,4,48,128]{3,2,1,0:T(8,128)(2,1)S(1)} collective-permute-done((bf16[4,4,48,128]{3,2,1,0:T(8,128)(2,1)S(1)}, bf16[4,4,48,128]{3,2,1,0:T(8,128)(2,1)S(1)}, u32[]{:S(2)}, u32[]{:S(2)}) %collective-permute-start.13) | collective-permute-done | bytes 196640 | tf_op jit(solution)/shard_map/ppermute | solution.py:19
  109.3 3.4 %collective-permute-start.18 = (bf16[4,4,80,128]{3,2,1,0:T(8,128)(2,1)S(1)}, bf16[4,4,80,128]{3,2,1,0:T(8,128)(2,1)S(1)}, u32[]{:S(2)}, u32[]{:S(2)}) collective-permute-start(bf16[4,4,80,128]{3,2,1,0:T(8,128)(2,1)S(1)} %get-tuple-element.44), channel_id=1, source_target_pairs={{0,16},{4,20},{8,24},{12,28},{16,0},{20,4},{24,8},{28,12},{1,17},{... | collective-permute-start | bytes 983048 | tf_op jit(solution)/shard_map/ppermute | solution.py:19
  112.7 4.4 %collective-permute-done.15.refs_3_ = bf16[4,4,48,128]{3,2,1,0:T(8,128)(2,1)S(1)} collective-permute-done((bf16[4,4,48,128]{3,2,1,0:T(8,128)(2,1)S(1)}, bf16[4,4,48,128]{3,2,1,0:T(8,128)(2,1)S(1)}, u32[]{:S(2)}, u32[]{:S(2)}) %collective-permute-start.15) | collective-permute-done | bytes 196640 | tf_op jit(solution)/shard_map/ppermute | solution.py:19
  117.6 17.0 %collective-permute-done.18.refs_6_ = bf16[4,4,80,128]{3,2,1,0:T(8,128)(2,1)S(1)} collective-permute-done((bf16[4,4,80,128]{3,2,1,0:T(8,128)(2,1)S(1)}, bf16[4,4,80,128]{3,2,1,0:T(8,128)(2,1)S(1)}, u32[]{:S(2)}, u32[]{:S(2)}) %collective-permute-start.18) | collective-permute-done | bytes 327712 | tf_op jit(solution)/shard_map/ppermute | solution.py:19
  134.6 6.8 %collective-permute-done.19.refs_7_ = bf16[4,4,80,128]{3,2,1,0:T(8,128)(2,1)S(1)} collective-permute-done((bf16[4,4,80,128]{3,2,1,0:T(8,128)(2,1)S(1)}, bf16[4,4,80,128]{3,2,1,0:T(8,128)(2,1)S(1)}, u32[]{:S(2)}, u32[]{:S(2)}) %collective-permute-start.19) | collective-permute-done | bytes 327712 | tf_op jit(solution)/shard_map/ppermute | solution.py:19
  141.4 1.4 shard_map.51
  (72 shorter events, 17.3 us)
Async XLA Ops:
  0.0 7.1 %copy-start = (bf16[64,128,128]{2,1,0:T(8,128)(2,1)S(1)}, bf16[64,128,128]{2,1,0:T(8,128)(2,1)}, u32[]{:S(2)}) copy-start(bf16[64,128,128]{2,1,0:T(8,128)(2,1)} %param.4) | copy-start | bytes 6291460
  3.3 24.5 %collective-permute-start = (bf16[4,4,48,128]{3,2,1,0:T(8,128)(2,1)}, bf16[4,4,48,128]{3,2,1,0:T(8,128)(2,1)S(1)}, u32[]{:S(2)}, u32[]{:S(2)}) collective-permute-start(bf16[4,4,48,128]{3,2,1,0:T(8,128)(2,1)} %slice.49), channel_id=1, source_target_pairs={{0,8},{4,12},{8,0},{12,4},{16,24},{20,28},{24,16},{28,20},{1,9},{5... | collective-permute-start | bytes 589832 | tf_op jit(solution)/shard_map/ppermute | solution.py:19
  4.1 25.0 %collective-permute-start.1 = (bf16[4,4,48,128]{3,2,1,0:T(8,128)(2,1)}, bf16[4,4,48,128]{3,2,1,0:T(8,128)(2,1)S(1)}, u32[]{:S(2)}, u32[]{:S(2)}) collective-permute-start(bf16[4,4,48,128]{3,2,1,0:T(8,128)(2,1)} %slice.50), channel_id=1, source_target_pairs={{0,16},{4,20},{8,24},{12,28},{16,0},{20,4},{24,8},{28,12},{1,17},{... | collective-permute-start | bytes 589832 | tf_op jit(solution)/shard_map/ppermute | solution.py:19
  8.1 6.5 %copy-start.4 = (bf16[4,2,2,128,128]{4,3,2,1,0:T(8,128)(2,1)S(1)}, bf16[4,2,2,128,128]{4,3,2,1,0:T(8,128)(2,1)}, u32[]{:S(2)}) copy-start(bf16[4,2,2,128,128]{4,3,2,1,0:T(8,128)(2,1)} %param.5) | copy-start | bytes 1572868
  8.9 16.3 %collective-permute-start.9 = (bf16[4,4,80,128]{3,2,1,0:T(8,128)(2,1)}, bf16[4,4,80,128]{3,2,1,0:T(8,128)(2,1)}, u32[]{:S(2)}, u32[]{:S(2)}) collective-permute-start(bf16[4,4,80,128]{3,2,1,0:T(8,128)(2,1)} %slice.55), channel_id=1, source_target_pairs={{0,3},{1,2},{2,1},{3,0},{4,7},{5,6},{6,5},{7,4},{8,11},{9,10},{10,... | collective-permute-start | bytes 983048 | tf_op jit(solution)/shard_map/ppermute | solution.py:19
  12.1 14.6 %collective-permute-start.8 = (bf16[4,4,80,128]{3,2,1,0:T(8,128)(2,1)}, bf16[4,4,80,128]{3,2,1,0:T(8,128)(2,1)}, u32[]{:S(2)}, u32[]{:S(2)}) collective-permute-start(bf16[4,4,80,128]{3,2,1,0:T(8,128)(2,1)} %slice.54), channel_id=1, source_target_pairs={{0,2},{1,3},{2,0},{3,1},{4,6},{5,7},{6,4},{7,5},{8,10},{9,11},{10,... | collective-permute-start | bytes 983048 | tf_op jit(solution)/shard_map/ppermute | solution.py:19
  13.3 14.4 %collective-permute-start.7 = (bf16[4,4,80,128]{3,2,1,0:T(8,128)(2,1)}, bf16[4,4,80,128]{3,2,1,0:T(8,128)(2,1)S(1)}, u32[]{:S(2)}, u32[]{:S(2)}) collective-permute-start(bf16[4,4,80,128]{3,2,1,0:T(8,128)(2,1)} %slice.53), channel_id=1, source_target_pairs={{0,1},{1,0},{2,3},{3,2},{4,5},{5,4},{6,7},{7,6},{8,9},{9,8},{10,11... | collective-permute-start | bytes 983048 | tf_op jit(solution)/shard_map/ppermute | solution.py:19
  19.4 2.1 %copy-start.3 = (f32[4,64,512]{2,1,0:T(8,128)S(1)}, f32[4,64,512]{2,1,0:T(8,128)}, u32[]{:S(2)}) copy-start(f32[4,64,512]{2,1,0:T(8,128)} %param.6) | copy-start | bytes 1572868
  23.5 1.4 copy-start.2
  23.5 1.6 %copy-start.5 = (bf16[4,4,48,128]{3,2,1,0:T(8,128)(2,1)S(1)}, bf16[4,4,48,128]{3,2,1,0:T(8,128)(2,1)}, u32[]{:S(2)}) copy-start(bf16[4,4,48,128]{3,2,1,0:T(8,128)(2,1)} %slice.51) | copy-start | bytes 589828
  25.1 11.0 %collective-permute-start.2 = (bf16[4,4,48,128]{3,2,1,0:T(8,128)(2,1)S(1)}, bf16[4,4,48,128]{3,2,1,0:T(8,128)(2,1)S(1)}, u32[]{:S(2)}, u32[]{:S(2)}) collective-permute-start(bf16[4,4,48,128]{3,2,1,0:T(8,128)(2,1)S(1)} %copy-done.5), channel_id=1, source_target_pairs={{0,24},{4,28},{8,16},{12,20},{16,8},{20,12},{24,0},{28,4},{1,25},{... | collective-permute-start | bytes 589832 | tf_op jit(solution)/shard_map/ppermute | solution.py:19
  27.8 15.6 %collective-permute-start.10 = (bf16[4,4,80,128]{3,2,1,0:T(8,128)(2,1)S(1)}, bf16[4,4,80,128]{3,2,1,0:T(8,128)(2,1)S(1)}, u32[]{:S(2)}, u32[]{:S(2)}) collective-permute-start(bf16[4,4,80,128]{3,2,1,0:T(8,128)(2,1)S(1)} %pad_maximum_fusion.1), channel_id=1, source_target_pairs={{0,8},{4,12},{8,0},{12,4},{16,24},{20,28},{24,16},{28,20},{1,9},{5... | collective-permute-start | bytes 983048 | tf_op jit(solution)/shard_map/ppermute | solution.py:19
  29.1 25.6 %collective-permute-start.12 = (bf16[4,4,80,128]{3,2,1,0:T(8,128)(2,1)S(1)}, bf16[4,4,80,128]{3,2,1,0:T(8,128)(2,1)S(1)}, u32[]{:S(2)}, u32[]{:S(2)}) collective-permute-start(bf16[4,4,80,128]{3,2,1,0:T(8,128)(2,1)S(1)} %pad_maximum_fusion.2), channel_id=1, source_target_pairs={{0,16},{4,20},{8,24},{12,28},{16,0},{20,4},{24,8},{28,12},{1,17},{... | collective-permute-start | bytes 983048 | tf_op jit(solution)/shard_map/ppermute | solution.py:19
  36.2 26.5 %collective-permute-start.14 = (bf16[4,4,80,128]{3,2,1,0:T(8,128)(2,1)S(1)}, bf16[4,4,80,128]{3,2,1,0:T(8,128)(2,1)S(1)}, u32[]{:S(2)}, u32[]{:S(2)}) collective-permute-start(bf16[4,4,80,128]{3,2,1,0:T(8,128)(2,1)S(1)} %pad_maximum_fusion.3), channel_id=1, source_target_pairs={{0,24},{4,28},{8,16},{12,20},{16,8},{20,12},{24,0},{28,4},{1,25},{... | collective-permute-start | bytes 983048 | tf_op jit(solution)/shard_map/ppermute | solution.py:19
  67.9 29.3 %collective-permute-start.16 = (bf16[4,4,2,80,256]{4,3,2,1,0:T(8,128)(2,1)}, bf16[4,4,2,80,256]{4,3,2,1,0:T(8,128)(2,1)}, u32[]{:S(2)}, u32[]{:S(2)}) collective-permute-start(bf16[4,4,2,80,256]{4,3,2,1,0:T(8,128)(2,1)} %shard_map.49.own), channel_id=1, source_target_pairs={{0,4},{4,0},{8,12},{12,8},{16,20},{20,16},{24,28},{28,24},{1,5},{5... | collective-permute-start | bytes 3932168 | tf_op jit(solution)/shard_map/ppermute | solution.py:19
  72.2 6.9 %collective-permute-start.3 = (bf16[4,4,2,48,256]{4,3,2,1,0:T(8,128)(2,1)S(1)}, bf16[4,4,2,48,256]{4,3,2,1,0:T(8,128)(2,1)S(1)}, u32[]{:S(2)}, u32[]{:S(2)}) collective-permute-start(bf16[4,4,2,48,256]{4,3,2,1,0:T(8,128)(2,1)S(1)} %shard_map.46.own), channel_id=1, source_target_pairs={{0,4},{4,0},{8,12},{12,8},{16,20},{20,16},{24,28},{28,24},{1,5},{5... | collective-permute-start | bytes 2359304 | tf_op jit(solution)/shard_map/ppermute | solution.py:19
  79.1 4.7 %copy-start.1 = (bf16[2,2,256,256]{3,2,1,0:T(8,128)(2,1)S(1)}, bf16[2,2,256,256]{3,2,1,0:T(8,128)(2,1)}, u32[]{:S(2)}) copy-start(bf16[2,2,256,256]{3,2,1,0:T(8,128)(2,1)} %reshape.70) | copy-start | bytes 1572868
  80.2 7.8 %collective-permute-start.4 = (bf16[4,2,48,256]{3,2,1,0:T(8,128)(2,1)S(1)}, bf16[4,2,48,256]{3,2,1,0:T(8,128)(2,1)S(1)}, u32[]{:S(2)}, u32[]{:S(2)}) collective-permute-start(bf16[4,2,48,256]{3,2,1,0:T(8,128)(2,1)S(1)} %get-tuple-element.27), channel_id=1, source_target_pairs={{0,1},{1,0},{2,3},{3,2},{4,5},{5,4},{6,7},{7,6},{8,9},{9,8},{10,11... | collective-permute-start | bytes 589832 | tf_op jit(solution)/shard_map/ppermute | solution.py:19
  81.7 10.8 %collective-permute-start.5 = (bf16[4,2,48,256]{3,2,1,0:T(8,128)(2,1)S(1)}, bf16[4,2,48,256]{3,2,1,0:T(8,128)(2,1)S(1)}, u32[]{:S(2)}, u32[]{:S(2)}) collective-permute-start(bf16[4,2,48,256]{3,2,1,0:T(8,128)(2,1)S(1)} %get-tuple-element.28), channel_id=1, source_target_pairs={{0,2},{1,3},{2,0},{3,1},{4,6},{5,7},{6,4},{7,5},{8,10},{9,11},{10,... | collective-permute-start | bytes 589832 | tf_op jit(solution)/shard_map/ppermute | solution.py:19
  83.2 9.2 %collective-permute-start.6 = (bf16[4,2,48,256]{3,2,1,0:T(8,128)(2,1)S(1)}, bf16[4,2,48,256]{3,2,1,0:T(8,128)(2,1)S(1)}, u32[]{:S(2)}, u32[]{:S(2)}) collective-permute-start(bf16[4,2,48,256]{3,2,1,0:T(8,128)(2,1)S(1)} %get-tuple-element.29), channel_id=1, source_target_pairs={{0,3},{1,2},{2,1},{3,0},{4,7},{5,6},{6,5},{7,4},{8,11},{9,10},{10,... | collective-permute-start | bytes 589832 | tf_op jit(solution)/shard_map/ppermute | solution.py:19
  93.7 8.8 %collective-permute-start.11 = (bf16[4,4,48,128]{3,2,1,0:T(8,128)(2,1)S(1)}, bf16[4,4,48,128]{3,2,1,0:T(8,128)(2,1)S(1)}, u32[]{:S(2)}, u32[]{:S(2)}) collective-permute-start(bf16[4,4,48,128]{3,2,1,0:T(8,128)(2,1)S(1)} %get-tuple-element.33), channel_id=1, source_target_pairs={{0,8},{4,12},{8,0},{12,4},{16,24},{20,28},{24,16},{28,20},{1,9},{5... | collective-permute-start | bytes 589832 | tf_op jit(solution)/shard_map/ppermute | solution.py:19
  93.8 15.6 %collective-permute-start.13 = (bf16[4,4,48,128]{3,2,1,0:T(8,128)(2,1)S(1)}, bf16[4,4,48,128]{3,2,1,0:T(8,128)(2,1)S(1)}, u32[]{:S(2)}, u32[]{:S(2)}) collective-permute-start(bf16[4,4,48,128]{3,2,1,0:T(8,128)(2,1)S(1)} %get-tuple-element.36), channel_id=1, source_target_pairs={{0,16},{4,20},{8,24},{12,28},{16,0},{20,4},{24,8},{28,12},{1,17},{... | collective-permute-start | bytes 589832 | tf_op jit(solution)/shard_map/ppermute | solution.py:19
  95.7 21.4 %collective-permute-start.15 = (bf16[4,4,48,128]{3,2,1,0:T(8,128)(2,1)S(1)}, bf16[4,4,48,128]{3,2,1,0:T(8,128)(2,1)S(1)}, u32[]{:S(2)}, u32[]{:S(2)}) collective-permute-start(bf16[4,4,48,128]{3,2,1,0:T(8,128)(2,1)S(1)} %get-tuple-element.39), channel_id=1, source_target_pairs={{0,24},{4,28},{8,16},{12,20},{16,8},{20,12},{24,0},{28,4},{1,25},{... | collective-permute-start | bytes 589832 | tf_op jit(solution)/shard_map/ppermute | solution.py:19
  102.5 15.2 %collective-permute-start.17 = (bf16[4,4,80,128]{3,2,1,0:T(8,128)(2,1)S(1)}, bf16[4,4,80,128]{3,2,1,0:T(8,128)(2,1)S(1)}, u32[]{:S(2)}, u32[]{:S(2)}) collective-permute-start(bf16[4,4,80,128]{3,2,1,0:T(8,128)(2,1)S(1)} %get-tuple-element.42), channel_id=1, source_target_pairs={{0,8},{4,12},{8,0},{12,4},{16,24},{20,28},{24,16},{28,20},{1,9},{5... | collective-permute-start | bytes 983048 | tf_op jit(solution)/shard_map/ppermute | solution.py:19
  109.3 25.3 %collective-permute-start.18 = (bf16[4,4,80,128]{3,2,1,0:T(8,128)(2,1)S(1)}, bf16[4,4,80,128]{3,2,1,0:T(8,128)(2,1)S(1)}, u32[]{:S(2)}, u32[]{:S(2)}) collective-permute-start(bf16[4,4,80,128]{3,2,1,0:T(8,128)(2,1)S(1)} %get-tuple-element.44), channel_id=1, source_target_pairs={{0,16},{4,20},{8,24},{12,28},{16,0},{20,4},{24,8},{28,12},{1,17},{... | collective-permute-start | bytes 983048 | tf_op jit(solution)/shard_map/ppermute | solution.py:19
  117.1 24.4 %collective-permute-start.19 = (bf16[4,4,80,128]{3,2,1,0:T(8,128)(2,1)S(1)}, bf16[4,4,80,128]{3,2,1,0:T(8,128)(2,1)S(1)}, u32[]{:S(2)}, u32[]{:S(2)}) collective-permute-start(bf16[4,4,80,128]{3,2,1,0:T(8,128)(2,1)S(1)} %get-tuple-element.46), channel_id=1, source_target_pairs={{0,24},{4,28},{8,16},{12,20},{16,8},{20,12},{24,0},{28,4},{1,25},{... | collective-permute-start | bytes 983048 | tf_op jit(solution)/shard_map/ppermute | solution.py:19

commit v2 on v1

v2 whole, which is shorter than its diff:
```python
import functools
import math

import jax
import jax.numpy as jnp
from jax import lax
from jax.experimental import pallas as pl
from jax.experimental.pallas import tpu as pltpu
from jax.sharding import PartitionSpec as P

SIN = (4.44288292, -7.3082457, 3.60635441, -0.84611289, 0.10982699)
COS = (1.4142135, -6.97885099, 5.73946117, -1.88356299, 0.31069819)
NEAREST = 12582912.0
FIRST = 64
VMEM = 48 * 2**20


def swapped(block, axis, mask):
    count = lax.axis_size(axis)
    return lax.ppermute(block, axis, [(at, at ^ mask) for at in range(count)])


def after(value, *earlier):
    return lax.optimization_barrier((value, *earlier))[0]


def turned(u, v, turns):
    part = turns - ((turns + NEAREST) - NEAREST)
    square = part * part
    sine, cosine = SIN[-1], COS[-1]
    for term in SIN[-2::-1]:
        sine = sine * square + term
    for term in COS[-2::-1]:
        cosine = cosine * square + term
    sine = sine * part
    cosine, sine = 1.0 - sine * sine, sine * cosine
    return u * cosine - v * sine, v * cosine + u * sine


def halves(y, turns):
    return turned(y[:, :128], y[:, 128:], turns)


def packed(y, turns):
    u, v = halves(y, turns)
    return jnp.concatenate([u, v], -1).astype(jnp.bfloat16)


def product(left, right, kern):
    return jnp.dot(jnp.concatenate([left, right], -1), kern, preferred_element_type=jnp.float32)


def split_pairs(y, turns):
    u, v = halves(y, turns)
    low = lax.broadcasted_iota(jnp.int32, u.shape, 1) < u.shape[1] // 2
    half = u.shape[1] // 2
    even = jnp.where(low, u, pltpu.roll(v, half, 1))
    odd = jnp.where(low, pltpu.roll(u, half, 1), v)
    return even.astype(jnp.bfloat16), odd.astype(jnp.bfloat16)


def prepare(at, src_in, freq_in, kern_in, src, freq, wide):
    turn = 1.0 / (2.0 * math.pi)
    lanes = lax.broadcasted_iota(jnp.int32, (128, 128), 1) < 64
    for level in range(4):
        rows = src_in[level].T * turn
        both = jnp.concatenate([rows, rows], -1)
        low = lax.broadcasted_iota(jnp.int32, both.shape, 1) < 64
        src[level] = jnp.where(low, both, pltpu.roll(both, both.shape[0] - 1, 0))
        rows = freq_in[level].T
        freq[level] = jnp.concatenate([rows, rows], -1)
        for b in range(2):
            for c in range(2):
                kern = kern_in[level, b ^ at[level], c ^ at[level]].astype(jnp.float32)
                over = pltpu.roll(kern, 64, 1)
                none = jnp.zeros_like(kern)
                forms = [
                    jnp.concatenate([jnp.where(lanes, kern, none), jnp.where(lanes, over, none)], -1),
                    jnp.concatenate([jnp.where(lanes, none, over), jnp.where(lanes, none, kern)], -1),
                ]
                for t in range(2):
                    form = forms[t].astype(jnp.bfloat16)
                    if level == 0:
                        wide[level, b, pl.ds(256 * c + 128 * t, 128)] = form
                    else:
                        for part in range(2):
                            wide[level, b, pl.ds(256 * c + 128 * part + 64 * t, 64)] = form[64 * part : 64 * part + 64]


def first_levels(low, count, early, at, x0, x1, x2, x3, kern0, kern1, src, freq, *outs):
    x = (x0, x1, x2, x3)
    pairs = outs[0].shape[1]
    rows = pairs * count
    chip, here = at[0], at[2]
    block = here if early else pl.program_id(0)
    first = block * (8 * pairs) + chip * (2 * pairs)
    turns = [freq[level, 0, low : low + count] for level in range(2)]

    def source(level, k, p):
        return src[level, chip ^ k, 0, pl.ds(first + 2 * p, 1)]

    def raw(block):
        both = block[0].reshape(pairs, 2, count, 128)
        return jnp.concatenate([both[:, 0].reshape(rows, 128), both[:, 1].reshape(rows, 128)], -1)

    left = jnp.concatenate([raw(x[0]), raw(x[1])], 0)
    right = jnp.concatenate([raw(x[2]), raw(x[3])], 0)
    mid = [[None, None], [None, None]]
    for b0 in range(2):
        y = product(left, right, kern0[0, b0])
        for b1 in range(2):
            mid[b0][b1] = jnp.concatenate(
                [
                    packed(
                        y[b1 * rows + p * count : b1 * rows + (p + 1) * count],
                        source(0, 2 * b0 + b1, p) * turns[0],
                    )
                    for p in range(pairs)
                ],
                0,
            )
    left = jnp.concatenate([mid[0][0], mid[1][0]], 0)
    right = jnp.concatenate([mid[0][1], mid[1][1]], 0)
    for b1 in range(2):
        y = product(left, right, kern1[0, b1])
        for b0 in range(2):
            for p in range(pairs):
                outs[2 * b0 + b1][0, p] = packed(
                    y[b0 * rows + p * count : b0 * rows + (p + 1) * count],
                    source(1, 2 * b0 + b1, p) * turns[1],
                )


def level_two(low, count, at, own, other, kern, src, freq, boxes, outs):
    pairs = own[0].shape[1]
    chip = at[0]
    for n in range(own[0].shape[0]):
        part, near, far = boxes(n)
        turns = freq[0, far, low : low + count]
        first = near * (8 * pairs) + chip * (2 * pairs)
        left, right = (
            jnp.concatenate([x[part].reshape(pairs * count, 256) for x in state], 0) for state in (own, other)
        )
        y = product(left, right, kern[0, 0])
        for k in range(4):
            for p in range(pairs):
                row = (k * pairs + p) * count
                angle = src[0, chip ^ k, 0, pl.ds(first + 2 * p, 1)] * turns
                outs(n, k, p, packed(y[row : row + count], angle))


def level_three(low, count, back, at, x, kern, src, freq, outs):
    parts = len(x)
    pairs = x[0].shape[1]
    chip, here = at[0], at[2]
    for q in range(parts // 2):
        left = x[q][...].reshape(4 * pairs * count, 256)
        right = x[q + parts // 2][...].reshape(4 * pairs * count, 256)
        for b in range(2):
            to = here ^ (q + b * (parts // 2))
            turns = freq[0, to, low : low + count]
            y = product(left, right, kern[0, b])
            for k in range(4):
                chunk, near = (chip, chip ^ k) if back else (chip ^ k, chip)
                first = here * (8 * pairs) + near * (2 * pairs)
                for p in range(pairs):
                    row = (k * pairs + p) * count
                    angle = src[0, chunk, 0, pl.ds(first + 2 * p, 1)] * turns
                    outs[k][2 * p, to], outs[k][2 * p + 1, to] = split_pairs(y[row : row + count], angle)


def third_level(low, count, at, *refs):
    own, other, (kern, src, freq), outs = refs[:4], refs[4:8], refs[8:11], refs[11:]
    here = at[2]

    def put(n, k, p, value):
        outs[k][n, p] = value

    level_two(low, count, at, own, other, kern, src, freq, lambda n: (n, n, here), put)


def fourth_level(low, count, at, *refs):
    x, (kern, src, freq), outs = refs[:-7], refs[-7:-4], refs[-4:]
    level_three(low, count, True, at, x, kern, src, freq, outs)


def last_levels(low, count, at, *refs):
    own, other, (kern2, src2, freq2, kern3, src3, freq3) = refs[:4], refs[4:8], refs[8:14]
    outs, held = refs[14:18], refs[18:]
    here = at[2]

    def put(n, k, p, value):
        held[n][k, p] = value

    level_two(low, count, at, own, other, kern2, src2, freq2, lambda n: (n, here, here ^ n), put)
    level_three(low, count, False, at, held, kern3, src3, freq3, outs)


def gather(spans, at, *refs):
    count = 4 * len(spans)
    parts, out, sems = refs[:count], refs[count], refs[count + 1]
    copies = []
    for c, (low, size) in enumerate(spans):
        for k in range(4):
            n = 4 * c + k
            copies.append(
                pltpu.make_async_copy(parts[n], out.at[at[0] ^ k, :, :, pl.ds(low, size)], sems.at[n])
            )
    for copy in copies:
        copy.start()
    for copy in copies:
        copy.wait()


def whole(shape):
    return pl.BlockSpec(shape, lambda *_: (0,) * len(shape))


def call(kernel, at, operands, outs, scratch=(), grid=(1,), in_specs=None, out_specs=None):
    return pl.pallas_call(
        kernel,
        out_shape=outs,
        grid_spec=pltpu.PrefetchScalarGridSpec(
            num_scalar_prefetch=1,
            grid=grid,
            in_specs=in_specs or [whole(x.shape) for x in operands],
            out_specs=out_specs or [whole(x.shape) for x in outs],
            scratch_shapes=list(scratch),
        ),
        compiler_params=pltpu.CompilerParams(vmem_limit_bytes=VMEM),
        cost_estimate=pl.CostEstimate(
            flops=0,
            bytes_accessed=0,
            transcendentals=0,
        ),
    )(at, *operands)


def body(weights, kernels, src_phase, freq_phase):
    n_src, n_freq = lax.axis_size("src"), lax.axis_size("freq")
    src_index, here = lax.axis_index("src"), lax.axis_index("freq")
    s_dev, f_dev, _ = weights.shape
    bits = n_src.bit_length() - 1
    shift = bits - 2
    chip = src_index >> shift
    rest = src_index & ((1 << shift) - 1)
    side = src_index >> (shift - 1) & 1
    near = s_dev // n_freq
    each = near // 4
    pairs = each // 2
    spans = ((0, FIRST), (FIRST, f_dev - FIRST))
    at = jnp.stack([chip, rest, here]).astype(jnp.int32)
    bf16 = jnp.bfloat16

    raw = weights.reshape(n_freq, 4, each, f_dev, 128)

    low, count = spans[0]
    out_a = [
        lax.dynamic_slice(raw, (0, chip ^ k, 0, low, 0), (n_freq, 1, each, count, 128)).reshape(n_freq, each, count, 128)
        for k in range(4)
    ]
    a3 = swapped(out_a[3], "src", 3 << shift)
    a2 = swapped(out_a[2], "src", 2 << shift)
    a1 = swapped(out_a[1], "src", 1 << shift)

    low, count = spans[1]
    out_f = [
        lax.dynamic_slice(raw, (here ^ q, 0, 0, low, 0), (1, 4, each, count, 128)).reshape(4, each, count, 128)
        for q in range(n_freq)
    ]
    moved = [out_f[0]] + [swapped(out_f[q], "freq", q) for q in range(1, n_freq)]
    out_b = [jnp.stack([lax.dynamic_index_in_dim(x, chip ^ k, 0, False) for x in moved], 0) for k in range(4)]
    b3 = swapped(after(out_b[3], a3), "src", 3 << shift)
    b2 = swapped(after(out_b[2], a2), "src", 2 << shift)
    b1 = swapped(after(out_b[1], a1), "src", 1 << shift)

    flips = jnp.stack([chip >> 1, chip & 1, side, here // (n_freq // 2)]).astype(jnp.int32)
    boxes, columns = src_phase.shape[2], freq_phase.shape[2]
    src, freq, wide = call(
        prepare,
        after(flips, out_f[3]),
        [src_phase, freq_phase, kernels],
        [
            jax.ShapeDtypeStruct((4, boxes, 128), jnp.float32),
            jax.ShapeDtypeStruct((4, columns, 128), jnp.float32),
            jax.ShapeDtypeStruct((4, 2, 512, 256), bf16),
        ],
    )
    src = src.reshape(4, 4, 1 << shift, s_dev, 128)
    freq = freq.reshape(4, n_freq, f_dev, 128)

    def tables(level, outputs=2):
        return [
            pl.BlockSpec((1, outputs, 512, 256), lambda *_: (level, 0, 0, 0)),
            pl.BlockSpec((1, 4, 1, s_dev, 128), lambda *a: (level, 0, a[-1][1], 0, 0)),
            pl.BlockSpec((1, n_freq, f_dev, 128), lambda *_: (level, 0, 0, 0)),
        ]

    def levels01(x, span, early):
        low, count = span
        rows = 4 * n_freq * pairs * count
        return call(
            functools.partial(first_levels, low, count, early),
            at,
            [*x, wide, wide, src, freq],
            [jax.ShapeDtypeStruct((n_freq, pairs, count, 256), bf16)] * 4,
            grid=(n_freq,),
            in_specs=[pl.BlockSpec((1, each, count, 128), lambda m, a: (m, 0, 0, 0))] * 4
            + [
                pl.BlockSpec((1, 2, 512, 256), lambda m, a: (0, 0, 0, 0)),
                pl.BlockSpec((1, 2, 512, 256), lambda m, a: (1, 0, 0, 0)),
                pl.BlockSpec((2, 4, 1, s_dev, 128), lambda m, a: (0, 0, a[1], 0, 0)),
                pl.BlockSpec((2, 1, f_dev, 128), lambda m, a: (0, a[2] ^ m if early else a[2], 0, 0)),
            ],
            out_specs=[pl.BlockSpec((1, pairs, count, 256), lambda m, a: (m, 0, 0, 0))] * 4,
        )

    def core(state):
        return [swapped(x, "src", 1 << (shift - 1)) for x in state]

    def back_shapes(count):
        return [jax.ShapeDtypeStruct((each, n_freq, count, 128), bf16)] * 4

    low, count = spans[0]
    state_a = levels01([out_a[0], a1, a2, a3], spans[0], False)
    sent = call(
        functools.partial(third_level, low, count),
        at,
        [*state_a, *core(state_a), wide, src, freq],
        [jax.ShapeDtypeStruct((n_freq, pairs, count, 256), bf16)] * 4,
        in_specs=[whole(state_a[0].shape)] * 8 + tables(2, outputs=1),
    )
    home = [sent[0], None, None, None]
    for k, earlier in ((3, b3), (2, b2), (1, b1)):
        home[k] = swapped(after(sent[k], earlier), "src", k << shift)

    low, count = spans[1]
    state_b = levels01([after(out_b[0], sent[0]), b1, b2, b3], spans[1], True)
    back_b = call(
        functools.partial(last_levels, low, count),
        at,
        [*state_b, *core(state_b), wide, src, freq, wide, src, freq],
        back_shapes(count),
        scratch=[pltpu.VMEM((4, pairs, count, 256), bf16)] * n_freq,
        in_specs=[whole(state_b[0].shape)] * 8 + tables(2, outputs=1) + tables(3),
    )
    end_b = [back_b[0], None, None, None]
    for k in (3, 2, 1):
        end_b[k] = swapped(after(back_b[k], home[k]), "src", k << shift)

    low, count = spans[0]
    home = [after(x, back_b[0]) for x in home]
    cross = [
        jnp.stack([lax.dynamic_index_in_dim(x, here ^ q, 0, False) for x in home], 0) for q in range(n_freq)
    ]
    got = [cross[0]] + [swapped(cross[q], "freq", q) for q in range(1, n_freq)]
    end_a = call(
        functools.partial(fourth_level, low, count),
        at,
        [*got, wide, src, freq],
        back_shapes(count),
        in_specs=[whole(got[0].shape)] * n_freq + tables(3),
    )

    ends = [*end_a, *end_b]
    out = call(
        functools.partial(gather, spans),
        jnp.reshape(chip, (1,)).astype(jnp.int32),
        ends,
        [jax.ShapeDtypeStruct((4, each, n_freq, f_dev, 128), bf16)],
        scratch=[pltpu.SemaphoreType.DMA((len(ends),))],
        in_specs=[pl.BlockSpec(memory_space=pl.ANY)] * len(ends),
        out_specs=[pl.BlockSpec(memory_space=pl.ANY)],
    )[0]
    return out.reshape(near, n_freq * f_dev, 128)


def solution(mesh):
    placed = (P("src", "freq", None), P(), P(), P())
    return jax.shard_map(
        body, mesh=mesh, in_specs=placed, out_specs=P(("src", "freq"), None, None), check_vma=False
    )
```

time: 143 us -> 119 us (0.83)
  the two profiles are of different devices: /device:TPU:8 before, /device:TPU:0 now
where the time goes in v2:
time: 119 us; the launch traced here: 118 us
  waiting for transfers between devices  57.2 us (48%)
  starting transfers between devices  27.5 us (23%)
  Pallas kernels  23.9 us (20%)
  local copies, waits for them, and re-layouts  9.05 us (8%)
    ppermute x26, waiting for transfers between devices, swapped(): return lax.ppermute(block, axis, [(at, at ^ mask) for at in range(count)])  57.2 us
    ppermute x26, starting transfers between devices, swapped(): return lax.ppermute(block, axis, [(at, at ^ mask) for at in range(count)])  27.5 us
    pallas_call x7, Pallas kernels, call(): pl.pallas_call(kernel, out_shape=outs, grid_spec=pltpu.PrefetchScalarGrid...  23.9 us
    dynamic_slice x4, local copies, waits for them, and re-layouts, body(): lax.dynamic_index_in_dim(x, chip ^ k, 0, False)  3.55 us
  transfers between devices with their start and end apart: 26, of which 8 were waited for; matrix products, arithmetic and copies ran while one was open for 5% of the time, Pallas kernels for 15%

profile of v2, /device:TPU:0, one launch (start us, length us, event | category | flops | bytes accessed | tf_op | source)
XLA Modules:
  0.0 118.3 jit_solution(16607311042303172074)
XLA Ops:
  0.0 2.1 %dynamic-slice_bitcast_fusion.3 = (bf16[4,4,64,128]{3,2,1,0:T(8,128)(2,1)}, bf16[4,4,64,128]{3,2,1,0:T(8,128)(2,1)S(1)}, bf16[4,4,64,128]{3,2,1,0:T(8,128)(2,1)S(1)}, bf16[4,4,64,128]{3,2,1,0:T(8,128)(2,1)S(1)}) fusion(bf16[4,4,4,128,128]{4,3,2,1,0:T(8,128)(2,1)} %bitcast.45, s32[]{:T(128)S(6)} %select_n.76, s32[]{:T(128)S(6)} %select_n.75, ...), kind=kLoop, calls=%fused_computation.11 | loop fusion | bytes 2097168 | tf_op jit(solution)/shard_map/reshape | solution.py:259
  2.1 5.1 %collective-permute-start.2 = (bf16[4,4,64,128]{3,2,1,0:T(8,128)(2,1)}, bf16[4,4,64,128]{3,2,1,0:T(8,128)(2,1)S(1)}, u32[]{:S(2)}, u32[]{:S(2)}) collective-permute-start(bf16[4,4,64,128]{3,2,1,0:T(8,128)(2,1)} %get-tuple-element.88), channel_id=1, source_target_pairs={{0,24},{4,28},{8,16},{12,20},{16,8},{20,12},{24,0},{28,4},{1,25},{... | collective-permute-start | bytes 786440 | tf_op jit(solution)/shard_map/ppermute | solution.py:20
  7.2 2.0 %dynamic-slice_bitcast_fusion.1 = (bf16[4,4,64,128]{3,2,1,0:T(8,128)(2,1)}, bf16[4,4,64,128]{3,2,1,0:T(8,128)(2,1)}, bf16[4,4,64,128]{3,2,1,0:T(8,128)(2,1)S(1)}) fusion(bf16[4,4,4,128,128]{4,3,2,1,0:T(8,128)(2,1)} %bitcast.46, s32[]{:T(128)S(6)} %select_n.82, s32[]{:T(128)S(6)} %select_n.83, s32[]{:T(128)S(6)} %select_n.78), kind=kLoop, calls=%fused_computation.9 | loop fusion | bytes 1572876 | tf_op jit(solution)/shard_map/reshape | solution.py:268
  9.2 1.5 %collective-permute-start.7 = (bf16[4,4,64,128]{3,2,1,0:T(8,128)(2,1)}, bf16[4,4,64,128]{3,2,1,0:T(8,128)(2,1)}, u32[]{:S(2)}, u32[]{:S(2)}) collective-permute-start(bf16[4,4,64,128]{3,2,1,0:T(8,128)(2,1)} %get-tuple-element.85), channel_id=1, source_target_pairs={{0,1},{1,0},{2,3},{3,2},{4,5},{5,4},{6,7},{7,6},{8,9},{9,8},{10,11... | collective-permute-start | bytes 786440 | tf_op jit(solution)/shard_map/ppermute | solution.py:20
  10.6 1.5 %collective-permute-start.8 = (bf16[4,4,64,128]{3,2,1,0:T(8,128)(2,1)}, bf16[4,4,64,128]{3,2,1,0:T(8,128)(2,1)}, u32[]{:S(2)}, u32[]{:S(2)}) collective-permute-start(bf16[4,4,64,128]{3,2,1,0:T(8,128)(2,1)} %get-tuple-element.86), channel_id=1, source_target_pairs={{0,2},{1,3},{2,0},{3,1},{4,6},{5,7},{6,4},{7,5},{8,10},{9,11},{10,... | collective-permute-start | bytes 786440 | tf_op jit(solution)/shard_map/ppermute | solution.py:20
  12.2 0.8 collective-permute-start
  13.0 1.6 %dynamic-slice_bitcast_fusion.8 = (bf16[1,4,64,128]{3,2,1,0:T(8,128)(2,1)}, bf16[1,4,64,128]{3,2,1,0:T(8,128)(2,1)}, bf16[1,4,64,128]{3,2,1,0:T(8,128)(2,1)S(1)}, bf16[1,4,64,128]{3,2,1,0:T(8,128)(2,1)S(1)}) fusion(bf16[4,4,4,128,128]{4,3,2,1,0:T(8,128)(2,1)} %bitcast.47, s32[]{:T(128)S(6)} %select_n.80, s32[]{:T(128)S(6)} %select_n.85, s32[]{:T(128)S(6)} %select_n.86, ...), kind=kLoop, calls=%fused_computation.16 | loop fusion | bytes 524308 | tf_op jit(solution)/shard_map/jit(dynamic_index_in_dim)/dynamic_slice | solution.py:272
  14.6 2.6 %collective-permute-start.9 = (bf16[4,4,64,128]{3,2,1,0:T(8,128)(2,1)S(1)}, bf16[4,4,64,128]{3,2,1,0:T(8,128)(2,1)S(1)}, u32[]{:S(2)}, u32[]{:S(2)}) collective-permute-start(bf16[4,4,64,128]{3,2,1,0:T(8,128)(2,1)S(1)} %get-tuple-element.87), channel_id=1, source_target_pairs={{0,3},{1,2},{2,1},{3,0},{4,7},{5,6},{6,5},{7,4},{8,11},{9,10},{10,... | collective-permute-start | bytes 786440 | tf_op jit(solution)/shard_map/ppermute | solution.py:20
  17.4 1.9 %shard_map.46 = (f32[4,512,128]{2,1,0:T(8,128)S(1)}, f32[4,512,128]{2,1,0:T(8,128)S(1)}, bf16[4,2,512,256]{3,2,1,0:T(8,128)(2,1)S(1)}) custom-call(s32[4]{0:T(128)S(1)} %pad_add_fusion.1.at, f32[4,64,512]{2,1,0:T(8,128)S(1)} %copy-done.1, f32[4,64,512]{2,1,0:T(8,128)S(1)} %copy-done.2, bf16[4,2,2,128,128]{4,3,2,1,0:T(8,128)(2,1)S(1)} %copy-done.3), custom_call_target="tpu_custom_call" | custom-call | tf_op jit(solution)/shard_map/pallas_call | solution.py:220
  19.3 1.3 %copy-done = bf16[4,2,512,256]{3,2,1,0:T(8,128)(2,1)} copy-done((bf16[4,2,512,256]{3,2,1,0:T(8,128)(2,1)}, bf16[4,2,512,256]{3,2,1,0:T(8,128)(2,1)S(1)}, u32[]{:S(2)}) %copy-start) | copy-done | bytes 2097176
  20.6 9.1 %collective-permute-done.1.x2 = bf16[4,4,64,128]{3,2,1,0:T(8,128)(2,1)S(1)} collective-permute-done((bf16[4,4,64,128]{3,2,1,0:T(8,128)(2,1)S(1)}, bf16[4,4,64,128]{3,2,1,0:T(8,128)(2,1)S(1)}, u32[]{:S(2)}, u32[]{:S(2)}) %collective-permute-start.1) | collective-permute-done | bytes 262176 | tf_op jit(solution)/shard_map/ppermute | solution.py:20
  29.7 5.0 %shard_map.47 = (bf16[4,2,64,256]{3,2,1,0:T(8,128)(2,1)S(1)}, bf16[4,2,64,256]{3,2,1,0:T(8,128)(2,1)S(1)}, bf16[4,2,64,256]{3,2,1,0:T(8,128)(2,1)S(1)}, bf16[4,2,64,256]{3,2,1,0:T(8,128)(2,1)S(1)}) custom-call(s32[3]{0:T(128)S(1)} %pad_add_fusion.at, bf16[4,4,64,128]{3,2,1,0:T(8,128)(2,1)S(1)} %get-tuple-element.91.x0, ...), custom_call_target="tpu_custom_call" | custom-call | tf_op jit(solution)/shard_map/pallas_call | solution.py:220
  35.4 1.0 constant_dynamic-slice_fusion.21
  36.3 1.0 constant_dynamic-slice_fusion.20
  37.4 2.5 %collective-permute-start.12 = (bf16[4,4,64,128]{3,2,1,0:T(8,128)(2,1)S(1)}, bf16[4,4,64,128]{3,2,1,0:T(8,128)(2,1)S(1)}, u32[]{:S(2)}, u32[]{:S(2)}) collective-permute-start(bf16[4,4,64,128]{3,2,1,0:T(8,128)(2,1)S(1)} %pad_maximum_fusion.3), channel_id=1, source_target_pairs={{0,24},{4,28},{8,16},{12,20},{16,8},{20,12},{24,0},{28,4},{1,25},{... | collective-permute-start | bytes 786440 | tf_op jit(solution)/shard_map/ppermute | solution.py:20
  41.4 1.2 %collective-permute-start.10 = (bf16[4,4,64,128]{3,2,1,0:T(8,128)(2,1)S(1)}, bf16[4,4,64,128]{3,2,1,0:T(8,128)(2,1)S(1)}, u32[]{:S(2)}, u32[]{:S(2)}) collective-permute-start(bf16[4,4,64,128]{3,2,1,0:T(8,128)(2,1)S(1)} %pad_maximum_fusion.1), channel_id=1, source_target_pairs={{0,8},{4,12},{8,0},{12,4},{16,24},{20,28},{24,16},{28,20},{1,9},{5... | collective-permute-start | bytes 786440 | tf_op jit(solution)/shard_map/ppermute | solution.py:20
  42.6 2.9 %shard_map.48 = (bf16[4,2,64,256]{3,2,1,0:T(8,128)(2,1)S(1)}, bf16[4,2,64,256]{3,2,1,0:T(8,128)(2,1)S(1)}, bf16[4,2,64,256]{3,2,1,0:T(8,128)(2,1)S(1)}, bf16[4,2,64,256]{3,2,1,0:T(8,128)(2,1)S(1)}) custom-call(s32[3]{0:T(128)S(1)} %pad_add_fusion.at, bf16[4,2,64,256]{3,2,1,0:T(8,128)(2,1)S(1)} %get-tuple-element.47.refs_0_, ...), custom_call_target="tpu_custom_call" | custom-call | tf_op jit(solution)/shard_map/pallas_call | solution.py:220
  45.5 3.1 %collective-permute-done.12.x3 = bf16[4,4,64,128]{3,2,1,0:T(8,128)(2,1)S(1)} collective-permute-done((bf16[4,4,64,128]{3,2,1,0:T(8,128)(2,1)S(1)}, bf16[4,4,64,128]{3,2,1,0:T(8,128)(2,1)S(1)}, u32[]{:S(2)}, u32[]{:S(2)}) %collective-permute-start.12) | collective-permute-done | bytes 262176 | tf_op jit(solution)/shard_map/ppermute | solution.py:20
  48.6 15.2 %collective-permute-done.11.x2 = bf16[4,4,64,128]{3,2,1,0:T(8,128)(2,1)S(1)} collective-permute-done((bf16[4,4,64,128]{3,2,1,0:T(8,128)(2,1)S(1)}, bf16[4,4,64,128]{3,2,1,0:T(8,128)(2,1)S(1)}, u32[]{:S(2)}, u32[]{:S(2)}) %collective-permute-start.11) | collective-permute-done | bytes 262176 | tf_op jit(solution)/shard_map/ppermute | solution.py:20
  63.8 5.1 %shard_map.49 = (bf16[4,2,64,256]{3,2,1,0:T(8,128)(2,1)S(1)}, bf16[4,2,64,256]{3,2,1,0:T(8,128)(2,1)S(1)}, bf16[4,2,64,256]{3,2,1,0:T(8,128)(2,1)S(1)}, bf16[4,2,64,256]{3,2,1,0:T(8,128)(2,1)S(1)}) custom-call(s32[3]{0:T(128)S(1)} %pad_add_fusion.at, bf16[4,4,64,128]{3,2,1,0:T(8,128)(2,1)S(1)} %pad_maximum_fusion.x0, ...), custom_call_target="tpu_custom_call" | custom-call | tf_op jit(solution)/shard_map/pallas_call | solution.py:220
  69.9 2.6 %collective-permute-start.19 = (bf16[4,2,64,256]{3,2,1,0:T(8,128)(2,1)S(1)}, bf16[4,2,64,256]{3,2,1,0:T(8,128)(2,1)S(1)}, u32[]{:S(2)}, u32[]{:S(2)}) collective-permute-start(bf16[4,2,64,256]{3,2,1,0:T(8,128)(2,1)S(1)} %get-tuple-element.69), channel_id=1, source_target_pairs={{0,24},{4,28},{8,16},{12,20},{16,8},{20,12},{24,0},{28,4},{1,25},{... | collective-permute-start | bytes 786440 | tf_op jit(solution)/shard_map/ppermute | solution.py:20
  72.6 1.7 %collective-permute-start.17 = (bf16[4,2,64,256]{3,2,1,0:T(8,128)(2,1)S(1)}, bf16[4,2,64,256]{3,2,1,0:T(8,128)(2,1)S(1)}, u32[]{:S(2)}, u32[]{:S(2)}) collective-permute-start(bf16[4,2,64,256]{3,2,1,0:T(8,128)(2,1)S(1)} %get-tuple-element.63), channel_id=1, source_target_pairs={{0,8},{4,12},{8,0},{12,4},{16,24},{20,28},{24,16},{28,20},{1,9},{5... | collective-permute-start | bytes 786440 | tf_op jit(solution)/shard_map/ppermute | solution.py:20
  74.3 4.5 %shard_map.50 = (bf16[4,4,64,128]{3,2,1,0:T(8,128)(2,1)S(1)}, bf16[4,4,64,128]{3,2,1,0:T(8,128)(2,1)S(1)}, bf16[4,4,64,128]{3,2,1,0:T(8,128)(2,1)S(1)}, bf16[4,4,64,128]{3,2,1,0:T(8,128)(2,1)S(1)}) custom-call(s32[3]{0:T(128)S(1)} %pad_add_fusion.at, bf16[4,2,64,256]{3,2,1,0:T(8,128)(2,1)S(1)} %get-tuple-element.56.refs_0_, ...), custom_call_target="tpu_custom_call" | custom-call | tf_op jit(solution)/shard_map/pallas_call | solution.py:220
  78.8 2.2 %collective-permute-done.19 = bf16[4,2,64,256]{3,2,1,0:T(8,128)(2,1)S(1)} collective-permute-done((bf16[4,2,64,256]{3,2,1,0:T(8,128)(2,1)S(1)}, bf16[4,2,64,256]{3,2,1,0:T(8,128)(2,1)S(1)}, u32[]{:S(2)}, u32[]{:S(2)}) %collective-permute-start.19) | collective-permute-done | bytes 262176 | tf_op jit(solution)/shard_map/ppermute | solution.py:20
  81.0 13.3 %collective-permute-done.18 = bf16[4,2,64,256]{3,2,1,0:T(8,128)(2,1)S(1)} collective-permute-done((bf16[4,2,64,256]{3,2,1,0:T(8,128)(2,1)S(1)}, bf16[4,2,64,256]{3,2,1,0:T(8,128)(2,1)S(1)}, u32[]{:S(2)}, u32[]{:S(2)}) %collective-permute-start.18) | collective-permute-done | bytes 262176 | tf_op jit(solution)/shard_map/ppermute | solution.py:20
  95.1 1.2 %collective-permute-start.25 = (bf16[4,4,64,128]{3,2,1,0:T(8,128)(2,1)S(1)}, bf16[4,4,64,128]{3,2,1,0:T(8,128)(2,1)S(1)}, u32[]{:S(2)}, u32[]{:S(2)}) collective-permute-start(bf16[4,4,64,128]{3,2,1,0:T(8,128)(2,1)S(1)} %get-tuple-element.80), channel_id=1, source_target_pairs={{0,24},{4,28},{8,16},{12,20},{16,8},{20,12},{24,0},{28,4},{1,25},{... | collective-permute-start | bytes 786440 | tf_op jit(solution)/shard_map/ppermute | solution.py:20
  96.9 2.5 %collective-permute-start.22 = (bf16[4,2,64,256]{3,2,1,0:T(8,128)(2,1)S(1)}, bf16[4,2,64,256]{3,2,1,0:T(8,128)(2,1)S(1)}, u32[]{:S(2)}, u32[]{:S(2)}) collective-permute-start(bf16[4,2,64,256]{3,2,1,0:T(8,128)(2,1)S(1)} %pad_maximum_fusion.7), channel_id=1, source_target_pairs={{0,3},{1,2},{2,1},{3,0},{4,7},{5,6},{6,5},{7,4},{8,11},{9,10},{10,... | collective-permute-start | bytes 786440 | tf_op jit(solution)/shard_map/ppermute | solution.py:20
  99.4 4.4 %collective-permute-done.20.refs_1_ = bf16[4,2,64,256]{3,2,1,0:T(8,128)(2,1)S(1)} collective-permute-done((bf16[4,2,64,256]{3,2,1,0:T(8,128)(2,1)S(1)}, bf16[4,2,64,256]{3,2,1,0:T(8,128)(2,1)S(1)}, u32[]{:S(2)}, u32[]{:S(2)}) %collective-permute-start.20) | collective-permute-done | bytes 262176 | tf_op jit(solution)/shard_map/ppermute | solution.py:20
  103.8 5.1 %collective-permute-done.21.refs_2_ = bf16[4,2,64,256]{3,2,1,0:T(8,128)(2,1)S(1)} collective-permute-done((bf16[4,2,64,256]{3,2,1,0:T(8,128)(2,1)S(1)}, bf16[4,2,64,256]{3,2,1,0:T(8,128)(2,1)S(1)}, u32[]{:S(2)}, u32[]{:S(2)}) %collective-permute-start.21) | collective-permute-done | bytes 262176 | tf_op jit(solution)/shard_map/ppermute | solution.py:20
  108.9 3.2 %shard_map.51 = (bf16[4,4,64,128]{3,2,1,0:T(8,128)(2,1)S(1)}, bf16[4,4,64,128]{3,2,1,0:T(8,128)(2,1)S(1)}, bf16[4,4,64,128]{3,2,1,0:T(8,128)(2,1)S(1)}, bf16[4,4,64,128]{3,2,1,0:T(8,128)(2,1)S(1)}) custom-call(s32[3]{0:T(128)S(1)} %pad_add_fusion.at, bf16[4,2,64,256]{3,2,1,0:T(8,128)(2,1)S(1)} %pad_maximum_fusion.4.refs_0_, ...), custom_call_target="tpu_custom_call" | custom-call | tf_op jit(solution)/shard_map/pallas_call | solution.py:220
  112.1 4.8 %collective-permute-done.24.refs_6_ = bf16[4,4,64,128]{3,2,1,0:T(8,128)(2,1)S(1)} collective-permute-done((bf16[4,4,64,128]{3,2,1,0:T(8,128)(2,1)S(1)}, bf16[4,4,64,128]{3,2,1,0:T(8,128)(2,1)S(1)}, u32[]{:S(2)}, u32[]{:S(2)}) %collective-permute-start.24) | collective-permute-done | bytes 262176 | tf_op jit(solution)/shard_map/ppermute | solution.py:20
  116.9 1.4 %shard_map.52 = bf16[4,4,4,128,128]{4,3,2,1,0:T(8,128)(2,1)} custom-call(s32[1]{0:T(128)} %bitcast.at, bf16[4,4,64,128]{3,2,1,0:T(8,128)(2,1)S(1)} %get-tuple-element.71.refs_0_, bf16[4,4,64,128]{3,2,1,0:T(8,128)(2,1)S(1)} %get-tuple-element.72.refs_1_, bf16[4,4,64,128]{3,2,1,0:T(8,128)(2,1)S(1)} %get-tuple-element.73.refs_2_, ...), custom_call_target="tpu_custom_call" | custom-call | tf_op jit(solution)/shard_map/pallas_call | solution.py:220
  (57 shorter events, 4.8 us)
Async XLA Ops:
  0.0 17.4 %copy-start.1 = (f32[4,64,512]{2,1,0:T(8,128)S(1)}, f32[4,64,512]{2,1,0:T(8,128)}, u32[]{:S(2)}) copy-start(f32[4,64,512]{2,1,0:T(8,128)} %src_in.1) | copy-start | bytes 1572868
  0.0 17.4 %copy-start.2 = (f32[4,64,512]{2,1,0:T(8,128)S(1)}, f32[4,64,512]{2,1,0:T(8,128)}, u32[]{:S(2)}) copy-start(f32[4,64,512]{2,1,0:T(8,128)} %freq_in.1) | copy-start | bytes 1572868
  0.0 17.4 %copy-start.3 = (bf16[4,2,2,128,128]{4,3,2,1,0:T(8,128)(2,1)S(1)}, bf16[4,2,2,128,128]{4,3,2,1,0:T(8,128)(2,1)}, u32[]{:S(2)}) copy-start(bf16[4,2,2,128,128]{4,3,2,1,0:T(8,128)(2,1)} %kern_in.1) | copy-start | bytes 1572868
  2.1 12.5 %collective-permute-start.2 = (bf16[4,4,64,128]{3,2,1,0:T(8,128)(2,1)}, bf16[4,4,64,128]{3,2,1,0:T(8,128)(2,1)S(1)}, u32[]{:S(2)}, u32[]{:S(2)}) collective-permute-start(bf16[4,4,64,128]{3,2,1,0:T(8,128)(2,1)} %get-tuple-element.88), channel_id=1, source_target_pairs={{0,24},{4,28},{8,16},{12,20},{16,8},{20,12},{24,0},{28,4},{1,25},{... | collective-permute-start | bytes 786440 | tf_op jit(solution)/shard_map/ppermute | solution.py:20
  9.2 26.2 %collective-permute-start.7 = (bf16[4,4,64,128]{3,2,1,0:T(8,128)(2,1)}, bf16[4,4,64,128]{3,2,1,0:T(8,128)(2,1)}, u32[]{:S(2)}, u32[]{:S(2)}) collective-permute-start(bf16[4,4,64,128]{3,2,1,0:T(8,128)(2,1)} %get-tuple-element.85), channel_id=1, source_target_pairs={{0,1},{1,0},{2,3},{3,2},{4,5},{5,4},{6,7},{7,6},{8,9},{9,8},{10,11... | collective-permute-start | bytes 786440 | tf_op jit(solution)/shard_map/ppermute | solution.py:20
  10.6 25.7 %collective-permute-start.8 = (bf16[4,4,64,128]{3,2,1,0:T(8,128)(2,1)}, bf16[4,4,64,128]{3,2,1,0:T(8,128)(2,1)}, u32[]{:S(2)}, u32[]{:S(2)}) collective-permute-start(bf16[4,4,64,128]{3,2,1,0:T(8,128)(2,1)} %get-tuple-element.86), channel_id=1, source_target_pairs={{0,2},{1,3},{2,0},{3,1},{4,6},{5,7},{6,4},{7,5},{8,10},{9,11},{10,... | collective-permute-start | bytes 786440 | tf_op jit(solution)/shard_map/ppermute | solution.py:20
  12.2 17.5 %collective-permute-start.1 = (bf16[4,4,64,128]{3,2,1,0:T(8,128)(2,1)S(1)}, bf16[4,4,64,128]{3,2,1,0:T(8,128)(2,1)S(1)}, u32[]{:S(2)}, u32[]{:S(2)}) collective-permute-start(bf16[4,4,64,128]{3,2,1,0:T(8,128)(2,1)S(1)} %get-tuple-element.89), channel_id=1, source_target_pairs={{0,16},{4,20},{8,24},{12,28},{16,0},{20,4},{24,8},{28,12},{1,17},{... | collective-permute-start | bytes 786440 | tf_op jit(solution)/shard_map/ppermute | solution.py:20
  12.2 17.5 %collective-permute-start = (bf16[4,4,64,128]{3,2,1,0:T(8,128)(2,1)S(1)}, bf16[4,4,64,128]{3,2,1,0:T(8,128)(2,1)S(1)}, u32[]{:S(2)}, u32[]{:S(2)}) collective-permute-start(bf16[4,4,64,128]{3,2,1,0:T(8,128)(2,1)S(1)} %get-tuple-element.90), channel_id=1, source_target_pairs={{0,8},{4,12},{8,0},{12,4},{16,24},{20,28},{24,16},{28,20},{1,9},{5... | collective-permute-start | bytes 786440 | tf_op jit(solution)/shard_map/ppermute | solution.py:20
  14.6 22.7 %collective-permute-start.9 = (bf16[4,4,64,128]{3,2,1,0:T(8,128)(2,1)S(1)}, bf16[4,4,64,128]{3,2,1,0:T(8,128)(2,1)S(1)}, u32[]{:S(2)}, u32[]{:S(2)}) collective-permute-start(bf16[4,4,64,128]{3,2,1,0:T(8,128)(2,1)S(1)} %get-tuple-element.87), channel_id=1, source_target_pairs={{0,3},{1,2},{2,1},{3,0},{4,7},{5,6},{6,5},{7,4},{8,11},{9,10},{10,... | collective-permute-start | bytes 786440 | tf_op jit(solution)/shard_map/ppermute | solution.py:20
  19.3 1.3 %copy-start = (bf16[4,2,512,256]{3,2,1,0:T(8,128)(2,1)}, bf16[4,2,512,256]{3,2,1,0:T(8,128)(2,1)S(1)}, u32[]{:S(2)}) copy-start(bf16[4,2,512,256]{3,2,1,0:T(8,128)(2,1)S(1)} %get-tuple-element.44.kern0.kern1.refs_8_.refs_11_.refs_4_) | copy-start | bytes 6291460
  29.7 7.6 %copy-start.5 = (bf16[1,4,64,128]{3,2,1,0:T(8,128)(2,1)S(1)}, bf16[1,4,64,128]{3,2,1,0:T(8,128)(2,1)}, u32[]{:S(2)}) copy-start(bf16[1,4,64,128]{3,2,1,0:T(8,128)(2,1)} %get-tuple-element.82) | copy-start | bytes 196612
  34.8 5.2 %copy-start.4 = (bf16[1,4,64,128]{3,2,1,0:T(8,128)(2,1)S(1)}, bf16[1,4,64,128]{3,2,1,0:T(8,128)(2,1)}, u32[]{:S(2)}) copy-start(bf16[1,4,64,128]{3,2,1,0:T(8,128)(2,1)} %get-tuple-element.81) | copy-start | bytes 196612
  34.8 5.8 %collective-permute-start.3 = (bf16[4,2,64,256]{3,2,1,0:T(8,128)(2,1)S(1)}, bf16[4,2,64,256]{3,2,1,0:T(8,128)(2,1)S(1)}, u32[]{:S(2)}, u32[]{:S(2)}) collective-permute-start(bf16[4,2,64,256]{3,2,1,0:T(8,128)(2,1)S(1)} %get-tuple-element.47.refs_0_), channel_id=1, source_target_pairs={{0,4},{4,0},{8,12},{12,8},{16,20},{20,16},{24,28},{28,24},{1,5},{5... | collective-permute-start | bytes 786440 | tf_op jit(solution)/shard_map/ppermute | solution.py:20
  34.9 6.5 %collective-permute-start.4 = (bf16[4,2,64,256]{3,2,1,0:T(8,128)(2,1)S(1)}, bf16[4,2,64,256]{3,2,1,0:T(8,128)(2,1)S(1)}, u32[]{:S(2)}, u32[]{:S(2)}) collective-permute-start(bf16[4,2,64,256]{3,2,1,0:T(8,128)(2,1)S(1)} %get-tuple-element.48.refs_1_), channel_id=1, source_target_pairs={{0,4},{4,0},{8,12},{12,8},{16,20},{20,16},{24,28},{28,24},{1,5},{5... | collective-permute-start | bytes 786440 | tf_op jit(solution)/shard_map/ppermute | solution.py:20
  37.4 11.2 %collective-permute-start.12 = (bf16[4,4,64,128]{3,2,1,0:T(8,128)(2,1)S(1)}, bf16[4,4,64,128]{3,2,1,0:T(8,128)(2,1)S(1)}, u32[]{:S(2)}, u32[]{:S(2)}) collective-permute-start(bf16[4,4,64,128]{3,2,1,0:T(8,128)(2,1)S(1)} %pad_maximum_fusion.3), channel_id=1, source_target_pairs={{0,24},{4,28},{8,16},{12,20},{16,8},{20,12},{24,0},{28,4},{1,25},{... | collective-permute-start | bytes 786440 | tf_op jit(solution)/shard_map/ppermute | solution.py:20
  40.0 2.6 %collective-permute-start.5 = (bf16[4,2,64,256]{3,2,1,0:T(8,128)(2,1)S(1)}, bf16[4,2,64,256]{3,2,1,0:T(8,128)(2,1)S(1)}, u32[]{:S(2)}, u32[]{:S(2)}) collective-permute-start(bf16[4,2,64,256]{3,2,1,0:T(8,128)(2,1)S(1)} %get-tuple-element.49.refs_2_), channel_id=1, source_target_pairs={{0,4},{4,0},{8,12},{12,8},{16,20},{20,16},{24,28},{28,24},{1,5},{5... | collective-permute-start | bytes 786440 | tf_op jit(solution)/shard_map/ppermute | solution.py:20
  40.1 2.6 %collective-permute-start.6 = (bf16[4,2,64,256]{3,2,1,0:T(8,128)(2,1)S(1)}, bf16[4,2,64,256]{3,2,1,0:T(8,128)(2,1)S(1)}, u32[]{:S(2)}, u32[]{:S(2)}) collective-permute-start(bf16[4,2,64,256]{3,2,1,0:T(8,128)(2,1)S(1)} %get-tuple-element.50.refs_3_), channel_id=1, source_target_pairs={{0,4},{4,0},{8,12},{12,8},{16,20},{20,16},{24,28},{28,24},{1,5},{5... | collective-permute-start | bytes 786440 | tf_op jit(solution)/shard_map/ppermute | solution.py:20
  40.6 23.2 %collective-permute-start.11 = (bf16[4,4,64,128]{3,2,1,0:T(8,128)(2,1)S(1)}, bf16[4,4,64,128]{3,2,1,0:T(8,128)(2,1)S(1)}, u32[]{:S(2)}, u32[]{:S(2)}) collective-permute-start(bf16[4,4,64,128]{3,2,1,0:T(8,128)(2,1)S(1)} %pad_maximum_fusion.2), channel_id=1, source_target_pairs={{0,16},{4,20},{8,24},{12,28},{16,0},{20,4},{24,8},{28,12},{1,17},{... | collective-permute-start | bytes 786440 | tf_op jit(solution)/shard_map/ppermute | solution.py:20
  41.4 22.4 %collective-permute-start.10 = (bf16[4,4,64,128]{3,2,1,0:T(8,128)(2,1)S(1)}, bf16[4,4,64,128]{3,2,1,0:T(8,128)(2,1)S(1)}, u32[]{:S(2)}, u32[]{:S(2)}) collective-permute-start(bf16[4,4,64,128]{3,2,1,0:T(8,128)(2,1)S(1)} %pad_maximum_fusion.1), channel_id=1, source_target_pairs={{0,8},{4,12},{8,0},{12,4},{16,24},{20,28},{24,16},{28,20},{1,9},{5... | collective-permute-start | bytes 786440 | tf_op jit(solution)/shard_map/ppermute | solution.py:20
  68.8 3.7 %collective-permute-start.13 = (bf16[4,2,64,256]{3,2,1,0:T(8,128)(2,1)S(1)}, bf16[4,2,64,256]{3,2,1,0:T(8,128)(2,1)S(1)}, u32[]{:S(2)}, u32[]{:S(2)}) collective-permute-start(bf16[4,2,64,256]{3,2,1,0:T(8,128)(2,1)S(1)} %get-tuple-element.56.refs_0_), channel_id=1, source_target_pairs={{0,4},{4,0},{8,12},{12,8},{16,20},{20,16},{24,28},{28,24},{1,5},{5... | collective-permute-start | bytes 786440 | tf_op jit(solution)/shard_map/ppermute | solution.py:20
  68.9 3.7 %collective-permute-start.14 = (bf16[4,2,64,256]{3,2,1,0:T(8,128)(2,1)S(1)}, bf16[4,2,64,256]{3,2,1,0:T(8,128)(2,1)S(1)}, u32[]{:S(2)}, u32[]{:S(2)}) collective-permute-start(bf16[4,2,64,256]{3,2,1,0:T(8,128)(2,1)S(1)} %get-tuple-element.57.refs_1_), channel_id=1, source_target_pairs={{0,4},{4,0},{8,12},{12,8},{16,20},{20,16},{24,28},{28,24},{1,5},{5... | collective-permute-start | bytes 786440 | tf_op jit(solution)/shard_map/ppermute | solution.py:20
  69.4 4.9 %collective-permute-start.15 = (bf16[4,2,64,256]{3,2,1,0:T(8,128)(2,1)S(1)}, bf16[4,2,64,256]{3,2,1,0:T(8,128)(2,1)S(1)}, u32[]{:S(2)}, u32[]{:S(2)}) collective-permute-start(bf16[4,2,64,256]{3,2,1,0:T(8,128)(2,1)S(1)} %get-tuple-element.58.refs_2_), channel_id=1, source_target_pairs={{0,4},{4,0},{8,12},{12,8},{16,20},{20,16},{24,28},{28,24},{1,5},{5... | collective-permute-start | bytes 786440 | tf_op jit(solution)/shard_map/ppermute | solution.py:20
  69.5 4.8 %collective-permute-start.16 = (bf16[4,2,64,256]{3,2,1,0:T(8,128)(2,1)S(1)}, bf16[4,2,64,256]{3,2,1,0:T(8,128)(2,1)S(1)}, u32[]{:S(2)}, u32[]{:S(2)}) collective-permute-start(bf16[4,2,64,256]{3,2,1,0:T(8,128)(2,1)S(1)} %get-tuple-element.59.refs_3_), channel_id=1, source_target_pairs={{0,4},{4,0},{8,12},{12,8},{16,20},{20,16},{24,28},{28,24},{1,5},{5... | collective-permute-start | bytes 786440 | tf_op jit(solution)/shard_map/ppermute | solution.py:20
  69.9 11.1 %collective-permute-start.19 = (bf16[4,2,64,256]{3,2,1,0:T(8,128)(2,1)S(1)}, bf16[4,2,64,256]{3,2,1,0:T(8,128)(2,1)S(1)}, u32[]{:S(2)}, u32[]{:S(2)}) collective-permute-start(bf16[4,2,64,256]{3,2,1,0:T(8,128)(2,1)S(1)} %get-tuple-element.69), channel_id=1, source_target_pairs={{0,24},{4,28},{8,16},{12,20},{16,8},{20,12},{24,0},{28,4},{1,25},{... | collective-permute-start | bytes 786440 | tf_op jit(solution)/shard_map/ppermute | solution.py:20
  72.6 21.8 %collective-permute-start.18 = (bf16[4,2,64,256]{3,2,1,0:T(8,128)(2,1)S(1)}, bf16[4,2,64,256]{3,2,1,0:T(8,128)(2,1)S(1)}, u32[]{:S(2)}, u32[]{:S(2)}) collective-permute-start(bf16[4,2,64,256]{3,2,1,0:T(8,128)(2,1)S(1)} %get-tuple-element.66), channel_id=1, source_target_pairs={{0,16},{4,20},{8,24},{12,28},{16,0},{20,4},{24,8},{28,12},{1,17},{... | collective-permute-start | bytes 786440 | tf_op jit(solution)/shard_map/ppermute | solution.py:20
  72.6 21.8 %collective-permute-start.17 = (bf16[4,2,64,256]{3,2,1,0:T(8,128)(2,1)S(1)}, bf16[4,2,64,256]{3,2,1,0:T(8,128)(2,1)S(1)}, u32[]{:S(2)}, u32[]{:S(2)}) collective-permute-start(bf16[4,2,64,256]{3,2,1,0:T(8,128)(2,1)S(1)} %get-tuple-element.63), channel_id=1, source_target_pairs={{0,8},{4,12},{8,0},{12,4},{16,24},{20,28},{24,16},{28,20},{1,9},{5... | collective-permute-start | bytes 786440 | tf_op jit(solution)/shard_map/ppermute | solution.py:20
  94.5 9.3 %collective-permute-start.20 = (bf16[4,2,64,256]{3,2,1,0:T(8,128)(2,1)S(1)}, bf16[4,2,64,256]{3,2,1,0:T(8,128)(2,1)S(1)}, u32[]{:S(2)}, u32[]{:S(2)}) collective-permute-start(bf16[4,2,64,256]{3,2,1,0:T(8,128)(2,1)S(1)} %pad_maximum_fusion.5), channel_id=1, source_target_pairs={{0,1},{1,0},{2,3},{3,2},{4,5},{5,4},{6,7},{7,6},{8,9},{9,8},{10,11... | collective-permute-start | bytes 786440 | tf_op jit(solution)/shard_map/ppermute | solution.py:20
  95.1 17.0 %collective-permute-start.25 = (bf16[4,4,64,128]{3,2,1,0:T(8,128)(2,1)S(1)}, bf16[4,4,64,128]{3,2,1,0:T(8,128)(2,1)S(1)}, u32[]{:S(2)}, u32[]{:S(2)}) collective-permute-start(bf16[4,4,64,128]{3,2,1,0:T(8,128)(2,1)S(1)} %get-tuple-element.80), channel_id=1, source_target_pairs={{0,24},{4,28},{8,16},{12,20},{16,8},{20,12},{24,0},{28,4},{1,25},{... | collective-permute-start | bytes 786440 | tf_op jit(solution)/shard_map/ppermute | solution.py:20
  96.3 20.6 %collective-permute-start.24 = (bf16[4,4,64,128]{3,2,1,0:T(8,128)(2,1)S(1)}, bf16[4,4,64,128]{3,2,1,0:T(8,128)(2,1)S(1)}, u32[]{:S(2)}, u32[]{:S(2)}) collective-permute-start(bf16[4,4,64,128]{3,2,1,0:T(8,128)(2,1)S(1)} %get-tuple-element.78), channel_id=1, source_target_pairs={{0,16},{4,20},{8,24},{12,28},{16,0},{20,4},{24,8},{28,12},{1,17},{... | collective-permute-start | bytes 786440 | tf_op jit(solution)/shard_map/ppermute | solution.py:20
  96.3 12.6 %collective-permute-start.21 = (bf16[4,2,64,256]{3,2,1,0:T(8,128)(2,1)S(1)}, bf16[4,2,64,256]{3,2,1,0:T(8,128)(2,1)S(1)}, u32[]{:S(2)}, u32[]{:S(2)}) collective-permute-start(bf16[4,2,64,256]{3,2,1,0:T(8,128)(2,1)S(1)} %pad_maximum_fusion.6), channel_id=1, source_target_pairs={{0,2},{1,3},{2,0},{3,1},{4,6},{5,7},{6,4},{7,5},{8,10},{9,11},{10,... | collective-permute-start | bytes 786440 | tf_op jit(solution)/shard_map/ppermute | solution.py:20
  96.9 12.0 %collective-permute-start.22 = (bf16[4,2,64,256]{3,2,1,0:T(8,128)(2,1)S(1)}, bf16[4,2,64,256]{3,2,1,0:T(8,128)(2,1)S(1)}, u32[]{:S(2)}, u32[]{:S(2)}) collective-permute-start(bf16[4,2,64,256]{3,2,1,0:T(8,128)(2,1)S(1)} %pad_maximum_fusion.7), channel_id=1, source_target_pairs={{0,3},{1,2},{2,1},{3,0},{4,7},{5,6},{6,5},{7,4},{8,11},{9,10},{10,... | collective-permute-start | bytes 786440 | tf_op jit(solution)/shard_map/ppermute | solution.py:20
  103.8 13.1 %collective-permute-start.23 = (bf16[4,4,64,128]{3,2,1,0:T(8,128)(2,1)S(1)}, bf16[4,4,64,128]{3,2,1,0:T(8,128)(2,1)S(1)}, u32[]{:S(2)}, u32[]{:S(2)}) collective-permute-start(bf16[4,4,64,128]{3,2,1,0:T(8,128)(2,1)S(1)} %get-tuple-element.76), channel_id=1, source_target_pairs={{0,8},{4,12},{8,0},{12,4},{16,24},{20,28},{24,16},{28,20},{1,9},{5... | collective-permute-start | bytes 786440 | tf_op jit(solution)/shard_map/ppermute | solution.py:20

commit v3 on v0

v3 whole, which is shorter than its diff:
```python
import functools
import math

import jax
import jax.numpy as jnp
from jax import lax
from jax.experimental import pallas as pl
from jax.experimental.pallas import tpu as pltpu
from jax.sharding import PartitionSpec as P

SIN = (4.44288292, -7.3082457, 3.60635441, -0.84611289, 0.10982699)
COS = (1.4142135, -6.97885099, 5.73946117, -1.88356299, 0.31069819)
NEAREST = 12582912.0
VMEM = 12 * 2**20
FIRST = 64
ORDER = (7, 3, 6, 5, 2, 4, 1, 0)
G_F = {3: (1, (7,))}
G_R = ()
G_A = (7, 6, 5)
G_B = (7, 6, 5)
G_C = {3: (7,)}


def after(value, *earlier):
    return lax.optimization_barrier((value, *earlier))[0]


def turned(u, v, turns):
    part = turns - ((turns + NEAREST) - NEAREST)
    square = part * part
    sine, cosine = SIN[-1], COS[-1]
    for term in SIN[-2::-1]:
        sine = sine * square + term
    for term in COS[-2::-1]:
        cosine = cosine * square + term
    sine = sine * part
    cosine, sine = 1.0 - sine * sine, sine * cosine
    return u * cosine - v * sine, v * cosine + u * sine


def packed(y, turns):
    u, v = turned(y[:, :128], y[:, 128:], turns)
    return jnp.concatenate([u, v], -1).astype(jnp.bfloat16)


def split_pairs(y, turns):
    u, v = turned(y[:, :128], y[:, 128:], turns)
    low = lax.broadcasted_iota(jnp.int32, u.shape, 1) < 64
    first = jnp.where(low, u, pltpu.roll(v, 64, 1))
    second = jnp.where(low, pltpu.roll(u, 64, 1), v)
    return first.astype(jnp.bfloat16), second.astype(jnp.bfloat16)


def product(left, right, kern):
    both = [jnp.concatenate(rows, 0) for rows in (left, right)]
    return jnp.dot(jnp.concatenate(both, -1), kern, preferred_element_type=jnp.float32)


def prepare(spans, parts, at, src_in, freq_in, kern_in, src, src_all, src_home, freq_a, freq_b, wide, held):
    turn = 1.0 / (2.0 * math.pi)
    lanes = lax.broadcasted_iota(jnp.int32, (128, 128), 1) < 64
    group, rest, here = at[0], at[1], at[2]
    each = src.shape[2]
    boxes, columns = src_in.shape[2], freq_in.shape[2]
    s_dev, f_dev = at[3], columns // parts
    for level in range(4):
        rows = src_in[level].T * turn
        held[...] = jnp.concatenate([rows, rows], -1)
        for k in range(8):
            first = ((group ^ k) * (boxes // (8 * s_dev)) + rest) * s_dev + group * each
            for e in range(each):
                src[level, k, pl.ds(e, 1)] = held[pl.ds(first + here * (8 * each) + e, 1)]
                if level == 3:
                    own = (group * (boxes // (8 * s_dev)) + rest) * s_dev + here * (8 * each) + (group ^ k) * each
                    src_home[k, pl.ds(e, 1)] = held[pl.ds(own + e, 1)]
                else:
                    for part in range(parts):
                        src_all[level, k, part, pl.ds(e, 1)] = held[pl.ds(first + part * (8 * each) + e, 1)]
        rows = freq_in[level].T
        for part in range(parts):
            for (low, count), out in zip(spans, (freq_a, freq_b), strict=True):
                base = part * f_dev + low
                half = count // 2
                out[level, part] = jnp.concatenate([rows[base : base + half], rows[base + half : base + count]], -1)
        for b in range(2):
            for c in range(2):
                if level < 3:
                    bit = group >> (2 - level) & 1
                    places = [(level, kern_in[level, b ^ bit, c ^ bit])]
                else:
                    bit = at[4]
                    places = [(3, kern_in[3, b, c]), (4, kern_in[3, b ^ bit, c ^ bit])]
                for place, kern in places:
                    kern = kern.astype(jnp.float32)
                    over = pltpu.roll(kern, 64, 1)
                    none = jnp.zeros_like(kern)
                    forms = [
                        jnp.concatenate([jnp.where(lanes, kern, none), jnp.where(lanes, over, none)], -1),
                        jnp.concatenate([jnp.where(lanes, none, over), jnp.where(lanes, none, kern)], -1),
                    ]
                    for t in range(2):
                        form = forms[t].astype(jnp.bfloat16)
                        if level == 0:
                            wide[place, b, pl.ds(256 * c + 128 * t, 128)] = form
                        else:
                            for ri in range(2):
                                row = 256 * c + 128 * ri + 64 * t
                                wide[place, b, pl.ds(row, 64)] = form[64 * ri : 64 * ri + 64]


def ordered(parts):
    return [parts[ORDER.index(k)] for k in range(8)]


def raw(rows):
    half = rows.shape[0] // 2
    return jnp.concatenate([rows[:half], rows[half:]], -1)


def three_levels(state, tiles, half, wide, angle):
    for level in range(3):
        mask = 4 >> level
        lows = [k for k in range(8) if not k & mask]
        left = [state[k][tile] for k in lows for tile in tiles]
        right = [state[k | mask][tile] for k in lows for tile in tiles]
        new = [None] * 8
        for b in range(2):
            y = product(left, right, wide[level, b])
            for n, k in enumerate(lows):
                to = k | b * mask
                new[to] = {}
                for i, tile in enumerate(tiles):
                    row = (n * len(tiles) + i) * half
                    new[to][tile] = packed(y[row : row + half], angle(level, to, tile))
        state = new
    return state


def all_levels(at, *refs):
    x, (wide, src, freq), outs = ordered(refs[:8]), refs[8:11], refs[11:]
    each, _, _, count, _ = outs[0].shape
    half = count // 2
    tiles = [(part, e) for part in range(2) for e in range(each)]
    state = [{(part, e): raw(x[k][part, 0, e]) for part, e in tiles} for k in range(8)]

    def angle(level, k, tile):
        part, e = tile
        return src[level, k, e : e + 1] * freq[level, part, 0]

    state = three_levels(state, tiles, half, wide, angle)
    keys = [(k, e) for k in range(8) for e in range(each)]
    left = [state[k][0, e] for k, e in keys]
    right = [state[k][1, e] for k, e in keys]
    for part in range(2):
        y = product(left, right, wide[3, part])
        for n, (k, e) in enumerate(keys):
            first, second = split_pairs(y[n * half : n * half + half], angle(3, k, (part, e)))
            outs[k][e, part, 0, :half] = first
            outs[k][e, part, 0, half:] = second


def first_levels(parts, at, *refs):
    x, (wide, src, freq), outs = ordered(refs[:8]), refs[8:11], refs[11:]
    _, each, half, _ = outs[0].shape
    here = at[2]
    tiles = [(part, e) for part in range(parts) for e in range(each)]
    state = [{(part, e): raw(x[k][part, e]) for part, e in tiles} for k in range(8)]

    def angle(level, k, tile):
        part, e = tile
        return src[level, k, part, e : e + 1] * freq[level, here]

    state = three_levels(state, tiles, half, wide, angle)
    for k in range(8):
        for part, e in tiles:
            outs[k][part, e] = state[k][part, e]


def last_level(parts, at, *refs):
    x, (wide, src, freq), outs = refs[:parts], refs[parts : parts + 3], refs[parts + 3 :]
    _, each, half, _ = x[0].shape
    here = at[2]
    keys = [(k, e) for k in range(8) for e in range(each)]
    for q in range(parts // 2):
        left = [x[q][k, e] for k, e in keys]
        right = [x[q + parts // 2][k, e] for k, e in keys]
        for b in range(2):
            to = here ^ (q + b * (parts // 2))
            y = product(left, right, wide[4, b])
            for n, (k, e) in enumerate(keys):
                angle = src[k, e : e + 1] * freq[3, to]
                first, second = split_pairs(y[n * half : n * half + half], angle)
                outs[k][e, to, :half] = first
                outs[k][e, to, half:] = second


def cut_groups(span, at, x, *refs):
    low, count = span
    outs, sems = refs[:-1], refs[-1]
    copies = [
        pltpu.make_async_copy(x.at[:, at[0] ^ k, :, pl.ds(low, count)], out, sems.at[k]) for k, out in enumerate(outs)
    ]
    for copy in copies:
        copy.start()
    for copy in copies:
        copy.wait()


def cut_parts(span, at, x, *refs):
    low, count = span
    outs, sems = refs[:-1], refs[-1]
    copies = [
        pltpu.make_async_copy(x.at[at[2] ^ q, :, :, pl.ds(low, count)], out, sems.at[q]) for q, out in enumerate(outs)
    ]
    for copy in copies:
        copy.start()
    for copy in copies:
        copy.wait()


def regroup(at, *refs):
    outs = refs[-8:]
    for q, x in enumerate(refs[:-8]):
        for k in range(8):
            outs[k][at[2] ^ q] = x[at[0] ^ k]


def regroup_home(at, *refs):
    for k, x in enumerate(ordered(refs[:8])):
        for q, out in enumerate(refs[8:]):
            out[k] = x[at[2] ^ q]


def gather(span, at, *refs):
    parts, out, sems = ordered(refs[:8]), refs[-2], refs[-1]
    low, count = span
    copies = [
        pltpu.make_async_copy(parts[k], out.at[at[0] ^ k, :, :, pl.ds(low, count)], sems.at[k])
        for k in range(8)
    ]
    for copy in copies:
        copy.start()
    for copy in copies:
        copy.wait()


def whole(shape):
    return pl.BlockSpec(shape, lambda *_: (0,) * len(shape))


def call(kernel, at, operands, outs, scratch=(), grid=(1,), in_specs=None, out_specs=None, aliases=None, vmem=VMEM):
    return pl.pallas_call(
        kernel,
        out_shape=outs,
        grid_spec=pltpu.PrefetchScalarGridSpec(
            num_scalar_prefetch=1,
            grid=grid,
            in_specs=in_specs or [whole(x.shape) for x in operands],
            out_specs=out_specs or [whole(x.shape) for x in outs],
            scratch_shapes=list(scratch),
        ),
        input_output_aliases=aliases or {},
        compiler_params=pltpu.CompilerParams(vmem_limit_bytes=vmem),
    )(at, *operands)


def body(weights, kernels, src_phase, freq_phase):
    n_src, n_freq = lax.axis_size("src"), lax.axis_size("freq")
    src_index, here = lax.axis_index("src"), lax.axis_index("freq")
    s_dev, f_dev, _ = weights.shape
    shift = n_src.bit_length() - 4
    group, rest = src_index >> shift, src_index & ((1 << shift) - 1)
    each = s_dev // n_freq // 8
    pairs = n_freq // 2
    first = FIRST * f_dev // 128
    spans = ((0, first), (first, f_dev - first))
    bf16 = jnp.bfloat16
    at = jnp.stack([group, rest, here, jnp.full_like(here, s_dev), here // pairs]).astype(jnp.int32)
    raw_rows = weights.reshape(n_freq, 8, each, f_dev, 128)
    anywhere = pl.BlockSpec(memory_space=pl.ANY)

    def over_src(block, k):
        return lax.ppermute(block, "src", [(i, i ^ k << shift) for i in range(n_src)])

    def over_freq(block, q):
        return lax.ppermute(block, "freq", [(j, j ^ q) for j in range(n_freq)])

    def sent(parts, gates):
        got = [*parts]
        for k in range(1, 8):
            got[k] = over_src(after(parts[k], *gates[k]) if k in gates else parts[k], k)
        return got

    def cut(kernel, span, at, shape, many, vmem):
        return call(
            functools.partial(kernel, span),
            at,
            [raw_rows],
            [jax.ShapeDtypeStruct(shape, bf16)] * many,
            scratch=[pltpu.SemaphoreType.DMA((many,))],
            in_specs=[pl.BlockSpec(memory_space=pltpu.HBM)],
            out_specs=[anywhere] * many,
            vmem=vmem,
        )

    def in_order(parts):
        return [parts[k] for k in ORDER]

    count_a, count_b = first, f_dev - first
    out_a = cut(cut_groups, spans[0], at, (n_freq, each, count_a, 128), 8, VMEM)
    in_a = sent(out_a, {})
    out_f = cut(cut_parts, spans[1], after(at, out_a[0]), (8, each, count_b, 128), n_freq, VMEM)
    src, src_all, src_home, freq_a, freq_b, wide = call(
        functools.partial(prepare, spans, n_freq),
        after(at, out_f[0]),
        [src_phase, freq_phase, kernels],
        [
            jax.ShapeDtypeStruct((4, 8, each, 128), jnp.float32),
            jax.ShapeDtypeStruct((3, 8, n_freq, each, 128), jnp.float32),
            jax.ShapeDtypeStruct((8, each, 128), jnp.float32),
            jax.ShapeDtypeStruct((4, n_freq, count_a // 2, 128), jnp.float32),
            jax.ShapeDtypeStruct((4, n_freq, count_b // 2, 128), jnp.float32),
            jax.ShapeDtypeStruct((5, 2, 512, 256), bf16),
        ],
        scratch=[pltpu.VMEM((src_phase.shape[2], 128), jnp.float32)],
    )
    waits = {q: [wide] * w + [in_a[k] for k in ks] for q, (w, ks) in G_F.items()}
    moved = [out_f[0]] + [
        over_freq(after(out_f[q], *waits[q]) if q in waits else out_f[q], q) for q in range(1, n_freq)
    ]
    out_b = call(regroup, after(at, *[in_a[k] for k in G_R]) if G_R else at, moved, [jax.ShapeDtypeStruct((n_freq, each, count_b, 128), bf16)] * 8)
    in_b = sent(out_b, {})

    back_a = call(
        functools.partial(first_levels, n_freq),
        at,
        [*in_order(in_a), wide, src_all, freq_a],
        [jax.ShapeDtypeStruct((n_freq, each, count_a // 2, 256), bf16)] * 8,
    )
    some = [in_b[k] for k in G_A]
    home = sent(back_a, {k: some for k in range(1, 8)})

    x_spec = pl.BlockSpec((2, 1, each, count_b, 128), lambda n, a: (0, n, 0, 0, 0))
    back_b = call(
        all_levels,
        at,
        [
            *[x.reshape(2, pairs, each, count_b, 128) for x in in_order([after(in_b[0], back_a[0]), *in_b[1:]])],
            wide,
            src,
            freq_b.reshape(4, 2, pairs, count_b // 2, 128),
        ],
        [jax.ShapeDtypeStruct((each, 2, pairs, count_b, 128), bf16)] * 8,
        grid=(pairs,),
        in_specs=[x_spec] * 8
        + [
            whole(wide.shape),
            whole(src.shape),
            pl.BlockSpec((4, 2, 1, count_b // 2, 128), lambda n, a: (0, 0, n, 0, 0)),
        ],
        out_specs=[pl.BlockSpec((each, 2, 1, count_b, 128), lambda n, a: (0, 0, n, 0, 0))] * 8,
    )
    back_b = [x.reshape(each, n_freq, count_b, 128) for x in back_b]
    some = [home[k] for k in G_B]
    end_b = sent(back_b, {k: some for k in range(1, 8)})

    cross = call(
        regroup_home,
        after(at, back_b[0]),
        in_order(home),
        [jax.ShapeDtypeStruct((8, each, count_a // 2, 256), bf16)] * n_freq,
    )
    got = [cross[0]] + [
        over_freq(after(cross[q], *[end_b[k] for k in G_C[q]]) if q in G_C else cross[q], q) for q in range(1, n_freq)
    ]
    end_a = call(
        functools.partial(last_level, n_freq),
        at,
        [*got, wide, src_home, freq_a],
        [jax.ShapeDtypeStruct((each, n_freq, count_a, 128), bf16)] * 8,
    )

    def place(span, parts, out=None):
        operands = in_order(parts) if out is None else [*in_order(parts), out]
        return call(
            functools.partial(gather, span),
            at,
            operands,
            [jax.ShapeDtypeStruct((8, each, n_freq, f_dev, 128), bf16)],
            scratch=[pltpu.SemaphoreType.DMA((8,))],
            in_specs=[anywhere] * len(operands),
            out_specs=[anywhere],
            aliases=None if out is None else {9: 0},
        )[0]

    out = place(spans[0], end_a)
    out = place(spans[1], end_b, out)
    return out.reshape(s_dev // n_freq, n_freq * f_dev, 128)


def solution(mesh):
    placed = (P("src", "freq", None), P(), P(), P())
    return jax.shard_map(
        body, mesh=mesh, in_specs=placed, out_specs=P(("src", "freq"), None, None), check_vma=False
    )
```

time: 265 us -> 108 us (0.41)
  waiting for transfers between devices: 143 us -> 43.1 us
  other arithmetic: 82.3 us -> 0 us
  starting transfers between devices: 8.7 us -> 42.2 us
  Pallas kernels: 0 us -> 21 us
  matrix products: 19.3 us -> 0 us
  local copies, waits for them, and re-layouts: 11 us -> 1.69 us
    convert_element_type x5 -> x0, other arithmetic: 76.6 us -> none  [rotate(): (values * jnp.cos(angle) + flipped * jnp.sin(angle)).astype(jnp.bfloat16)]
    ppermute x3 -> x34, waiting for transfers between devices: 119 us -> 43.1 us  [the longest x28 36.2 us: over_src(): lax.ppermute(block, 'src', [(i, i ^ k << shift) for i in range(n_src)])]
    ppermute x3 -> x34, starting transfers between devices: 4.83 us -> 42.2 us  [the longest x28 36.3 us: over_src(): lax.ppermute(block, 'src', [(i, i ^ k << shift) for i in range(n_src)])]
    all_to_all x1 -> x0, waiting for transfers between devices: 24.4 us -> none  [finish_early(): lax.all_to_all(state, 'freq', split_axis=0, concat_axis=1, tiled=True)]
    pallas_call x0 -> x10, Pallas kernels: none -> 21 us  [call(): pl.pallas_call(kernel, out_shape=outs, grid_spec=pltpu.PrefetchScalarGrid...]
    dot_general x10 -> x0, matrix products: 19.3 us -> none  [the longest x3 10.4 us: pair_level(): jnp.dot(state.reshape(-1, width), own_kern, preferred_element_type=jnp.fl...]
    neg x4 -> x0, other arithmetic: 5.19 us -> none  [rotate(): flipped = jnp.concatenate([-values[..., half:], values[..., :half]], -1)]
    all_to_all x1 -> x0, starting transfers between devices: 3.87 us -> none  [finish_early(): lax.all_to_all(state, 'freq', split_axis=0, concat_axis=1, tiled=True)]
  transfers between devices with their start and end apart: 4 -> 34, of which waited for: 3 -> 13; matrix products, arithmetic and copies ran while one was open for 10% -> 0% of each run, Pallas kernels for 0% -> 17%
where the time goes in v3:
time: 108 us
  waiting for transfers between devices  43.1 us (40%)
  starting transfers between devices  42.2 us (39%)
  Pallas kernels  21 us (19%)
  local copies, waits for them, and re-layouts  1.69 us (2%)
    ppermute x28, starting transfers between devices, over_src(): lax.ppermute(block, 'src', [(i, i ^ k << shift) for i in range(n_src)])  36.3 us
    ppermute x28, waiting for transfers between devices, over_src(): lax.ppermute(block, 'src', [(i, i ^ k << shift) for i in range(n_src)])  36.2 us
    pallas_call x10, Pallas kernels, call(): pl.pallas_call(kernel, out_shape=outs, grid_spec=pltpu.PrefetchScalarGrid...  21 us
    ppermute x6, waiting for transfers between devices, over_freq(): return lax.ppermute(block, 'freq', [(j, j ^ q) for j in range(n_freq)])  6.87 us
    ppermute x6, starting transfers between devices, over_freq(): return lax.ppermute(block, 'freq', [(j, j ^ q) for j in range(n_freq)])  5.81 us
  transfers between devices with their start and end apart: 34, of which 13 were waited for; matrix products, arithmetic and copies ran while one was open for 0% of the time, Pallas kernels for 17%

profile of v3, /device:TPU:0, one launch (start us, length us, event | category | flops | bytes accessed | tf_op | source)
XLA Modules:
  0.0 108.2 jit_solution(1713391217958611144)
XLA Ops:
  0.1 1.6 %copy-done = bf16[64,128,128]{2,1,0:T(8,128)(2,1)S(1)} copy-done((bf16[64,128,128]{2,1,0:T(8,128)(2,1)S(1)}, bf16[64,128,128]{2,1,0:T(8,128)(2,1)}, u32[]{:S(2)}) %copy-start) | copy-done | bytes 2097176
  2.5 4.6 %collective-permute-start.2 = (bf16[4,2,64,128]{3,2,1,0:T(8,128)(2,1)S(1)}, bf16[4,2,64,128]{3,2,1,0:T(8,128)(2,1)S(1)}, u32[]{:S(2)}, u32[]{:S(2)}) collective-permute-start(bf16[4,2,64,128]{3,2,1,0:T(8,128)(2,1)S(1)} %get-tuple-element.87), channel_id=1, source_target_pairs={{0,28},{4,24},{8,20},{12,16},{16,12},{20,8},{24,4},{28,0},{1,29},{... | collective-permute-start | bytes 393224 | tf_op jit(solution)/shard_map/ppermute | solution.py:283
  7.7 1.6 %collective-permute-start = (bf16[8,2,64,128]{3,2,1,0:T(8,128)(2,1)S(1)}, bf16[8,2,64,128]{3,2,1,0:T(8,128)(2,1)S(1)}, u32[]{:S(2)}, u32[]{:S(2)}) collective-permute-start(bf16[8,2,64,128]{3,2,1,0:T(8,128)(2,1)S(1)} %get-tuple-element.82), channel_id=1, source_target_pairs={{0,1},{1,0},{2,3},{3,2},{4,5},{5,4},{6,7},{7,6},{8,9},{9,8},{10,11... | collective-permute-start | bytes 786440 | tf_op jit(solution)/shard_map/ppermute | solution.py:286
  9.3 1.5 %collective-permute-start.1 = (bf16[8,2,64,128]{3,2,1,0:T(8,128)(2,1)S(1)}, bf16[8,2,64,128]{3,2,1,0:T(8,128)(2,1)S(1)}, u32[]{:S(2)}, u32[]{:S(2)}) collective-permute-start(bf16[8,2,64,128]{3,2,1,0:T(8,128)(2,1)S(1)} %get-tuple-element.83), channel_id=1, source_target_pairs={{0,2},{1,3},{2,0},{3,1},{4,6},{5,7},{6,4},{7,5},{8,10},{9,11},{10,... | collective-permute-start | bytes 786440 | tf_op jit(solution)/shard_map/ppermute | solution.py:286
  10.8 1.9 %shard_map.48 = (f32[4,8,2,128]{3,2,1,0:T(2,128)S(1)}, f32[3,8,4,2,128]{4,3,2,1,0:T(2,128)S(1)}, f32[8,2,128]{2,1,0:T(2,128)S(1)}, f32[4,4,32,128]{3,2,1,0:T(8,1...) custom-call(s32[5]{0:T(128)S(1)} %stack.15.at, f32[4,64,512]{2,1,0:T(8,128)S(1)} %copy-done.1, ...), custom_call_target="tpu_custom_call" | custom-call | tf_op jit(solution)/shard_map/pallas_call | solution.py:252
  13.9 2.2 %collective-permute-start.11 = (bf16[4,2,64,128]{3,2,1,0:T(8,128)(2,1)S(1)}, bf16[4,2,64,128]{3,2,1,0:T(8,128)(2,1)S(1)}, u32[]{:S(2)}, u32[]{:S(2)}) collective-permute-start(bf16[4,2,64,128]{3,2,1,0:T(8,128)(2,1)S(1)} %get-tuple-element.97), channel_id=1, source_target_pairs={{0,12},{4,8},{8,4},{12,0},{16,28},{20,24},{24,20},{28,16},{1,13},{... | collective-permute-start | bytes 393224 | tf_op jit(solution)/shard_map/ppermute | solution.py:283
  16.1 2.5 %collective-permute-start.12 = (bf16[4,2,64,128]{3,2,1,0:T(8,128)(2,1)S(1)}, bf16[4,2,64,128]{3,2,1,0:T(8,128)(2,1)S(1)}, u32[]{:S(2)}, u32[]{:S(2)}) collective-permute-start(bf16[4,2,64,128]{3,2,1,0:T(8,128)(2,1)S(1)} %get-tuple-element.98), channel_id=1, source_target_pairs={{0,24},{4,28},{8,16},{12,20},{16,8},{20,12},{24,0},{28,4},{1,25},{... | collective-permute-start | bytes 393224 | tf_op jit(solution)/shard_map/ppermute | solution.py:283
  20.0 3.2 %collective-permute-start.13 = (bf16[4,2,64,128]{3,2,1,0:T(8,128)(2,1)S(1)}, bf16[4,2,64,128]{3,2,1,0:T(8,128)(2,1)S(1)}, u32[]{:S(2)}, u32[]{:S(2)}) collective-permute-start(bf16[4,2,64,128]{3,2,1,0:T(8,128)(2,1)S(1)} %get-tuple-element.99), channel_id=1, source_target_pairs={{0,20},{4,16},{8,28},{12,24},{16,4},{20,0},{24,12},{28,8},{1,21},{... | collective-permute-start | bytes 393224 | tf_op jit(solution)/shard_map/ppermute | solution.py:283
  25.8 2.6 %collective-permute-start.4 = (bf16[4,2,64,128]{3,2,1,0:T(8,128)(2,1)S(1)}, bf16[4,2,64,128]{3,2,1,0:T(8,128)(2,1)S(1)}, u32[]{:S(2)}, u32[]{:S(2)}) collective-permute-start(bf16[4,2,64,128]{3,2,1,0:T(8,128)(2,1)S(1)} %get-tuple-element.89), channel_id=1, source_target_pairs={{0,28},{4,24},{8,20},{12,16},{16,12},{20,8},{24,4},{28,0},{1,29},{... | collective-permute-start | bytes 393224 | tf_op jit(solution)/shard_map/ppermute | solution.py:283
  28.4 3.3 %collective-permute-done.13.refs_3_ = bf16[4,2,64,128]{3,2,1,0:T(8,128)(2,1)S(1)} collective-permute-done((bf16[4,2,64,128]{3,2,1,0:T(8,128)(2,1)S(1)}, bf16[4,2,64,128]{3,2,1,0:T(8,128)(2,1)S(1)}, u32[]{:S(2)}, u32[]{:S(2)}) %collective-permute-start.13) | collective-permute-done | bytes 131104 | tf_op jit(solution)/shard_map/ppermute | solution.py:283
  33.0 12.4 %collective-permute-done.15.refs_5_ = bf16[4,2,64,128]{3,2,1,0:T(8,128)(2,1)S(1)} collective-permute-done((bf16[4,2,64,128]{3,2,1,0:T(8,128)(2,1)S(1)}, bf16[4,2,64,128]{3,2,1,0:T(8,128)(2,1)S(1)}, u32[]{:S(2)}, u32[]{:S(2)}) %collective-permute-start.15) | collective-permute-done | bytes 131104 | tf_op jit(solution)/shard_map/ppermute | solution.py:283
  45.4 1.7 %collective-permute-start.8 = (bf16[4,2,64,128]{3,2,1,0:T(8,128)(2,1)S(1)}, bf16[4,2,64,128]{3,2,1,0:T(8,128)(2,1)S(1)}, u32[]{:S(2)}, u32[]{:S(2)}) collective-permute-start(bf16[4,2,64,128]{3,2,1,0:T(8,128)(2,1)S(1)} %get-tuple-element.93), channel_id=1, source_target_pairs={{0,8},{4,12},{8,0},{12,4},{16,24},{20,28},{24,16},{28,20},{1,9},{5... | collective-permute-start | bytes 393224 | tf_op jit(solution)/shard_map/ppermute | solution.py:283
  47.1 1.9 %collective-permute-start.9 = (bf16[4,2,64,128]{3,2,1,0:T(8,128)(2,1)S(1)}, bf16[4,2,64,128]{3,2,1,0:T(8,128)(2,1)S(1)}, u32[]{:S(2)}, u32[]{:S(2)}) collective-permute-start(bf16[4,2,64,128]{3,2,1,0:T(8,128)(2,1)S(1)} %get-tuple-element.94), channel_id=1, source_target_pairs={{0,16},{4,20},{8,24},{12,28},{16,0},{20,4},{24,8},{28,12},{1,17},{... | collective-permute-start | bytes 393224 | tf_op jit(solution)/shard_map/ppermute | solution.py:283
  49.0 4.6 %shard_map.50 = (bf16[4,2,32,256]{3,2,1,0:T(8,128)(2,1)S(1)}, bf16[4,2,32,256]{3,2,1,0:T(8,128)(2,1)S(1)}, bf16[4,2,32,256]{3,2,1,0:T(8,128)(2,1)S(1)}, bf16[4,2...) custom-call(s32[5]{0:T(128)S(1)} %stack.15.at, ...), custom_call_target="tpu_custom_call" | custom-call | tf_op jit(solution)/shard_map/pallas_call | solution.py:252
  53.6 3.1 %collective-permute-done.7 = bf16[4,2,64,128]{3,2,1,0:T(8,128)(2,1)S(1)} collective-permute-done((bf16[4,2,64,128]{3,2,1,0:T(8,128)(2,1)S(1)}, bf16[4,2,64,128]{3,2,1,0:T(8,128)(2,1)S(1)}, u32[]{:S(2)}, u32[]{:S(2)}) %collective-permute-start.7) | collective-permute-done | bytes 131104 | tf_op jit(solution)/shard_map/ppermute | solution.py:283
  56.7 3.4 %collective-permute-start.18 = (bf16[4,2,32,256]{3,2,1,0:T(8,128)(2,1)S(1)}, bf16[4,2,32,256]{3,2,1,0:T(8,128)(2,1)S(1)}, u32[]{:S(2)}, u32[]{:S(2)}) collective-permute-start(bf16[4,2,32,256]{3,2,1,0:T(8,128)(2,1)S(1)} %get-tuple-element.113), channel_id=1, source_target_pairs={{0,24},{4,28},{8,16},{12,20},{16,8},{20,12},{24,0},{28,4},{1,25},{... | collective-permute-start | bytes 393224 | tf_op jit(solution)/shard_map/ppermute | solution.py:283
  60.2 1.7 %collective-permute-start.27 = (bf16[4,2,32,256]{3,2,1,0:T(8,128)(2,1)S(1)}, bf16[4,2,32,256]{3,2,1,0:T(8,128)(2,1)S(1)}, u32[]{:S(2)}, u32[]{:S(2)}) collective-permute-start(bf16[4,2,32,256]{3,2,1,0:T(8,128)(2,1)S(1)} %get-tuple-element.132), channel_id=1, source_target_pairs={{0,12},{4,8},{8,4},{12,0},{16,28},{20,24},{24,20},{28,16},{1,13},{... | collective-permute-start | bytes 393224 | tf_op jit(solution)/shard_map/ppermute | solution.py:283
  62.1 6.6 %shard_map.51 = (bf16[2,2,2,64,128]{4,3,2,1,0:T(8,128)(2,1)S(1)}, bf16[2,2,2,64,128]{4,3,2,1,0:T(8,128)(2,1)S(1)}, bf16[2,2,2,64,128]{4,3,2,1,0:T(8,128)(2,1)S(1...) custom-call(s32[5]{0:T(128)S(1)} %stack.15.at, ...), custom_call_target="tpu_custom_call" | custom-call | tf_op jit(solution)/shard_map/pallas_call | solution.py:252
  68.7 2.9 %collective-permute-start.29 = (bf16[4,2,32,256]{3,2,1,0:T(8,128)(2,1)S(1)}, bf16[4,2,32,256]{3,2,1,0:T(8,128)(2,1)S(1)}, u32[]{:S(2)}, u32[]{:S(2)}) collective-permute-start(bf16[4,2,32,256]{3,2,1,0:T(8,128)(2,1)S(1)} %get-tuple-element.136), channel_id=1, source_target_pairs={{0,16},{4,20},{8,24},{12,28},{16,0},{20,4},{24,8},{28,12},{1,17},{... | collective-permute-start | bytes 393224 | tf_op jit(solution)/shard_map/ppermute | solution.py:283
  71.6 7.5 %collective-permute-done.19.refs_3_ = bf16[4,2,32,256]{3,2,1,0:T(8,128)(2,1)S(1)} collective-permute-done((bf16[4,2,32,256]{3,2,1,0:T(8,128)(2,1)S(1)}, bf16[4,2,32,256]{3,2,1,0:T(8,128)(2,1)S(1)}, u32[]{:S(2)}, u32[]{:S(2)}) %collective-permute-start.19) | collective-permute-done | bytes 131104 | tf_op jit(solution)/shard_map/ppermute | solution.py:283
  79.1 1.5 %collective-permute-start.20 = (bf16[2,4,64,128]{3,2,1,0:T(8,128)(2,1)S(1)}, bf16[2,4,64,128]{3,2,1,0:T(8,128)(2,1)S(1)}, u32[]{:S(2)}, u32[]{:S(2)}) collective-permute-start(bf16[2,4,64,128]{3,2,1,0:T(8,128)(2,1)S(1)} %bitcast.40), channel_id=1, source_target_pairs={{0,28},{4,24},{8,20},{12,16},{16,12},{20,8},{24,4},{28,0},{1,29},{... | collective-permute-start | bytes 393224 | tf_op jit(solution)/shard_map/ppermute | solution.py:283
  80.6 1.4 %collective-permute-done.29.refs_5_ = bf16[4,2,32,256]{3,2,1,0:T(8,128)(2,1)S(1)} collective-permute-done((bf16[4,2,32,256]{3,2,1,0:T(8,128)(2,1)S(1)}, bf16[4,2,32,256]{3,2,1,0:T(8,128)(2,1)S(1)}, u32[]{:S(2)}, u32[]{:S(2)}) %collective-permute-start.29) | collective-permute-done | bytes 131104 | tf_op jit(solution)/shard_map/ppermute | solution.py:283
  83.8 2.8 %collective-permute-done.20.refs_0_ = bf16[2,4,64,128]{3,2,1,0:T(8,128)(2,1)S(1)} collective-permute-done((bf16[2,4,64,128]{3,2,1,0:T(8,128)(2,1)S(1)}, bf16[2,4,64,128]{3,2,1,0:T(8,128)(2,1)S(1)}, u32[]{:S(2)}, u32[]{:S(2)}) %collective-permute-start.20) | collective-permute-done | bytes 131104 | tf_op jit(solution)/shard_map/ppermute | solution.py:283
  87.0 1.9 %collective-permute-start.25 = (bf16[2,4,64,128]{3,2,1,0:T(8,128)(2,1)S(1)}, bf16[2,4,64,128]{3,2,1,0:T(8,128)(2,1)S(1)}, u32[]{:S(2)}, u32[]{:S(2)}) collective-permute-start(bf16[2,4,64,128]{3,2,1,0:T(8,128)(2,1)S(1)} %bitcast.38), channel_id=1, source_target_pairs={{0,16},{4,20},{8,24},{12,28},{16,0},{20,4},{24,8},{28,12},{1,17},{... | collective-permute-start | bytes 393224 | tf_op jit(solution)/shard_map/ppermute | solution.py:283
  90.0 1.9 %collective-permute-done.31.refs_1_ = bf16[8,2,32,256]{3,2,1,0:T(8,128)(2,1)S(1)} collective-permute-done((bf16[8,2,32,256]{3,2,1,0:T(8,128)(2,1)S(1)}, bf16[8,2,32,256]{3,2,1,0:T(8,128)(2,1)S(1)}, u32[]{:S(2)}, u32[]{:S(2)}) %collective-permute-start.31) | collective-permute-done | bytes 262176 | tf_op jit(solution)/shard_map/ppermute | solution.py:286
  91.9 4.9 %collective-permute-done.32.refs_2_ = bf16[8,2,32,256]{3,2,1,0:T(8,128)(2,1)S(1)} collective-permute-done((bf16[8,2,32,256]{3,2,1,0:T(8,128)(2,1)S(1)}, bf16[8,2,32,256]{3,2,1,0:T(8,128)(2,1)S(1)}, u32[]{:S(2)}, u32[]{:S(2)}) %collective-permute-start.32) | collective-permute-done | bytes 262176 | tf_op jit(solution)/shard_map/ppermute | solution.py:286
  96.8 1.7 %collective-permute-start.22 = (bf16[2,4,64,128]{3,2,1,0:T(8,128)(2,1)S(1)}, bf16[2,4,64,128]{3,2,1,0:T(8,128)(2,1)S(1)}, u32[]{:S(2)}, u32[]{:S(2)}) collective-permute-start(bf16[2,4,64,128]{3,2,1,0:T(8,128)(2,1)S(1)} %bitcast.35), channel_id=1, source_target_pairs={{0,24},{4,28},{8,16},{12,20},{16,8},{20,12},{24,0},{28,4},{1,25},{... | collective-permute-start | bytes 393224 | tf_op jit(solution)/shard_map/ppermute | solution.py:283
  98.6 2.1 %shard_map.53 = (bf16[2,4,64,128]{3,2,1,0:T(8,128)(2,1)S(1)}, bf16[2,4,64,128]{3,2,1,0:T(8,128)(2,1)S(1)}, bf16[2,4,64,128]{3,2,1,0:T(8,128)(2,1)S(1)}, bf16[2,4...) custom-call(s32[5]{0:T(128)S(1)} %stack.15.at, ...), custom_call_target="tpu_custom_call" | custom-call | tf_op jit(solution)/shard_map/pallas_call | solution.py:252
  100.7 1.6 %shard_map.54.refs_8_ = bf16[8,2,4,128,128]{4,3,2,1,0:T(8,128)(2,1)} custom-call(s32[5]{0:T(128)S(1)} %stack.15.at, bf16[2,4,64,128]{3,2,1,0:T(8,128)(2,1)S(1)} %get-tuple-element.145.refs_0_, bf16[2,4,64,128]{3,2,1,0:T(8,128)(2,1)S(1)} %get-tuple-element.146.refs_1_, bf16[2,4,64,128]{3,2,1,0:T(8,128)(2,1)S(1)} %get-tuple-element.147.refs_2_, ...), custom_call_target="tpu_custom_call" | custom-call | tf_op jit(solution)/shard_map/pallas_call | solution.py:252
  102.3 2.2 %collective-permute-done.23.refs_3_ = bf16[2,4,64,128]{3,2,1,0:T(8,128)(2,1)S(1)} collective-permute-done((bf16[2,4,64,128]{3,2,1,0:T(8,128)(2,1)S(1)}, bf16[2,4,64,128]{3,2,1,0:T(8,128)(2,1)S(1)}, u32[]{:S(2)}, u32[]{:S(2)}) %collective-permute-start.23) | collective-permute-done | bytes 131104 | tf_op jit(solution)/shard_map/ppermute | solution.py:283
  104.8 1.6 %collective-permute-done.21.refs_1_ = bf16[2,4,64,128]{3,2,1,0:T(8,128)(2,1)S(1)} collective-permute-done((bf16[2,4,64,128]{3,2,1,0:T(8,128)(2,1)S(1)}, bf16[2,4,64,128]{3,2,1,0:T(8,128)(2,1)S(1)}, u32[]{:S(2)}, u32[]{:S(2)}) %collective-permute-start.21) | collective-permute-done | bytes 131104 | tf_op jit(solution)/shard_map/ppermute | solution.py:283
  106.5 1.6 %shard_map.55 = bf16[8,2,4,128,128]{4,3,2,1,0:T(8,128)(2,1)} custom-call(s32[5]{0:T(128)S(1)} %stack.15.at, bf16[2,4,64,128]{3,2,1,0:T(8,128)(2,1)S(1)} %collective-permute-done.20.refs_0_, bf16[2,4,64,128]{3,2,1,0:T(8,128)(2,1)S(1)} %collective-permute-done.21.refs_1_, ...), custom_call_target="tpu_custom_call", output_to_operand_aliasing={{}: (9, {})} | custom-call | tf_op jit(solution)/shard_map/pallas_call | solution.py:252
  (55 shorter events, 12.1 us)
Async XLA Ops:
  2.5 10.2 %collective-permute-start.2 = (bf16[4,2,64,128]{3,2,1,0:T(8,128)(2,1)S(1)}, bf16[4,2,64,128]{3,2,1,0:T(8,128)(2,1)S(1)}, u32[]{:S(2)}, u32[]{:S(2)}) collective-permute-start(bf16[4,2,64,128]{3,2,1,0:T(8,128)(2,1)S(1)} %get-tuple-element.87), channel_id=1, source_target_pairs={{0,28},{4,24},{8,20},{12,16},{16,12},{20,8},{24,4},{28,0},{1,29},{... | collective-permute-start | bytes 393224 | tf_op jit(solution)/shard_map/ppermute | solution.py:283
  7.7 15.5 %collective-permute-start = (bf16[8,2,64,128]{3,2,1,0:T(8,128)(2,1)S(1)}, bf16[8,2,64,128]{3,2,1,0:T(8,128)(2,1)S(1)}, u32[]{:S(2)}, u32[]{:S(2)}) collective-permute-start(bf16[8,2,64,128]{3,2,1,0:T(8,128)(2,1)S(1)} %get-tuple-element.82), channel_id=1, source_target_pairs={{0,1},{1,0},{2,3},{3,2},{4,5},{5,4},{6,7},{7,6},{8,9},{9,8},{10,11... | collective-permute-start | bytes 786440 | tf_op jit(solution)/shard_map/ppermute | solution.py:286
  9.3 14.5 %collective-permute-start.1 = (bf16[8,2,64,128]{3,2,1,0:T(8,128)(2,1)S(1)}, bf16[8,2,64,128]{3,2,1,0:T(8,128)(2,1)S(1)}, u32[]{:S(2)}, u32[]{:S(2)}) collective-permute-start(bf16[8,2,64,128]{3,2,1,0:T(8,128)(2,1)S(1)} %get-tuple-element.83), channel_id=1, source_target_pairs={{0,2},{1,3},{2,0},{3,1},{4,6},{5,7},{6,4},{7,5},{8,10},{9,11},{10,... | collective-permute-start | bytes 786440 | tf_op jit(solution)/shard_map/ppermute | solution.py:286
  12.7 12.4 %collective-permute-start.3 = (bf16[8,2,64,128]{3,2,1,0:T(8,128)(2,1)S(1)}, bf16[8,2,64,128]{3,2,1,0:T(8,128)(2,1)S(1)}, u32[]{:S(2)}, u32[]{:S(2)}) collective-permute-start(bf16[8,2,64,128]{3,2,1,0:T(8,128)(2,1)S(1)} %get-tuple-element.88), channel_id=1, source_target_pairs={{0,3},{1,2},{2,1},{3,0},{4,7},{5,6},{6,5},{7,4},{8,11},{9,10},{10,... | collective-permute-start | bytes 786440 | tf_op jit(solution)/shard_map/ppermute | solution.py:286
  16.1 9.7 %collective-permute-start.12 = (bf16[4,2,64,128]{3,2,1,0:T(8,128)(2,1)S(1)}, bf16[4,2,64,128]{3,2,1,0:T(8,128)(2,1)S(1)}, u32[]{:S(2)}, u32[]{:S(2)}) collective-permute-start(bf16[4,2,64,128]{3,2,1,0:T(8,128)(2,1)S(1)} %get-tuple-element.98), channel_id=1, source_target_pairs={{0,24},{4,28},{8,16},{12,20},{16,8},{20,12},{24,0},{28,4},{1,25},{... | collective-permute-start | bytes 393224 | tf_op jit(solution)/shard_map/ppermute | solution.py:283
  20.0 11.7 %collective-permute-start.13 = (bf16[4,2,64,128]{3,2,1,0:T(8,128)(2,1)S(1)}, bf16[4,2,64,128]{3,2,1,0:T(8,128)(2,1)S(1)}, u32[]{:S(2)}, u32[]{:S(2)}) collective-permute-start(bf16[4,2,64,128]{3,2,1,0:T(8,128)(2,1)S(1)} %get-tuple-element.99), channel_id=1, source_target_pairs={{0,20},{4,16},{8,28},{12,24},{16,4},{20,0},{24,12},{28,8},{1,21},{... | collective-permute-start | bytes 393224 | tf_op jit(solution)/shard_map/ppermute | solution.py:283
  23.2 9.9 %collective-permute-start.14 = (bf16[4,2,64,128]{3,2,1,0:T(8,128)(2,1)S(1)}, bf16[4,2,64,128]{3,2,1,0:T(8,128)(2,1)S(1)}, u32[]{:S(2)}, u32[]{:S(2)}) collective-permute-start(bf16[4,2,64,128]{3,2,1,0:T(8,128)(2,1)S(1)} %get-tuple-element.100), channel_id=1, source_target_pairs={{0,8},{4,12},{8,0},{12,4},{16,24},{20,28},{24,16},{28,20},{1,9},{5... | collective-permute-start | bytes 393224 | tf_op jit(solution)/shard_map/ppermute | solution.py:283
  23.7 21.7 %collective-permute-start.15 = (bf16[4,2,64,128]{3,2,1,0:T(8,128)(2,1)S(1)}, bf16[4,2,64,128]{3,2,1,0:T(8,128)(2,1)S(1)}, u32[]{:S(2)}, u32[]{:S(2)}) collective-permute-start(bf16[4,2,64,128]{3,2,1,0:T(8,128)(2,1)S(1)} %get-tuple-element.101), channel_id=1, source_target_pairs={{0,16},{4,20},{8,24},{12,28},{16,0},{20,4},{24,8},{28,12},{1,17},{... | collective-permute-start | bytes 393224 | tf_op jit(solution)/shard_map/ppermute | solution.py:283
  25.1 20.3 %collective-permute-start.16 = (bf16[4,2,64,128]{3,2,1,0:T(8,128)(2,1)S(1)}, bf16[4,2,64,128]{3,2,1,0:T(8,128)(2,1)S(1)}, u32[]{:S(2)}, u32[]{:S(2)}) collective-permute-start(bf16[4,2,64,128]{3,2,1,0:T(8,128)(2,1)S(1)} %get-tuple-element.102), channel_id=1, source_target_pairs={{0,4},{4,0},{8,12},{12,8},{16,20},{20,16},{24,28},{28,24},{1,5},{5... | collective-permute-start | bytes 393224 | tf_op jit(solution)/shard_map/ppermute | solution.py:283
  25.8 21.3 %collective-permute-start.4 = (bf16[4,2,64,128]{3,2,1,0:T(8,128)(2,1)S(1)}, bf16[4,2,64,128]{3,2,1,0:T(8,128)(2,1)S(1)}, u32[]{:S(2)}, u32[]{:S(2)}) collective-permute-start(bf16[4,2,64,128]{3,2,1,0:T(8,128)(2,1)S(1)} %get-tuple-element.89), channel_id=1, source_target_pairs={{0,28},{4,24},{8,20},{12,16},{16,12},{20,8},{24,4},{28,0},{1,29},{... | collective-permute-start | bytes 393224 | tf_op jit(solution)/shard_map/ppermute | solution.py:283
  31.7 17.3 %collective-permute-start.6 = (bf16[4,2,64,128]{3,2,1,0:T(8,128)(2,1)S(1)}, bf16[4,2,64,128]{3,2,1,0:T(8,128)(2,1)S(1)}, u32[]{:S(2)}, u32[]{:S(2)}) collective-permute-start(bf16[4,2,64,128]{3,2,1,0:T(8,128)(2,1)S(1)} %get-tuple-element.91), channel_id=1, source_target_pairs={{0,24},{4,28},{8,16},{12,20},{16,8},{20,12},{24,0},{28,4},{1,25},{... | collective-permute-start | bytes 393224 | tf_op jit(solution)/shard_map/ppermute | solution.py:283
  33.0 23.7 %collective-permute-start.7 = (bf16[4,2,64,128]{3,2,1,0:T(8,128)(2,1)S(1)}, bf16[4,2,64,128]{3,2,1,0:T(8,128)(2,1)S(1)}, u32[]{:S(2)}, u32[]{:S(2)}) collective-permute-start(bf16[4,2,64,128]{3,2,1,0:T(8,128)(2,1)S(1)} %get-tuple-element.92), channel_id=1, source_target_pairs={{0,20},{4,16},{8,28},{12,24},{16,4},{20,0},{24,12},{28,8},{1,21},{... | collective-permute-start | bytes 393224 | tf_op jit(solution)/shard_map/ppermute | solution.py:283
  45.4 11.3 %collective-permute-start.5 = (bf16[4,2,64,128]{3,2,1,0:T(8,128)(2,1)S(1)}, bf16[4,2,64,128]{3,2,1,0:T(8,128)(2,1)S(1)}, u32[]{:S(2)}, u32[]{:S(2)}) collective-permute-start(bf16[4,2,64,128]{3,2,1,0:T(8,128)(2,1)S(1)} %get-tuple-element.90), channel_id=1, source_target_pairs={{0,12},{4,8},{8,4},{12,0},{16,28},{20,24},{24,20},{28,16},{1,13},{... | collective-permute-start | bytes 393224 | tf_op jit(solution)/shard_map/ppermute | solution.py:283
  45.4 14.7 %collective-permute-start.8 = (bf16[4,2,64,128]{3,2,1,0:T(8,128)(2,1)S(1)}, bf16[4,2,64,128]{3,2,1,0:T(8,128)(2,1)S(1)}, u32[]{:S(2)}, u32[]{:S(2)}) collective-permute-start(bf16[4,2,64,128]{3,2,1,0:T(8,128)(2,1)S(1)} %get-tuple-element.93), channel_id=1, source_target_pairs={{0,8},{4,12},{8,0},{12,4},{16,24},{20,28},{24,16},{28,20},{1,9},{5... | collective-permute-start | bytes 393224 | tf_op jit(solution)/shard_map/ppermute | solution.py:283
  47.1 13.1 %collective-permute-start.9 = (bf16[4,2,64,128]{3,2,1,0:T(8,128)(2,1)S(1)}, bf16[4,2,64,128]{3,2,1,0:T(8,128)(2,1)S(1)}, u32[]{:S(2)}, u32[]{:S(2)}) collective-permute-start(bf16[4,2,64,128]{3,2,1,0:T(8,128)(2,1)S(1)} %get-tuple-element.94), channel_id=1, source_target_pairs={{0,16},{4,20},{8,24},{12,28},{16,0},{20,4},{24,8},{28,12},{1,17},{... | collective-permute-start | bytes 393224 | tf_op jit(solution)/shard_map/ppermute | solution.py:283
  49.0 12.9 %collective-permute-start.10 = (bf16[4,2,64,128]{3,2,1,0:T(8,128)(2,1)S(1)}, bf16[4,2,64,128]{3,2,1,0:T(8,128)(2,1)S(1)}, u32[]{:S(2)}, u32[]{:S(2)}) collective-permute-start(bf16[4,2,64,128]{3,2,1,0:T(8,128)(2,1)S(1)} %get-tuple-element.95), channel_id=1, source_target_pairs={{0,4},{4,0},{8,12},{12,8},{16,20},{20,16},{24,28},{28,24},{1,5},{5... | collective-permute-start | bytes 393224 | tf_op jit(solution)/shard_map/ppermute | solution.py:283
  56.7 11.9 %collective-permute-start.17 = (bf16[4,2,32,256]{3,2,1,0:T(8,128)(2,1)S(1)}, bf16[4,2,32,256]{3,2,1,0:T(8,128)(2,1)S(1)}, u32[]{:S(2)}, u32[]{:S(2)}) collective-permute-start(bf16[4,2,32,256]{3,2,1,0:T(8,128)(2,1)S(1)} %get-tuple-element.111), channel_id=1, source_target_pairs={{0,28},{4,24},{8,20},{12,16},{16,12},{20,8},{24,4},{28,0},{1,29},{... | collective-permute-start | bytes 393224 | tf_op jit(solution)/shard_map/ppermute | solution.py:283
  56.7 14.8 %collective-permute-start.18 = (bf16[4,2,32,256]{3,2,1,0:T(8,128)(2,1)S(1)}, bf16[4,2,32,256]{3,2,1,0:T(8,128)(2,1)S(1)}, u32[]{:S(2)}, u32[]{:S(2)}) collective-permute-start(bf16[4,2,32,256]{3,2,1,0:T(8,128)(2,1)S(1)} %get-tuple-element.113), channel_id=1, source_target_pairs={{0,24},{4,28},{8,16},{12,20},{16,8},{20,12},{24,0},{28,4},{1,25},{... | collective-permute-start | bytes 393224 | tf_op jit(solution)/shard_map/ppermute | solution.py:283
  60.2 19.0 %collective-permute-start.19 = (bf16[4,2,32,256]{3,2,1,0:T(8,128)(2,1)S(1)}, bf16[4,2,32,256]{3,2,1,0:T(8,128)(2,1)S(1)}, u32[]{:S(2)}, u32[]{:S(2)}) collective-permute-start(bf16[4,2,32,256]{3,2,1,0:T(8,128)(2,1)S(1)} %get-tuple-element.115), channel_id=1, source_target_pairs={{0,20},{4,16},{8,28},{12,24},{16,4},{20,0},{24,12},{28,8},{1,21},{... | collective-permute-start | bytes 393224 | tf_op jit(solution)/shard_map/ppermute | solution.py:283
  60.2 20.4 %collective-permute-start.27 = (bf16[4,2,32,256]{3,2,1,0:T(8,128)(2,1)S(1)}, bf16[4,2,32,256]{3,2,1,0:T(8,128)(2,1)S(1)}, u32[]{:S(2)}, u32[]{:S(2)}) collective-permute-start(bf16[4,2,32,256]{3,2,1,0:T(8,128)(2,1)S(1)} %get-tuple-element.132), channel_id=1, source_target_pairs={{0,12},{4,8},{8,4},{12,0},{16,28},{20,24},{24,20},{28,16},{1,13},{... | collective-permute-start | bytes 393224 | tf_op jit(solution)/shard_map/ppermute | solution.py:283
  61.9 18.7 %collective-permute-start.28 = (bf16[4,2,32,256]{3,2,1,0:T(8,128)(2,1)S(1)}, bf16[4,2,32,256]{3,2,1,0:T(8,128)(2,1)S(1)}, u32[]{:S(2)}, u32[]{:S(2)}) collective-permute-start(bf16[4,2,32,256]{3,2,1,0:T(8,128)(2,1)S(1)} %get-tuple-element.134), channel_id=1, source_target_pairs={{0,8},{4,12},{8,0},{12,4},{16,24},{20,28},{24,16},{28,20},{1,9},{5... | collective-permute-start | bytes 393224 | tf_op jit(solution)/shard_map/ppermute | solution.py:283
  68.7 13.4 %collective-permute-start.29 = (bf16[4,2,32,256]{3,2,1,0:T(8,128)(2,1)S(1)}, bf16[4,2,32,256]{3,2,1,0:T(8,128)(2,1)S(1)}, u32[]{:S(2)}, u32[]{:S(2)}) collective-permute-start(bf16[4,2,32,256]{3,2,1,0:T(8,128)(2,1)S(1)} %get-tuple-element.136), channel_id=1, source_target_pairs={{0,16},{4,20},{8,24},{12,28},{16,0},{20,4},{24,8},{28,12},{1,17},{... | collective-permute-start | bytes 393224 | tf_op jit(solution)/shard_map/ppermute | solution.py:283
  71.6 10.5 %collective-permute-start.30 = (bf16[4,2,32,256]{3,2,1,0:T(8,128)(2,1)S(1)}, bf16[4,2,32,256]{3,2,1,0:T(8,128)(2,1)S(1)}, u32[]{:S(2)}, u32[]{:S(2)}) collective-permute-start(bf16[4,2,32,256]{3,2,1,0:T(8,128)(2,1)S(1)} %get-tuple-element.138), channel_id=1, source_target_pairs={{0,4},{4,0},{8,12},{12,8},{16,20},{20,16},{24,28},{28,24},{1,5},{5... | collective-permute-start | bytes 393224 | tf_op jit(solution)/shard_map/ppermute | solution.py:283
  79.1 7.4 %collective-permute-start.20 = (bf16[2,4,64,128]{3,2,1,0:T(8,128)(2,1)S(1)}, bf16[2,4,64,128]{3,2,1,0:T(8,128)(2,1)S(1)}, u32[]{:S(2)}, u32[]{:S(2)}) collective-permute-start(bf16[2,4,64,128]{3,2,1,0:T(8,128)(2,1)S(1)} %bitcast.40), channel_id=1, source_target_pairs={{0,28},{4,24},{8,20},{12,16},{16,12},{20,8},{24,4},{28,0},{1,29},{... | collective-permute-start | bytes 393224 | tf_op jit(solution)/shard_map/ppermute | solution.py:283
  82.7 9.2 %collective-permute-start.31 = (bf16[8,2,32,256]{3,2,1,0:T(8,128)(2,1)S(1)}, bf16[8,2,32,256]{3,2,1,0:T(8,128)(2,1)S(1)}, u32[]{:S(2)}, u32[]{:S(2)}) collective-permute-start(bf16[8,2,32,256]{3,2,1,0:T(8,128)(2,1)S(1)} %get-tuple-element.140), channel_id=1, source_target_pairs={{0,1},{1,0},{2,3},{3,2},{4,5},{5,4},{6,7},{7,6},{8,9},{9,8},{10,11... | collective-permute-start | bytes 786440 | tf_op jit(solution)/shard_map/ppermute | solution.py:286
  83.3 13.6 %collective-permute-start.32 = (bf16[8,2,32,256]{3,2,1,0:T(8,128)(2,1)S(1)}, bf16[8,2,32,256]{3,2,1,0:T(8,128)(2,1)S(1)}, u32[]{:S(2)}, u32[]{:S(2)}) collective-permute-start(bf16[8,2,32,256]{3,2,1,0:T(8,128)(2,1)S(1)} %get-tuple-element.141), channel_id=1, source_target_pairs={{0,2},{1,3},{2,0},{3,1},{4,6},{5,7},{6,4},{7,5},{8,10},{9,11},{10,... | collective-permute-start | bytes 786440 | tf_op jit(solution)/shard_map/ppermute | solution.py:286
  86.5 12.0 %collective-permute-start.33 = (bf16[8,2,32,256]{3,2,1,0:T(8,128)(2,1)S(1)}, bf16[8,2,32,256]{3,2,1,0:T(8,128)(2,1)S(1)}, u32[]{:S(2)}, u32[]{:S(2)}) collective-permute-start(bf16[8,2,32,256]{3,2,1,0:T(8,128)(2,1)S(1)} %get-tuple-element.143), channel_id=1, source_target_pairs={{0,3},{1,2},{2,1},{3,0},{4,7},{5,6},{6,5},{7,4},{8,11},{9,10},{10,... | collective-permute-start | bytes 786440 | tf_op jit(solution)/shard_map/ppermute | solution.py:286
  87.0 15.2 %collective-permute-start.25 = (bf16[2,4,64,128]{3,2,1,0:T(8,128)(2,1)S(1)}, bf16[2,4,64,128]{3,2,1,0:T(8,128)(2,1)S(1)}, u32[]{:S(2)}, u32[]{:S(2)}) collective-permute-start(bf16[2,4,64,128]{3,2,1,0:T(8,128)(2,1)S(1)} %bitcast.38), channel_id=1, source_target_pairs={{0,16},{4,20},{8,24},{12,28},{16,0},{20,4},{24,8},{28,12},{1,17},{... | collective-permute-start | bytes 393224 | tf_op jit(solution)/shard_map/ppermute | solution.py:283
  88.9 13.4 %collective-permute-start.24 = (bf16[2,4,64,128]{3,2,1,0:T(8,128)(2,1)S(1)}, bf16[2,4,64,128]{3,2,1,0:T(8,128)(2,1)S(1)}, u32[]{:S(2)}, u32[]{:S(2)}) collective-permute-start(bf16[2,4,64,128]{3,2,1,0:T(8,128)(2,1)S(1)} %bitcast.37), channel_id=1, source_target_pairs={{0,8},{4,12},{8,0},{12,4},{16,24},{20,28},{24,16},{28,20},{1,9},{5... | collective-permute-start | bytes 393224 | tf_op jit(solution)/shard_map/ppermute | solution.py:283
  91.9 12.6 %collective-permute-start.23 = (bf16[2,4,64,128]{3,2,1,0:T(8,128)(2,1)S(1)}, bf16[2,4,64,128]{3,2,1,0:T(8,128)(2,1)S(1)}, u32[]{:S(2)}, u32[]{:S(2)}) collective-permute-start(bf16[2,4,64,128]{3,2,1,0:T(8,128)(2,1)S(1)} %bitcast.36), channel_id=1, source_target_pairs={{0,20},{4,16},{8,28},{12,24},{16,4},{20,0},{24,12},{28,8},{1,21},{... | collective-permute-start | bytes 393224 | tf_op jit(solution)/shard_map/ppermute | solution.py:283
  96.8 8.0 %collective-permute-start.22 = (bf16[2,4,64,128]{3,2,1,0:T(8,128)(2,1)S(1)}, bf16[2,4,64,128]{3,2,1,0:T(8,128)(2,1)S(1)}, u32[]{:S(2)}, u32[]{:S(2)}) collective-permute-start(bf16[2,4,64,128]{3,2,1,0:T(8,128)(2,1)S(1)} %bitcast.35), channel_id=1, source_target_pairs={{0,24},{4,28},{8,16},{12,20},{16,8},{20,12},{24,0},{28,4},{1,25},{... | collective-permute-start | bytes 393224 | tf_op jit(solution)/shard_map/ppermute | solution.py:283
  98.6 7.9 %collective-permute-start.21 = (bf16[2,4,64,128]{3,2,1,0:T(8,128)(2,1)S(1)}, bf16[2,4,64,128]{3,2,1,0:T(8,128)(2,1)S(1)}, u32[]{:S(2)}, u32[]{:S(2)}) collective-permute-start(bf16[2,4,64,128]{3,2,1,0:T(8,128)(2,1)S(1)} %bitcast.34), channel_id=1, source_target_pairs={{0,12},{4,8},{8,4},{12,0},{16,28},{20,24},{24,20},{28,16},{1,13},{... | collective-permute-start | bytes 393224 | tf_op jit(solution)/shard_map/ppermute | solution.py:283
  (6 other events, 36.9 us)

commit v4 on v3

--- a/solution.py
+++ b/solution.py
@@ -13,12 +13,13 @@
 NEAREST = 12582912.0
 VMEM = 12 * 2**20
 FIRST = 64
-ORDER = (7, 3, 6, 5, 2, 4, 1, 0)
-G_F = {3: (1, (7,))}
+ORDER = (6, 3, 7, 5, 2, 4, 1, 0)
+ORDER_P = (7, 3, 6, 5, 2, 4, 1, 0)
+G_F = {3: (1, (6,))}
 G_R = ()
 G_A = (7, 6, 5)
 G_B = (7, 6, 5)
-G_C = {3: (7,)}
+G_C = {3: (6,)}
 
 
 def after(value, *earlier):
@@ -232,7 +233,7 @@
 
 
 def gather(span, at, *refs):
-    parts, out, sems = ordered(refs[:8]), refs[-2], refs[-1]
+    parts, out, sems = [refs[ORDER_P.index(k)] for k in range(8)], refs[-2], refs[-1]
     low, count = span
     copies = [
         pltpu.make_async_copy(parts[k], out.at[at[0] ^ k, :, :, pl.ds(low, count)], sems.at[k])
@@ -381,7 +382,7 @@
     )
 
     def place(span, parts, out=None):
-        operands = in_order(parts) if out is None else [*in_order(parts), out]
+        operands = [parts[k] for k in ORDER_P] + ([] if out is None else [out])
         return call(
             functools.partial(gather, span),
             at,

time: 108 us -> 107 us (level); the launches traced: 108 us -> 106 us
  waiting for transfers between devices: 43.1 us -> 36.3 us
  starting transfers between devices: 42.2 us -> 46.6 us
    ppermute x28, waiting for transfers between devices: 36.2 us -> 29.8 us  [over_src(): lax.ppermute(block, 'src', [(i, i ^ k << shift) for i in range(n_src)])]
    ppermute x28, starting transfers between devices: 36.3 us -> 40.5 us  [over_src(): lax.ppermute(block, 'src', [(i, i ^ k << shift) for i in range(n_src)])]
  transfers between devices with their start and end apart: 34 -> 34, of which waited for: 13 -> 11; matrix products, arithmetic and copies ran while one was open for 0% -> 0% of each run, Pallas kernels for 17% -> 18%
where the time goes in v4:
time: 107 us; the launch traced here: 106 us
  starting transfers between devices  46.6 us (44%)
  waiting for transfers between devices  36.3 us (34%)
  Pallas kernels  21 us (20%)
  local copies, waits for them, and re-layouts  1.69 us (2%)
    ppermute x28, starting transfers between devices, over_src(): lax.ppermute(block, 'src', [(i, i ^ k << shift) for i in range(n_src)])  40.5 us
    ppermute x28, waiting for transfers between devices, over_src(): lax.ppermute(block, 'src', [(i, i ^ k << shift) for i in range(n_src)])  29.8 us
    pallas_call x10, Pallas kernels, call(): pl.pallas_call(kernel, out_shape=outs, grid_spec=pltpu.PrefetchScalarGrid...  21 us
    ppermute x6, waiting for transfers between devices, over_freq(): return lax.ppermute(block, 'freq', [(j, j ^ q) for j in range(n_freq)])  6.48 us
    ppermute x6, starting transfers between devices, over_freq(): return lax.ppermute(block, 'freq', [(j, j ^ q) for j in range(n_freq)])  6.12 us
  transfers between devices with their start and end apart: 34, of which 11 were waited for; matrix products, arithmetic and copies ran while one was open for 0% of the time, Pallas kernels for 18%

profile of v4, /device:TPU:0, one launch (start us, length us, event | category | flops | bytes accessed | tf_op | source)
XLA Modules:
  0.0 105.9 jit_solution(11383668614830742849)
XLA Ops:
  0.1 1.6 %copy-done = bf16[64,128,128]{2,1,0:T(8,128)(2,1)S(1)} copy-done((bf16[64,128,128]{2,1,0:T(8,128)(2,1)S(1)}, bf16[64,128,128]{2,1,0:T(8,128)(2,1)}, u32[]{:S(2)}) %copy-start) | copy-done | bytes 2097176
  2.5 5.1 %collective-permute-start.2 = (bf16[4,2,64,128]{3,2,1,0:T(8,128)(2,1)S(1)}, bf16[4,2,64,128]{3,2,1,0:T(8,128)(2,1)S(1)}, u32[]{:S(2)}, u32[]{:S(2)}) collective-permute-start(bf16[4,2,64,128]{3,2,1,0:T(8,128)(2,1)S(1)} %get-tuple-element.87), channel_id=1, source_target_pairs={{0,24},{4,28},{8,16},{12,20},{16,8},{20,12},{24,0},{28,4},{1,25},{... | collective-permute-start | bytes 393224 | tf_op jit(solution)/shard_map/ppermute | solution.py:284
  8.3 1.6 %collective-permute-start = (bf16[8,2,64,128]{3,2,1,0:T(8,128)(2,1)S(1)}, bf16[8,2,64,128]{3,2,1,0:T(8,128)(2,1)S(1)}, u32[]{:S(2)}, u32[]{:S(2)}) collective-permute-start(bf16[8,2,64,128]{3,2,1,0:T(8,128)(2,1)S(1)} %get-tuple-element.82), channel_id=1, source_target_pairs={{0,1},{1,0},{2,3},{3,2},{4,5},{5,4},{6,7},{7,6},{8,9},{9,8},{10,11... | collective-permute-start | bytes 786440 | tf_op jit(solution)/shard_map/ppermute | solution.py:287
  9.8 1.5 %collective-permute-start.1 = (bf16[8,2,64,128]{3,2,1,0:T(8,128)(2,1)S(1)}, bf16[8,2,64,128]{3,2,1,0:T(8,128)(2,1)S(1)}, u32[]{:S(2)}, u32[]{:S(2)}) collective-permute-start(bf16[8,2,64,128]{3,2,1,0:T(8,128)(2,1)S(1)} %get-tuple-element.83), channel_id=1, source_target_pairs={{0,2},{1,3},{2,0},{3,1},{4,6},{5,7},{6,4},{7,5},{8,10},{9,11},{10,... | collective-permute-start | bytes 786440 | tf_op jit(solution)/shard_map/ppermute | solution.py:287
  11.4 1.9 %shard_map.48 = (f32[4,8,2,128]{3,2,1,0:T(2,128)S(1)}, f32[3,8,4,2,128]{4,3,2,1,0:T(2,128)S(1)}, f32[8,2,128]{2,1,0:T(2,128)S(1)}, f32[4,4,32,128]{3,2,1,0:T(8,1...) custom-call(s32[5]{0:T(128)S(1)} %stack.15.at, f32[4,64,512]{2,1,0:T(8,128)S(1)} %copy-done.1, ...), custom_call_target="tpu_custom_call" | custom-call | tf_op jit(solution)/shard_map/pallas_call | solution.py:253
  14.6 3.7 %collective-permute-start.12 = (bf16[4,2,64,128]{3,2,1,0:T(8,128)(2,1)S(1)}, bf16[4,2,64,128]{3,2,1,0:T(8,128)(2,1)S(1)}, u32[]{:S(2)}, u32[]{:S(2)}) collective-permute-start(bf16[4,2,64,128]{3,2,1,0:T(8,128)(2,1)S(1)} %get-tuple-element.98), channel_id=1, source_target_pairs={{0,28},{4,24},{8,20},{12,16},{16,12},{20,8},{24,4},{28,0},{1,29},{... | collective-permute-start | bytes 393224 | tf_op jit(solution)/shard_map/ppermute | solution.py:284
  18.9 2.2 %collective-permute-start.13 = (bf16[4,2,64,128]{3,2,1,0:T(8,128)(2,1)S(1)}, bf16[4,2,64,128]{3,2,1,0:T(8,128)(2,1)S(1)}, u32[]{:S(2)}, u32[]{:S(2)}) collective-permute-start(bf16[4,2,64,128]{3,2,1,0:T(8,128)(2,1)S(1)} %get-tuple-element.99), channel_id=1, source_target_pairs={{0,20},{4,16},{8,28},{12,24},{16,4},{20,0},{24,12},{28,8},{1,21},{... | collective-permute-start | bytes 393224 | tf_op jit(solution)/shard_map/ppermute | solution.py:284
  21.1 2.0 %collective-permute-start.14 = (bf16[4,2,64,128]{3,2,1,0:T(8,128)(2,1)S(1)}, bf16[4,2,64,128]{3,2,1,0:T(8,128)(2,1)S(1)}, u32[]{:S(2)}, u32[]{:S(2)}) collective-permute-start(bf16[4,2,64,128]{3,2,1,0:T(8,128)(2,1)S(1)} %get-tuple-element.100), channel_id=1, source_target_pairs={{0,8},{4,12},{8,0},{12,4},{16,24},{20,28},{24,16},{28,20},{1,9},{5... | collective-permute-start | bytes 393224 | tf_op jit(solution)/shard_map/ppermute | solution.py:284
  23.1 3.2 %collective-permute-start.15 = (bf16[4,2,64,128]{3,2,1,0:T(8,128)(2,1)S(1)}, bf16[4,2,64,128]{3,2,1,0:T(8,128)(2,1)S(1)}, u32[]{:S(2)}, u32[]{:S(2)}) collective-permute-start(bf16[4,2,64,128]{3,2,1,0:T(8,128)(2,1)S(1)} %get-tuple-element.101), channel_id=1, source_target_pairs={{0,16},{4,20},{8,24},{12,28},{16,0},{20,4},{24,8},{28,12},{1,17},{... | collective-permute-start | bytes 393224 | tf_op jit(solution)/shard_map/ppermute | solution.py:284
  26.9 2.3 %collective-permute-start.4 = (bf16[4,2,64,128]{3,2,1,0:T(8,128)(2,1)S(1)}, bf16[4,2,64,128]{3,2,1,0:T(8,128)(2,1)S(1)}, u32[]{:S(2)}, u32[]{:S(2)}) collective-permute-start(bf16[4,2,64,128]{3,2,1,0:T(8,128)(2,1)S(1)} %get-tuple-element.89), channel_id=1, source_target_pairs={{0,24},{4,28},{8,16},{12,20},{16,8},{20,12},{24,0},{28,4},{1,25},{... | collective-permute-start | bytes 393224 | tf_op jit(solution)/shard_map/ppermute | solution.py:284
  29.3 1.1 %collective-permute-done.13.refs_3_ = bf16[4,2,64,128]{3,2,1,0:T(8,128)(2,1)S(1)} collective-permute-done((bf16[4,2,64,128]{3,2,1,0:T(8,128)(2,1)S(1)}, bf16[4,2,64,128]{3,2,1,0:T(8,128)(2,1)S(1)}, u32[]{:S(2)}, u32[]{:S(2)}) %collective-permute-start.13) | collective-permute-done | bytes 131104 | tf_op jit(solution)/shard_map/ppermute | solution.py:284
  30.4 1.3 %collective-permute-start.6 = (bf16[4,2,64,128]{3,2,1,0:T(8,128)(2,1)S(1)}, bf16[4,2,64,128]{3,2,1,0:T(8,128)(2,1)S(1)}, u32[]{:S(2)}, u32[]{:S(2)}) collective-permute-start(bf16[4,2,64,128]{3,2,1,0:T(8,128)(2,1)S(1)} %get-tuple-element.91), channel_id=1, source_target_pairs={{0,28},{4,24},{8,20},{12,16},{16,12},{20,8},{24,4},{28,0},{1,29},{... | collective-permute-start | bytes 393224 | tf_op jit(solution)/shard_map/ppermute | solution.py:284
  31.7 9.7 %collective-permute-done.15.refs_5_ = bf16[4,2,64,128]{3,2,1,0:T(8,128)(2,1)S(1)} collective-permute-done((bf16[4,2,64,128]{3,2,1,0:T(8,128)(2,1)S(1)}, bf16[4,2,64,128]{3,2,1,0:T(8,128)(2,1)S(1)}, u32[]{:S(2)}, u32[]{:S(2)}) %collective-permute-start.15) | collective-permute-done | bytes 131104 | tf_op jit(solution)/shard_map/ppermute | solution.py:284
  41.5 1.5 %collective-permute-start.8 = (bf16[4,2,64,128]{3,2,1,0:T(8,128)(2,1)S(1)}, bf16[4,2,64,128]{3,2,1,0:T(8,128)(2,1)S(1)}, u32[]{:S(2)}, u32[]{:S(2)}) collective-permute-start(bf16[4,2,64,128]{3,2,1,0:T(8,128)(2,1)S(1)} %get-tuple-element.93), channel_id=1, source_target_pairs={{0,8},{4,12},{8,0},{12,4},{16,24},{20,28},{24,16},{28,20},{1,9},{5... | collective-permute-start | bytes 393224 | tf_op jit(solution)/shard_map/ppermute | solution.py:284
  43.0 3.5 %collective-permute-start.9 = (bf16[4,2,64,128]{3,2,1,0:T(8,128)(2,1)S(1)}, bf16[4,2,64,128]{3,2,1,0:T(8,128)(2,1)S(1)}, u32[]{:S(2)}, u32[]{:S(2)}) collective-permute-start(bf16[4,2,64,128]{3,2,1,0:T(8,128)(2,1)S(1)} %get-tuple-element.94), channel_id=1, source_target_pairs={{0,16},{4,20},{8,24},{12,28},{16,0},{20,4},{24,8},{28,12},{1,17},{... | collective-permute-start | bytes 393224 | tf_op jit(solution)/shard_map/ppermute | solution.py:284
  47.4 4.6 %shard_map.50 = (bf16[4,2,32,256]{3,2,1,0:T(8,128)(2,1)S(1)}, bf16[4,2,32,256]{3,2,1,0:T(8,128)(2,1)S(1)}, bf16[4,2,32,256]{3,2,1,0:T(8,128)(2,1)S(1)}, bf16[4,2...) custom-call(s32[5]{0:T(128)S(1)} %stack.15.at, ...), custom_call_target="tpu_custom_call" | custom-call | tf_op jit(solution)/shard_map/pallas_call | solution.py:253
  52.0 3.3 %collective-permute-done.7 = bf16[4,2,64,128]{3,2,1,0:T(8,128)(2,1)S(1)} collective-permute-done((bf16[4,2,64,128]{3,2,1,0:T(8,128)(2,1)S(1)}, bf16[4,2,64,128]{3,2,1,0:T(8,128)(2,1)S(1)}, u32[]{:S(2)}, u32[]{:S(2)}) %collective-permute-start.7) | collective-permute-done | bytes 131104 | tf_op jit(solution)/shard_map/ppermute | solution.py:284
  55.4 3.4 %collective-permute-start.18 = (bf16[4,2,32,256]{3,2,1,0:T(8,128)(2,1)S(1)}, bf16[4,2,32,256]{3,2,1,0:T(8,128)(2,1)S(1)}, u32[]{:S(2)}, u32[]{:S(2)}) collective-permute-start(bf16[4,2,32,256]{3,2,1,0:T(8,128)(2,1)S(1)} %get-tuple-element.113), channel_id=1, source_target_pairs={{0,24},{4,28},{8,16},{12,20},{16,8},{20,12},{24,0},{28,4},{1,25},{... | collective-permute-start | bytes 393224 | tf_op jit(solution)/shard_map/ppermute | solution.py:284
  59.5 2.4 %collective-permute-start.28 = (bf16[4,2,32,256]{3,2,1,0:T(8,128)(2,1)S(1)}, bf16[4,2,32,256]{3,2,1,0:T(8,128)(2,1)S(1)}, u32[]{:S(2)}, u32[]{:S(2)}) collective-permute-start(bf16[4,2,32,256]{3,2,1,0:T(8,128)(2,1)S(1)} %get-tuple-element.134), channel_id=1, source_target_pairs={{0,8},{4,12},{8,0},{12,4},{16,24},{20,28},{24,16},{28,20},{1,9},{5... | collective-permute-start | bytes 393224 | tf_op jit(solution)/shard_map/ppermute | solution.py:284
  61.9 6.5 %shard_map.51 = (bf16[2,2,2,64,128]{4,3,2,1,0:T(8,128)(2,1)S(1)}, bf16[2,2,2,64,128]{4,3,2,1,0:T(8,128)(2,1)S(1)}, bf16[2,2,2,64,128]{4,3,2,1,0:T(8,128)(2,1)S(1...) custom-call(s32[5]{0:T(128)S(1)} %stack.15.at, ...), custom_call_target="tpu_custom_call" | custom-call | tf_op jit(solution)/shard_map/pallas_call | solution.py:253
  68.5 1.7 %collective-permute-start.29 = (bf16[4,2,32,256]{3,2,1,0:T(8,128)(2,1)S(1)}, bf16[4,2,32,256]{3,2,1,0:T(8,128)(2,1)S(1)}, u32[]{:S(2)}, u32[]{:S(2)}) collective-permute-start(bf16[4,2,32,256]{3,2,1,0:T(8,128)(2,1)S(1)} %get-tuple-element.136), channel_id=1, source_target_pairs={{0,16},{4,20},{8,24},{12,28},{16,0},{20,4},{24,8},{28,12},{1,17},{... | collective-permute-start | bytes 393224 | tf_op jit(solution)/shard_map/ppermute | solution.py:284
  71.0 6.7 %collective-permute-done.19.refs_3_ = bf16[4,2,32,256]{3,2,1,0:T(8,128)(2,1)S(1)} collective-permute-done((bf16[4,2,32,256]{3,2,1,0:T(8,128)(2,1)S(1)}, bf16[4,2,32,256]{3,2,1,0:T(8,128)(2,1)S(1)}, u32[]{:S(2)}, u32[]{:S(2)}) %collective-permute-start.19) | collective-permute-done | bytes 131104 | tf_op jit(solution)/shard_map/ppermute | solution.py:284
  77.7 1.8 %collective-permute-start.22 = (bf16[2,4,64,128]{3,2,1,0:T(8,128)(2,1)S(1)}, bf16[2,4,64,128]{3,2,1,0:T(8,128)(2,1)S(1)}, u32[]{:S(2)}, u32[]{:S(2)}) collective-permute-start(bf16[2,4,64,128]{3,2,1,0:T(8,128)(2,1)S(1)} %bitcast.40), channel_id=1, source_target_pairs={{0,24},{4,28},{8,16},{12,20},{16,8},{20,12},{24,0},{28,4},{1,25},{... | collective-permute-start | bytes 393224 | tf_op jit(solution)/shard_map/ppermute | solution.py:284
  79.6 1.2 %collective-permute-done.29.refs_5_ = bf16[4,2,32,256]{3,2,1,0:T(8,128)(2,1)S(1)} collective-permute-done((bf16[4,2,32,256]{3,2,1,0:T(8,128)(2,1)S(1)}, bf16[4,2,32,256]{3,2,1,0:T(8,128)(2,1)S(1)}, u32[]{:S(2)}, u32[]{:S(2)}) %collective-permute-start.29) | collective-permute-done | bytes 131104 | tf_op jit(solution)/shard_map/ppermute | solution.py:284
  83.0 2.2 %collective-permute-done.22.refs_2_ = bf16[2,4,64,128]{3,2,1,0:T(8,128)(2,1)S(1)} collective-permute-done((bf16[2,4,64,128]{3,2,1,0:T(8,128)(2,1)S(1)}, bf16[2,4,64,128]{3,2,1,0:T(8,128)(2,1)S(1)}, u32[]{:S(2)}, u32[]{:S(2)}) %collective-permute-start.22) | collective-permute-done | bytes 131104 | tf_op jit(solution)/shard_map/ppermute | solution.py:284
  86.0 2.1 %collective-permute-start.25 = (bf16[2,4,64,128]{3,2,1,0:T(8,128)(2,1)S(1)}, bf16[2,4,64,128]{3,2,1,0:T(8,128)(2,1)S(1)}, u32[]{:S(2)}, u32[]{:S(2)}) collective-permute-start(bf16[2,4,64,128]{3,2,1,0:T(8,128)(2,1)S(1)} %bitcast.38), channel_id=1, source_target_pairs={{0,16},{4,20},{8,24},{12,28},{16,0},{20,4},{24,8},{28,12},{1,17},{... | collective-permute-start | bytes 393224 | tf_op jit(solution)/shard_map/ppermute | solution.py:284
  89.0 1.6 %collective-permute-done.31.refs_1_ = bf16[8,2,32,256]{3,2,1,0:T(8,128)(2,1)S(1)} collective-permute-done((bf16[8,2,32,256]{3,2,1,0:T(8,128)(2,1)S(1)}, bf16[8,2,32,256]{3,2,1,0:T(8,128)(2,1)S(1)}, u32[]{:S(2)}, u32[]{:S(2)}) %collective-permute-start.31) | collective-permute-done | bytes 262176 | tf_op jit(solution)/shard_map/ppermute | solution.py:287
  90.6 4.9 %collective-permute-done.32.refs_2_ = bf16[8,2,32,256]{3,2,1,0:T(8,128)(2,1)S(1)} collective-permute-done((bf16[8,2,32,256]{3,2,1,0:T(8,128)(2,1)S(1)}, bf16[8,2,32,256]{3,2,1,0:T(8,128)(2,1)S(1)}, u32[]{:S(2)}, u32[]{:S(2)}) %collective-permute-start.32) | collective-permute-done | bytes 262176 | tf_op jit(solution)/shard_map/ppermute | solution.py:287
  95.5 2.1 %shard_map.53 = (bf16[2,4,64,128]{3,2,1,0:T(8,128)(2,1)S(1)}, bf16[2,4,64,128]{3,2,1,0:T(8,128)(2,1)S(1)}, bf16[2,4,64,128]{3,2,1,0:T(8,128)(2,1)S(1)}, bf16[2,4...) custom-call(s32[5]{0:T(128)S(1)} %stack.15.at, ...), custom_call_target="tpu_custom_call" | custom-call | tf_op jit(solution)/shard_map/pallas_call | solution.py:253
  97.6 1.6 %shard_map.54.refs_8_ = bf16[8,2,4,128,128]{4,3,2,1,0:T(8,128)(2,1)} custom-call(s32[5]{0:T(128)S(1)} %stack.15.at, bf16[2,4,64,128]{3,2,1,0:T(8,128)(2,1)S(1)} %get-tuple-element.145.refs_0_, bf16[2,4,64,128]{3,2,1,0:T(8,128)(2,1)S(1)} %get-tuple-element.146.refs_1_, bf16[2,4,64,128]{3,2,1,0:T(8,128)(2,1)S(1)} %get-tuple-element.147.refs_2_, ...), custom_call_target="tpu_custom_call" | custom-call | tf_op jit(solution)/shard_map/pallas_call | solution.py:253
  99.2 4.6 %collective-permute-done.23.refs_3_ = bf16[2,4,64,128]{3,2,1,0:T(8,128)(2,1)S(1)} collective-permute-done((bf16[2,4,64,128]{3,2,1,0:T(8,128)(2,1)S(1)}, bf16[2,4,64,128]{3,2,1,0:T(8,128)(2,1)S(1)}, u32[]{:S(2)}, u32[]{:S(2)}) %collective-permute-start.23) | collective-permute-done | bytes 131104 | tf_op jit(solution)/shard_map/ppermute | solution.py:284
  104.2 1.6 %shard_map.55 = bf16[8,2,4,128,128]{4,3,2,1,0:T(8,128)(2,1)} custom-call(s32[5]{0:T(128)S(1)} %stack.15.at, bf16[2,4,64,128]{3,2,1,0:T(8,128)(2,1)S(1)} %collective-permute-done.20.refs_0_, bf16[2,4,64,128]{3,2,1,0:T(8,128)(2,1)S(1)} %collective-permute-done.21.refs_1_, ...), custom_call_target="tpu_custom_call", output_to_operand_aliasing={{}: (9, {})} | custom-call | tf_op jit(solution)/shard_map/pallas_call | solution.py:253
  (55 shorter events, 11.0 us)
Async XLA Ops:
  2.5 10.8 %collective-permute-start.2 = (bf16[4,2,64,128]{3,2,1,0:T(8,128)(2,1)S(1)}, bf16[4,2,64,128]{3,2,1,0:T(8,128)(2,1)S(1)}, u32[]{:S(2)}, u32[]{:S(2)}) collective-permute-start(bf16[4,2,64,128]{3,2,1,0:T(8,128)(2,1)S(1)} %get-tuple-element.87), channel_id=1, source_target_pairs={{0,24},{4,28},{8,16},{12,20},{16,8},{20,12},{24,0},{28,4},{1,25},{... | collective-permute-start | bytes 393224 | tf_op jit(solution)/shard_map/ppermute | solution.py:284
  8.3 12.8 %collective-permute-start = (bf16[8,2,64,128]{3,2,1,0:T(8,128)(2,1)S(1)}, bf16[8,2,64,128]{3,2,1,0:T(8,128)(2,1)S(1)}, u32[]{:S(2)}, u32[]{:S(2)}) collective-permute-start(bf16[8,2,64,128]{3,2,1,0:T(8,128)(2,1)S(1)} %get-tuple-element.82), channel_id=1, source_target_pairs={{0,1},{1,0},{2,3},{3,2},{4,5},{5,4},{6,7},{7,6},{8,9},{9,8},{10,11... | collective-permute-start | bytes 786440 | tf_op jit(solution)/shard_map/ppermute | solution.py:287
  9.8 13.3 %collective-permute-start.1 = (bf16[8,2,64,128]{3,2,1,0:T(8,128)(2,1)S(1)}, bf16[8,2,64,128]{3,2,1,0:T(8,128)(2,1)S(1)}, u32[]{:S(2)}, u32[]{:S(2)}) collective-permute-start(bf16[8,2,64,128]{3,2,1,0:T(8,128)(2,1)S(1)} %get-tuple-element.83), channel_id=1, source_target_pairs={{0,2},{1,3},{2,0},{3,1},{4,6},{5,7},{6,4},{7,5},{8,10},{9,11},{10,... | collective-permute-start | bytes 786440 | tf_op jit(solution)/shard_map/ppermute | solution.py:287
  13.3 13.0 %collective-permute-start.3 = (bf16[8,2,64,128]{3,2,1,0:T(8,128)(2,1)S(1)}, bf16[8,2,64,128]{3,2,1,0:T(8,128)(2,1)S(1)}, u32[]{:S(2)}, u32[]{:S(2)}) collective-permute-start(bf16[8,2,64,128]{3,2,1,0:T(8,128)(2,1)S(1)} %get-tuple-element.88), channel_id=1, source_target_pairs={{0,3},{1,2},{2,1},{3,0},{4,7},{5,6},{6,5},{7,4},{8,11},{9,10},{10,... | collective-permute-start | bytes 786440 | tf_op jit(solution)/shard_map/ppermute | solution.py:287
  14.6 12.4 %collective-permute-start.12 = (bf16[4,2,64,128]{3,2,1,0:T(8,128)(2,1)S(1)}, bf16[4,2,64,128]{3,2,1,0:T(8,128)(2,1)S(1)}, u32[]{:S(2)}, u32[]{:S(2)}) collective-permute-start(bf16[4,2,64,128]{3,2,1,0:T(8,128)(2,1)S(1)} %get-tuple-element.98), channel_id=1, source_target_pairs={{0,28},{4,24},{8,20},{12,16},{16,12},{20,8},{24,4},{28,0},{1,29},{... | collective-permute-start | bytes 393224 | tf_op jit(solution)/shard_map/ppermute | solution.py:284
  18.9 11.5 %collective-permute-start.13 = (bf16[4,2,64,128]{3,2,1,0:T(8,128)(2,1)S(1)}, bf16[4,2,64,128]{3,2,1,0:T(8,128)(2,1)S(1)}, u32[]{:S(2)}, u32[]{:S(2)}) collective-permute-start(bf16[4,2,64,128]{3,2,1,0:T(8,128)(2,1)S(1)} %get-tuple-element.99), channel_id=1, source_target_pairs={{0,20},{4,16},{8,28},{12,24},{16,4},{20,0},{24,12},{28,8},{1,21},{... | collective-permute-start | bytes 393224 | tf_op jit(solution)/shard_map/ppermute | solution.py:284
  21.1 10.6 %collective-permute-start.14 = (bf16[4,2,64,128]{3,2,1,0:T(8,128)(2,1)S(1)}, bf16[4,2,64,128]{3,2,1,0:T(8,128)(2,1)S(1)}, u32[]{:S(2)}, u32[]{:S(2)}) collective-permute-start(bf16[4,2,64,128]{3,2,1,0:T(8,128)(2,1)S(1)} %get-tuple-element.100), channel_id=1, source_target_pairs={{0,8},{4,12},{8,0},{12,4},{16,24},{20,28},{24,16},{28,20},{1,9},{5... | collective-permute-start | bytes 393224 | tf_op jit(solution)/shard_map/ppermute | solution.py:284
  23.1 18.2 %collective-permute-start.15 = (bf16[4,2,64,128]{3,2,1,0:T(8,128)(2,1)S(1)}, bf16[4,2,64,128]{3,2,1,0:T(8,128)(2,1)S(1)}, u32[]{:S(2)}, u32[]{:S(2)}) collective-permute-start(bf16[4,2,64,128]{3,2,1,0:T(8,128)(2,1)S(1)} %get-tuple-element.101), channel_id=1, source_target_pairs={{0,16},{4,20},{8,24},{12,28},{16,0},{20,4},{24,8},{28,12},{1,17},{... | collective-permute-start | bytes 393224 | tf_op jit(solution)/shard_map/ppermute | solution.py:284
  26.3 15.2 %collective-permute-start.16 = (bf16[4,2,64,128]{3,2,1,0:T(8,128)(2,1)S(1)}, bf16[4,2,64,128]{3,2,1,0:T(8,128)(2,1)S(1)}, u32[]{:S(2)}, u32[]{:S(2)}) collective-permute-start(bf16[4,2,64,128]{3,2,1,0:T(8,128)(2,1)S(1)} %get-tuple-element.102), channel_id=1, source_target_pairs={{0,4},{4,0},{8,12},{12,8},{16,20},{20,16},{24,28},{28,24},{1,5},{5... | collective-permute-start | bytes 393224 | tf_op jit(solution)/shard_map/ppermute | solution.py:284
  26.9 16.1 %collective-permute-start.4 = (bf16[4,2,64,128]{3,2,1,0:T(8,128)(2,1)S(1)}, bf16[4,2,64,128]{3,2,1,0:T(8,128)(2,1)S(1)}, u32[]{:S(2)}, u32[]{:S(2)}) collective-permute-start(bf16[4,2,64,128]{3,2,1,0:T(8,128)(2,1)S(1)} %get-tuple-element.89), channel_id=1, source_target_pairs={{0,24},{4,28},{8,16},{12,20},{16,8},{20,12},{24,0},{28,4},{1,25},{... | collective-permute-start | bytes 393224 | tf_op jit(solution)/shard_map/ppermute | solution.py:284
  30.4 16.1 %collective-permute-start.6 = (bf16[4,2,64,128]{3,2,1,0:T(8,128)(2,1)S(1)}, bf16[4,2,64,128]{3,2,1,0:T(8,128)(2,1)S(1)}, u32[]{:S(2)}, u32[]{:S(2)}) collective-permute-start(bf16[4,2,64,128]{3,2,1,0:T(8,128)(2,1)S(1)} %get-tuple-element.91), channel_id=1, source_target_pairs={{0,28},{4,24},{8,20},{12,16},{16,12},{20,8},{24,4},{28,0},{1,29},{... | collective-permute-start | bytes 393224 | tf_op jit(solution)/shard_map/ppermute | solution.py:284
  31.7 23.6 %collective-permute-start.7 = (bf16[4,2,64,128]{3,2,1,0:T(8,128)(2,1)S(1)}, bf16[4,2,64,128]{3,2,1,0:T(8,128)(2,1)S(1)}, u32[]{:S(2)}, u32[]{:S(2)}) collective-permute-start(bf16[4,2,64,128]{3,2,1,0:T(8,128)(2,1)S(1)} %get-tuple-element.92), channel_id=1, source_target_pairs={{0,20},{4,16},{8,28},{12,24},{16,4},{20,0},{24,12},{28,8},{1,21},{... | collective-permute-start | bytes 393224 | tf_op jit(solution)/shard_map/ppermute | solution.py:284
  41.4 14.0 %collective-permute-start.5 = (bf16[4,2,64,128]{3,2,1,0:T(8,128)(2,1)S(1)}, bf16[4,2,64,128]{3,2,1,0:T(8,128)(2,1)S(1)}, u32[]{:S(2)}, u32[]{:S(2)}) collective-permute-start(bf16[4,2,64,128]{3,2,1,0:T(8,128)(2,1)S(1)} %get-tuple-element.90), channel_id=1, source_target_pairs={{0,12},{4,8},{8,4},{12,0},{16,28},{20,24},{24,20},{28,16},{1,13},{... | collective-permute-start | bytes 393224 | tf_op jit(solution)/shard_map/ppermute | solution.py:284
  41.5 17.3 %collective-permute-start.8 = (bf16[4,2,64,128]{3,2,1,0:T(8,128)(2,1)S(1)}, bf16[4,2,64,128]{3,2,1,0:T(8,128)(2,1)S(1)}, u32[]{:S(2)}, u32[]{:S(2)}) collective-permute-start(bf16[4,2,64,128]{3,2,1,0:T(8,128)(2,1)S(1)} %get-tuple-element.93), channel_id=1, source_target_pairs={{0,8},{4,12},{8,0},{12,4},{16,24},{20,28},{24,16},{28,20},{1,9},{5... | collective-permute-start | bytes 393224 | tf_op jit(solution)/shard_map/ppermute | solution.py:284
  43.0 15.8 %collective-permute-start.9 = (bf16[4,2,64,128]{3,2,1,0:T(8,128)(2,1)S(1)}, bf16[4,2,64,128]{3,2,1,0:T(8,128)(2,1)S(1)}, u32[]{:S(2)}, u32[]{:S(2)}) collective-permute-start(bf16[4,2,64,128]{3,2,1,0:T(8,128)(2,1)S(1)} %get-tuple-element.94), channel_id=1, source_target_pairs={{0,16},{4,20},{8,24},{12,28},{16,0},{20,4},{24,8},{28,12},{1,17},{... | collective-permute-start | bytes 393224 | tf_op jit(solution)/shard_map/ppermute | solution.py:284
  46.5 13.0 %collective-permute-start.10 = (bf16[4,2,64,128]{3,2,1,0:T(8,128)(2,1)S(1)}, bf16[4,2,64,128]{3,2,1,0:T(8,128)(2,1)S(1)}, u32[]{:S(2)}, u32[]{:S(2)}) collective-permute-start(bf16[4,2,64,128]{3,2,1,0:T(8,128)(2,1)S(1)} %get-tuple-element.95), channel_id=1, source_target_pairs={{0,4},{4,0},{8,12},{12,8},{16,20},{20,16},{24,28},{28,24},{1,5},{5... | collective-permute-start | bytes 393224 | tf_op jit(solution)/shard_map/ppermute | solution.py:284
  55.3 13.2 %collective-permute-start.17 = (bf16[4,2,32,256]{3,2,1,0:T(8,128)(2,1)S(1)}, bf16[4,2,32,256]{3,2,1,0:T(8,128)(2,1)S(1)}, u32[]{:S(2)}, u32[]{:S(2)}) collective-permute-start(bf16[4,2,32,256]{3,2,1,0:T(8,128)(2,1)S(1)} %get-tuple-element.111), channel_id=1, source_target_pairs={{0,28},{4,24},{8,20},{12,16},{16,12},{20,8},{24,4},{28,0},{1,29},{... | collective-permute-start | bytes 393224 | tf_op jit(solution)/shard_map/ppermute | solution.py:284
  55.4 14.9 %collective-permute-start.18 = (bf16[4,2,32,256]{3,2,1,0:T(8,128)(2,1)S(1)}, bf16[4,2,32,256]{3,2,1,0:T(8,128)(2,1)S(1)}, u32[]{:S(2)}, u32[]{:S(2)}) collective-permute-start(bf16[4,2,32,256]{3,2,1,0:T(8,128)(2,1)S(1)} %get-tuple-element.113), channel_id=1, source_target_pairs={{0,24},{4,28},{8,16},{12,20},{16,8},{20,12},{24,0},{28,4},{1,25},{... | collective-permute-start | bytes 393224 | tf_op jit(solution)/shard_map/ppermute | solution.py:284
  58.8 18.9 %collective-permute-start.19 = (bf16[4,2,32,256]{3,2,1,0:T(8,128)(2,1)S(1)}, bf16[4,2,32,256]{3,2,1,0:T(8,128)(2,1)S(1)}, u32[]{:S(2)}, u32[]{:S(2)}) collective-permute-start(bf16[4,2,32,256]{3,2,1,0:T(8,128)(2,1)S(1)} %get-tuple-element.115), channel_id=1, source_target_pairs={{0,20},{4,16},{8,28},{12,24},{16,4},{20,0},{24,12},{28,8},{1,21},{... | collective-permute-start | bytes 393224 | tf_op jit(solution)/shard_map/ppermute | solution.py:284
  58.8 20.7 %collective-permute-start.27 = (bf16[4,2,32,256]{3,2,1,0:T(8,128)(2,1)S(1)}, bf16[4,2,32,256]{3,2,1,0:T(8,128)(2,1)S(1)}, u32[]{:S(2)}, u32[]{:S(2)}) collective-permute-start(bf16[4,2,32,256]{3,2,1,0:T(8,128)(2,1)S(1)} %get-tuple-element.132), channel_id=1, source_target_pairs={{0,12},{4,8},{8,4},{12,0},{16,28},{20,24},{24,20},{28,16},{1,13},{... | collective-permute-start | bytes 393224 | tf_op jit(solution)/shard_map/ppermute | solution.py:284
  59.5 20.1 %collective-permute-start.28 = (bf16[4,2,32,256]{3,2,1,0:T(8,128)(2,1)S(1)}, bf16[4,2,32,256]{3,2,1,0:T(8,128)(2,1)S(1)}, u32[]{:S(2)}, u32[]{:S(2)}) collective-permute-start(bf16[4,2,32,256]{3,2,1,0:T(8,128)(2,1)S(1)} %get-tuple-element.134), channel_id=1, source_target_pairs={{0,8},{4,12},{8,0},{12,4},{16,24},{20,28},{24,16},{28,20},{1,9},{5... | collective-permute-start | bytes 393224 | tf_op jit(solution)/shard_map/ppermute | solution.py:284
  68.5 12.2 %collective-permute-start.29 = (bf16[4,2,32,256]{3,2,1,0:T(8,128)(2,1)S(1)}, bf16[4,2,32,256]{3,2,1,0:T(8,128)(2,1)S(1)}, u32[]{:S(2)}, u32[]{:S(2)}) collective-permute-start(bf16[4,2,32,256]{3,2,1,0:T(8,128)(2,1)S(1)} %get-tuple-element.136), channel_id=1, source_target_pairs={{0,16},{4,20},{8,24},{12,28},{16,0},{20,4},{24,8},{28,12},{1,17},{... | collective-permute-start | bytes 393224 | tf_op jit(solution)/shard_map/ppermute | solution.py:284
  70.2 10.5 %collective-permute-start.30 = (bf16[4,2,32,256]{3,2,1,0:T(8,128)(2,1)S(1)}, bf16[4,2,32,256]{3,2,1,0:T(8,128)(2,1)S(1)}, u32[]{:S(2)}, u32[]{:S(2)}) collective-permute-start(bf16[4,2,32,256]{3,2,1,0:T(8,128)(2,1)S(1)} %get-tuple-element.138), channel_id=1, source_target_pairs={{0,4},{4,0},{8,12},{12,8},{16,20},{20,16},{24,28},{28,24},{1,5},{5... | collective-permute-start | bytes 393224 | tf_op jit(solution)/shard_map/ppermute | solution.py:284
  77.7 7.4 %collective-permute-start.22 = (bf16[2,4,64,128]{3,2,1,0:T(8,128)(2,1)S(1)}, bf16[2,4,64,128]{3,2,1,0:T(8,128)(2,1)S(1)}, u32[]{:S(2)}, u32[]{:S(2)}) collective-permute-start(bf16[2,4,64,128]{3,2,1,0:T(8,128)(2,1)S(1)} %bitcast.40), channel_id=1, source_target_pairs={{0,24},{4,28},{8,16},{12,20},{16,8},{20,12},{24,0},{28,4},{1,25},{... | collective-permute-start | bytes 393224 | tf_op jit(solution)/shard_map/ppermute | solution.py:284
  81.3 9.2 %collective-permute-start.31 = (bf16[8,2,32,256]{3,2,1,0:T(8,128)(2,1)S(1)}, bf16[8,2,32,256]{3,2,1,0:T(8,128)(2,1)S(1)}, u32[]{:S(2)}, u32[]{:S(2)}) collective-permute-start(bf16[8,2,32,256]{3,2,1,0:T(8,128)(2,1)S(1)} %get-tuple-element.140), channel_id=1, source_target_pairs={{0,1},{1,0},{2,3},{3,2},{4,5},{5,4},{6,7},{7,6},{8,9},{9,8},{10,11... | collective-permute-start | bytes 786440 | tf_op jit(solution)/shard_map/ppermute | solution.py:287
  82.0 13.5 %collective-permute-start.32 = (bf16[8,2,32,256]{3,2,1,0:T(8,128)(2,1)S(1)}, bf16[8,2,32,256]{3,2,1,0:T(8,128)(2,1)S(1)}, u32[]{:S(2)}, u32[]{:S(2)}) collective-permute-start(bf16[8,2,32,256]{3,2,1,0:T(8,128)(2,1)S(1)} %get-tuple-element.141), channel_id=1, source_target_pairs={{0,2},{1,3},{2,0},{3,1},{4,6},{5,7},{6,4},{7,5},{8,10},{9,11},{10,... | collective-permute-start | bytes 786440 | tf_op jit(solution)/shard_map/ppermute | solution.py:287
  85.1 10.3 %collective-permute-start.33 = (bf16[8,2,32,256]{3,2,1,0:T(8,128)(2,1)S(1)}, bf16[8,2,32,256]{3,2,1,0:T(8,128)(2,1)S(1)}, u32[]{:S(2)}, u32[]{:S(2)}) collective-permute-start(bf16[8,2,32,256]{3,2,1,0:T(8,128)(2,1)S(1)} %get-tuple-element.143), channel_id=1, source_target_pairs={{0,3},{1,2},{2,1},{3,0},{4,7},{5,6},{6,5},{7,4},{8,11},{9,10},{10,... | collective-permute-start | bytes 786440 | tf_op jit(solution)/shard_map/ppermute | solution.py:287
  86.0 13.1 %collective-permute-start.25 = (bf16[2,4,64,128]{3,2,1,0:T(8,128)(2,1)S(1)}, bf16[2,4,64,128]{3,2,1,0:T(8,128)(2,1)S(1)}, u32[]{:S(2)}, u32[]{:S(2)}) collective-permute-start(bf16[2,4,64,128]{3,2,1,0:T(8,128)(2,1)S(1)} %bitcast.38), channel_id=1, source_target_pairs={{0,16},{4,20},{8,24},{12,28},{16,0},{20,4},{24,8},{28,12},{1,17},{... | collective-permute-start | bytes 393224 | tf_op jit(solution)/shard_map/ppermute | solution.py:284
  88.2 11.0 %collective-permute-start.24 = (bf16[2,4,64,128]{3,2,1,0:T(8,128)(2,1)S(1)}, bf16[2,4,64,128]{3,2,1,0:T(8,128)(2,1)S(1)}, u32[]{:S(2)}, u32[]{:S(2)}) collective-permute-start(bf16[2,4,64,128]{3,2,1,0:T(8,128)(2,1)S(1)} %bitcast.37), channel_id=1, source_target_pairs={{0,8},{4,12},{8,0},{12,4},{16,24},{20,28},{24,16},{28,20},{1,9},{5... | collective-permute-start | bytes 393224 | tf_op jit(solution)/shard_map/ppermute | solution.py:284
  90.6 13.2 %collective-permute-start.23 = (bf16[2,4,64,128]{3,2,1,0:T(8,128)(2,1)S(1)}, bf16[2,4,64,128]{3,2,1,0:T(8,128)(2,1)S(1)}, u32[]{:S(2)}, u32[]{:S(2)}) collective-permute-start(bf16[2,4,64,128]{3,2,1,0:T(8,128)(2,1)S(1)} %bitcast.36), channel_id=1, source_target_pairs={{0,20},{4,16},{8,28},{12,24},{16,4},{20,0},{24,12},{28,8},{1,21},{... | collective-permute-start | bytes 393224 | tf_op jit(solution)/shard_map/ppermute | solution.py:284
  95.5 8.3 %collective-permute-start.20 = (bf16[2,4,64,128]{3,2,1,0:T(8,128)(2,1)S(1)}, bf16[2,4,64,128]{3,2,1,0:T(8,128)(2,1)S(1)}, u32[]{:S(2)}, u32[]{:S(2)}) collective-permute-start(bf16[2,4,64,128]{3,2,1,0:T(8,128)(2,1)S(1)} %bitcast.35), channel_id=1, source_target_pairs={{0,28},{4,24},{8,20},{12,16},{16,12},{20,8},{24,4},{28,0},{1,29},{... | collective-permute-start | bytes 393224 | tf_op jit(solution)/shard_map/ppermute | solution.py:284
  95.5 8.7 %collective-permute-start.21 = (bf16[2,4,64,128]{3,2,1,0:T(8,128)(2,1)S(1)}, bf16[2,4,64,128]{3,2,1,0:T(8,128)(2,1)S(1)}, u32[]{:S(2)}, u32[]{:S(2)}) collective-permute-start(bf16[2,4,64,128]{3,2,1,0:T(8,128)(2,1)S(1)} %bitcast.34), channel_id=1, source_target_pairs={{0,12},{4,8},{8,4},{12,0},{16,28},{20,24},{24,20},{28,16},{1,13},{... | collective-permute-start | bytes 393224 | tf_op jit(solution)/shard_map/ppermute | solution.py:284
  (6 other events, 37.8 us)
